TPU v7x, 32 devices: a whole 2x2x4 slice. The times are simulated.
32 devices in a mesh: shard: 4 (over y, x), context: 2 (over core), tensor: 4 (over z).
Axes of the slice: x: 2, y: 2, z: 4, core: 2. Of those that a mesh axis runs over, the one named last changes fastest.
Arguments:
- inputs: bfloat16 [4096, 1024], P(('shard', 'context')), may hold values from -6 to 6
- teacher: bfloat16 [4096, 1024], P(('shard', 'context')), may hold values from -6 to 6
- segment_ids: int32 [4, 1024], P('shard', 'context'), may hold values from 0 to 11, never falling along the last dimension, each value on 1 to 256 neighbouring positions
- valid_mask: int32 [4, 1024], P('shard', 'context'), may hold values from 0 to 1, as said below
- norm_gain: float32 [1024], replicated, may hold values from 0.5 to 1.5
- norm_bias: float32 [1024], replicated, may hold values from -4 to 4
- gate_weight: bfloat16 [1024, 3072], P('shard', 'tensor'), may hold values from -0.1875 to 0.1875
- gate_bias: float32 [3072], P('tensor'), may hold values from -4 to 4
- reduce_weight: bfloat16 [1024, 512], P('shard', 'tensor'), may hold values from -0.1875 to 0.1875
- reduce_bias: float32 [512], P('tensor'), may hold values from -4 to 4
- damping: float32 [512, 512], P('tensor'), may hold values from 0.00024414062 to 0.03
- frequency: float32 [512, 512], P('tensor'), may hold values from 0.05 to 3
- timestep: float32 [512], P('tensor'), may hold values from 0.5 to 2
- mix_real: float32 [512, 512], P('tensor'), may hold values from -0.03125 to 0.03125
- mix_imaginary: float32 [512, 512], P('tensor'), may hold values from -0.03125 to 0.03125
- expand_weight: bfloat16 [512, 3072], P('shard', 'tensor'), may hold values from -0.25 to 0.25
- expand_bias: float32 [3072], P('tensor'), may hold values from -4 to 4
- output_weight: bfloat16 [3072, 1024], P('tensor', 'shard'), may hold values from -0.109375 to 0.109375
- output_bias: float32 [1024], replicated, may hold values from -4 to 4
Outputs:
- output: bfloat16 [4096, 1024], P(('shard', 'context'))
- loss: float32 [], replicated
- inputs_grad: bfloat16 [4096, 1024], P(('shard', 'context'))
- norm_gain_grad: float32 [1024], replicated
- norm_bias_grad: float32 [1024], replicated
- gate_weight_grad: float32 [1024, 3072], P('shard', 'tensor')
- gate_bias_grad: float32 [3072], P('tensor')
- reduce_weight_grad: float32 [1024, 512], P('shard', 'tensor')
- reduce_bias_grad: float32 [512], P('tensor')
- damping_grad: float32 [512, 512], P('tensor')
- frequency_grad: float32 [512, 512], P('tensor')
- timestep_grad: float32 [512], P('tensor')
- mix_real_grad: float32 [512, 512], P('tensor')
- mix_imaginary_grad: float32 [512, 512], P('tensor')
- expand_weight_grad: float32 [512, 3072], P('shard', 'tensor')
- expand_bias_grad: float32 [3072], P('tensor')
- output_weight_grad: float32 [3072, 1024], P('tensor', 'shard')
- output_bias_grad: float32 [1024], replicated
Inputs may be any that keep to these rules, and one draw needn't show every extreme that they name: `segment_ids`: ids never fall along a sequence; a document is one run of equal ids. `valid_mask`: the first token of every sequence is valid.
All inputs are finite; a program needn't handle non-finite values.
Results may differ from a plain program's by a relative error of at most 0.015.
Values may be sent and summed in bfloat16 or wider, within the bound.
No kernel may reach another device: no remote copies, remote signals or barrier semaphores. Data moves between devices by JAX's collectives and lax.ppermute only.
A program may use at most 320 MiB of HBM per device.

v0:
```python
from functools import partial

import jax
import jax.numpy as jnp
from jax import lax
from jax.sharding import PartitionSpec as P

BLOCK = 64


PRECISE = lax.Precision.HIGHEST
EPSILON = 1e-05


def prefix(shard, axis, join, neutral):
    place = lax.axis_index(axis)
    gathered = jax.tree.map(
        lambda a, kind: lax.all_gather(a.astype(kind), axis),
        shard,
        (jnp.bfloat16, jnp.bfloat16, jnp.bfloat16, jnp.bfloat16, jnp.bfloat16, jnp.bfloat16),
    )
    state = jax.tree.map(lambda a, e: jnp.zeros_like(a) + jnp.asarray(e, a.dtype), shard, neutral)

    def one(lap, state):
        return join(
            state,
            jax.tree.map(
                lambda a, own: lax.dynamic_index_in_dim(a, lap, 0, False).astype(own.dtype),
                gathered,
                shard,
            ),
        )

    return lax.fori_loop(0, place, one, state)


def prefix_2(shard, axis, join, neutral):
    count = lax.axis_size(axis)
    place = lax.axis_index(axis)
    ahead = count - 1 - place
    gathered = jax.tree.map(
        lambda a, kind: lax.all_gather(a.astype(kind), axis),
        shard,
        jax.tree.map(lambda a: jnp.bfloat16 if a.dtype == jnp.float32 else a.dtype, shard),
    )
    state = jax.tree.map(lambda a, e: jnp.zeros_like(a) + jnp.asarray(e, a.dtype), shard, neutral)

    def one(lap, state):
        source = count - 1 - lap
        return join(
            state,
            jax.tree.map(
                lambda a, own: lax.dynamic_index_in_dim(a, source, 0, False).astype(own.dtype),
                gathered,
                shard,
            ),
        )

    return lax.fori_loop(0, ahead, one, state)


def coefficients(damping, frequency, timestep, mix_real, mix_imaginary):
    rate_real = -timestep[:, None] * damping
    rate_imaginary = timestep[:, None] * frequency
    magnitude = jnp.exp(rate_real)
    minus_real = magnitude * jnp.cos(rate_imaginary) - 1.0
    minus_imaginary = magnitude * jnp.sin(rate_imaginary)
    divisor = damping * damping + frequency * frequency
    ratio_real = (minus_imaginary * frequency - minus_real * damping) / divisor
    ratio_imaginary = -(minus_real * frequency + minus_imaginary * damping) / divisor
    readout_real = mix_real * ratio_real - mix_imaginary * ratio_imaginary
    readout_imaginary = mix_real * ratio_imaginary + mix_imaginary * ratio_real
    return (rate_real, rate_imaginary, readout_real, readout_imaginary)


def powers(rate_real, rate_imaginary, exponents):
    magnitude = jnp.exp(rate_real[..., None] * exponents)
    angles = rate_imaginary[..., None] * exponents
    return (magnitude * jnp.cos(angles), magnitude * jnp.sin(angles))


def powers_first(rate_real, rate_imaginary, exponents):
    magnitude = jnp.exp(exponents[:, None, None] * rate_real[None])
    angles = exponents[:, None, None] * rate_imaginary[None]
    return (magnitude * jnp.cos(angles), magnitude * jnp.sin(angles))


def intra_part(segments, signal, rate_real, rate_imaginary, readout_real, readout_imaginary):
    length, channels = signal.shape
    blocks = length // BLOCK
    number_type = signal.dtype
    offsets = jnp.arange(BLOCK + 1).astype(number_type)
    power_real, power_imaginary = powers(rate_real, rate_imaginary, offsets)
    kernel = jnp.einsum(
        "hn,hnl->hl", readout_real, power_real[..., :BLOCK], precision=PRECISE
    ) - jnp.einsum("hn,hnl->hl", readout_imaginary, power_imaginary[..., :BLOCK], precision=PRECISE)
    places = jnp.arange(BLOCK)
    lag_matrix = places[:, None] - places[None, :]
    one_hot = (lag_matrix[:, :, None] == places[None, None, :]).astype(number_type)
    toeplitz = jnp.einsum("hl,tsl->hts", kernel, one_hot, precision=PRECISE)
    signal_blocks = signal.reshape(blocks, BLOCK, channels)
    segment_blocks = segments.reshape(blocks, BLOCK)
    same_segment = (segment_blocks[:, :, None] == segment_blocks[:, None, :]).astype(number_type)
    weighted = toeplitz[None] * same_segment[:, None]
    within = jnp.einsum("khts,ksh->kth", weighted, signal_blocks, precision=PRECISE)
    block_last = segment_blocks[:, -1]
    kept_rows = (
        signal_blocks * (segment_blocks == block_last[:, None]).astype(number_type)[:, :, None]
    )
    reverse_real = power_real[..., :BLOCK][..., ::-1]
    reverse_imaginary = power_imaginary[..., :BLOCK][..., ::-1]
    added_real = jnp.einsum("hns,ksh->khn", reverse_real, kept_rows, precision=PRECISE)
    added_imaginary = jnp.einsum("hns,ksh->khn", reverse_imaginary, kept_rows, precision=PRECISE)
    jump_real = power_real[..., BLOCK]
    jump_imaginary = power_imaginary[..., BLOCK]
    block_links = jnp.concatenate(
        [jnp.zeros((1,), number_type), (block_last[1:] == block_last[:-1]).astype(number_type)]
    )

    def advance(carried, pieces):
        state_real, state_imaginary = carried
        linked, add_real, add_imaginary = pieces
        new_real = linked * (jump_real * state_real - jump_imaginary * state_imaginary) + add_real
        new_imaginary = (
            linked * (jump_real * state_imaginary + jump_imaginary * state_real) + add_imaginary
        )
        return ((new_real, new_imaginary), (new_real, new_imaginary))

    zeros_state = jnp.zeros_like(jump_real)
    unused, states = lax.scan(
        advance, (zeros_state, zeros_state), (block_links, added_real, added_imaginary)
    )
    return (within.reshape(length, channels), states[0], states[1])


def state_part(
    segments,
    previous,
    ends_real,
    ends_imaginary,
    incoming_real,
    incoming_imaginary,
    rate_real,
    rate_imaginary,
    readout_real,
    readout_imaginary,
):
    length = segments.shape[0]
    blocks = length // BLOCK
    number_type = ends_real.dtype
    segment_blocks = segments.reshape(blocks, BLOCK)
    block_last = segment_blocks[:, -1]
    ahead_steps = jnp.arange(1, BLOCK + 1).astype(number_type)
    ahead_real, ahead_imaginary = powers(rate_real, rate_imaginary, ahead_steps)
    read_real = (
        readout_real[..., None] * ahead_real - readout_imaginary[..., None] * ahead_imaginary
    )
    read_imaginary = (
        readout_real[..., None] * ahead_imaginary + readout_imaginary[..., None] * ahead_real
    )
    span_steps = BLOCK * jnp.arange(1, blocks + 1).astype(number_type)
    span_real, span_imaginary = powers_first(rate_real, rate_imaginary, span_steps)
    carry_mask = (block_last == previous).astype(number_type)[:, None, None]
    full_real = ends_real + carry_mask * (
        span_real * incoming_real - span_imaginary * incoming_imaginary
    )
    full_imaginary = ends_imaginary + carry_mask * (
        span_real * incoming_imaginary + span_imaginary * incoming_real
    )
    start_real = jnp.concatenate([incoming_real[None], full_real[:-1]], 0)
    start_imaginary = jnp.concatenate([incoming_imaginary[None], full_imaginary[:-1]], 0)
    start_segment = jnp.concatenate(
        [jnp.reshape(previous, (1,)).astype(number_type), block_last[:-1]]
    )
    alive_mask = (segment_blocks == start_segment[:, None]).astype(number_type)
    reached = jnp.einsum("hnt,khn->kth", read_real, start_real, precision=PRECISE) - jnp.einsum(
        "hnt,khn->kth", read_imaginary, start_imaginary, precision=PRECISE
    )
    return (reached * alive_mask[:, :, None]).reshape(length, -1)


def end_part(linked, length_value, incoming_real, incoming_imaginary, rate_real, rate_imaginary):
    magnitude = jnp.exp(length_value * rate_real) * linked
    angles = length_value * rate_imaginary
    far_real = magnitude * jnp.cos(angles)
    far_imaginary = magnitude * jnp.sin(angles)
    return (
        far_real * incoming_real - far_imaginary * incoming_imaginary,
        far_real * incoming_imaginary + far_imaginary * incoming_real,
    )


def normalize(values, norm_gain, norm_bias):
    center = jnp.mean(values, axis=-1, keepdims=True)
    shifted = values - center
    spread = jnp.mean(shifted * shifted, axis=-1, keepdims=True)
    return shifted * lax.rsqrt(spread + EPSILON) * norm_gain + norm_bias


def smooth_gate(values):
    return jax.nn.gelu(values, approximate=True)


def join_states(earlier, following):
    early_real, early_imaginary, early_add_real, early_add_imaginary, early_first, early_last = (
        earlier
    )
    late_real, late_imaginary, late_add_real, late_add_imaginary, late_first, late_last = following
    joined = ((early_last == late_first) | (early_last < 0) | (late_first < 0)).astype(
        early_real.dtype
    )
    return (
        joined * (late_real * early_real - late_imaginary * early_imaginary),
        joined * (late_real * early_imaginary + late_imaginary * early_real),
        joined * (late_real * early_add_real - late_imaginary * early_add_imaginary)
        + late_add_real,
        joined * (late_real * early_add_imaginary + late_imaginary * early_add_real)
        + late_add_imaginary,
        jnp.where(early_first < 0, late_first, early_first),
        jnp.where(late_last < 0, early_last, late_last),
    )


def join_grads(earlier, following):
    early_real, early_imaginary, early_add_real, early_add_imaginary = earlier
    late_real, late_imaginary, late_add_real, late_add_imaginary = following
    return (
        late_real * early_real - late_imaginary * early_imaginary,
        late_real * early_imaginary + late_imaginary * early_real,
        late_real * early_add_real - late_imaginary * early_add_imaginary + late_add_real,
        late_real * early_add_imaginary + late_imaginary * early_add_real + late_add_imaginary,
    )


def per_device(
    inputs,
    teacher,
    segment_ids,
    valid_mask,
    norm_gain,
    norm_bias,
    gate_weight,
    gate_bias,
    reduce_weight,
    reduce_bias,
    damping,
    frequency,
    timestep,
    mix_real,
    mix_imaginary,
    expand_weight,
    expand_bias,
    output_weight,
    output_bias,
):
    rows_in = inputs.astype(jnp.float32)
    normed = normalize(rows_in, norm_gain, norm_bias).astype(jnp.bfloat16)
    gate_full, reduce_full, expand_full, output_full = (
        lax.all_gather(gate_weight, "shard", axis=0, tiled=True),
        lax.all_gather(reduce_weight, "shard", axis=0, tiled=True),
        lax.all_gather(expand_weight, "shard", axis=0, tiled=True),
        lax.all_gather(output_weight, "shard", axis=1, tiled=True),
    )
    gate_pre = jnp.dot(normed, gate_full, preferred_element_type=jnp.float32) + gate_bias
    gate_act, gate_pull = jax.vjp(smooth_gate, gate_pre)
    reduce_pre = jnp.dot(normed, reduce_full, preferred_element_type=jnp.float32) + reduce_bias
    reduced, reduce_pull = jax.vjp(smooth_gate, reduce_pre)
    segment_float = segment_ids[0].astype(jnp.float32)
    span_length = segment_float.shape[0]
    rate_terms, rate_pull = jax.vjp(
        coefficients, damping, frequency, timestep, mix_real, mix_imaginary
    )
    rate_real, rate_imaginary = (rate_terms[0], rate_terms[1])
    intra_out, intra_pull = jax.vjp(partial(intra_part, segment_float), reduced, *rate_terms)
    within, ends_real, ends_imaginary = intra_out
    far_real, far_imaginary = powers(
        rate_real, rate_imaginary, jnp.full((1,), span_length, jnp.float32)
    )
    far_real = far_real[..., 0]
    far_imaginary = far_imaginary[..., 0]
    whole_span = (segment_float[0] == segment_float[-1]).astype(jnp.float32)
    ones_state = jnp.ones_like(far_real)
    zeros_state = jnp.zeros_like(far_real)
    unknown = jnp.full((), -1.0, jnp.float32)
    before = prefix(
        (
            whole_span * far_real,
            whole_span * far_imaginary,
            ends_real[-1],
            ends_imaginary[-1],
            segment_float[0],
            segment_float[-1],
        ),
        "context",
        join_states,
        (ones_state, zeros_state, zeros_state, zeros_state, unknown, unknown),
    )
    incoming_real, incoming_imaginary, previous = (before[2], before[3], before[5])
    reached, state_pull = jax.vjp(
        partial(state_part, segment_float, previous),
        ends_real,
        ends_imaginary,
        incoming_real,
        incoming_imaginary,
        *rate_terms
    )
    mixed_rows = (within + reached).astype(jnp.bfloat16)
    mixed_full = lax.all_gather(mixed_rows, "tensor", axis=1, tiled=True)
    expanded = jnp.dot(mixed_full, expand_full, preferred_element_type=jnp.float32) + expand_bias
    gated_rows = (expanded * gate_act).astype(jnp.bfloat16)
    branch = lax.psum(
        jnp.dot(gated_rows, output_full, preferred_element_type=jnp.float32), "tensor"
    )
    result = rows_in + branch + output_bias
    difference = result - teacher.astype(jnp.float32)
    mask_row = valid_mask[0].astype(jnp.float32)
    errors = jnp.sum(difference * difference, axis=-1)
    error_total, counted = lax.psum(
        (jnp.sum(mask_row * errors), jnp.sum(mask_row)), ("shard", "context")
    )
    tokens_all = span_length * lax.axis_size("shard") * lax.axis_size("context")
    loss_value = error_total / (counted * inputs.shape[1])
    result_back = tokens_all / counted * mask_row[:, None] * difference
    branch_back = result_back.astype(jnp.bfloat16)
    output_grad = jnp.dot(gated_rows.T, branch_back, preferred_element_type=jnp.float32)
    gated_back = jnp.dot(branch_back, output_full.T, preferred_element_type=jnp.float32)
    expanded_back = gated_back * gate_act
    activation_back = gated_back * expanded
    expand_low = expanded_back.astype(jnp.bfloat16)
    expand_grad = jnp.dot(mixed_full.T, expand_low, preferred_element_type=jnp.float32)
    mixed_back = lax.psum_scatter(
        jnp.dot(expand_low, expand_full.T, preferred_element_type=jnp.float32),
        "tensor",
        scatter_dimension=1,
        tiled=True,
    )
    (gate_pre_back,) = gate_pull(activation_back)
    state_grads = state_pull(mixed_back)
    linked = (segment_float[-1] == previous).astype(jnp.float32)
    behind = prefix_2(
        (linked * far_real, -linked * far_imaginary, state_grads[2], state_grads[3]),
        "context",
        join_grads,
        (ones_state, zeros_state, zeros_state, zeros_state),
    )
    leaving_real, leaving_imaginary = (behind[2], behind[3])
    unused, end_pull = jax.vjp(
        partial(end_part, linked, float(span_length), incoming_real, incoming_imaginary),
        rate_real,
        rate_imaginary,
    )
    end_rates = end_pull((leaving_real, leaving_imaginary))
    ends_real_back = state_grads[0].at[-1].add(leaving_real)
    ends_imaginary_back = state_grads[1].at[-1].add(leaving_imaginary)
    intra_grads = intra_pull((mixed_back, ends_real_back, ends_imaginary_back))
    signal_back = intra_grads[0]
    rate_grads = (
        intra_grads[1] + state_grads[4] + end_rates[0],
        intra_grads[2] + state_grads[5] + end_rates[1],
        intra_grads[3] + state_grads[6],
        intra_grads[4] + state_grads[7],
    )
    damping_grad, frequency_grad, timestep_grad, mix_real_grad, mix_imaginary_grad = rate_pull(
        rate_grads
    )
    (reduce_pre_back,) = reduce_pull(signal_back)
    gate_low = gate_pre_back.astype(jnp.bfloat16)
    reduce_low = reduce_pre_back.astype(jnp.bfloat16)
    gate_grad = jnp.dot(normed.T, gate_low, preferred_element_type=jnp.float32)
    reduce_grad = jnp.dot(normed.T, reduce_low, preferred_element_type=jnp.float32)
    normed_part = jnp.dot(gate_low, gate_full.T, preferred_element_type=jnp.float32) + jnp.dot(
        reduce_low, reduce_full.T, preferred_element_type=jnp.float32
    )
    normed_back = lax.psum(normed_part, "tensor")
    unused_norm, norm_pull = jax.vjp(normalize, rows_in, norm_gain, norm_bias)
    rows_back, gain_grad, bias_grad = norm_pull(normed_back)
    inputs_grad = (result_back + rows_back).astype(jnp.bfloat16)
    small_sums = (
        lax.psum(gain_grad.astype(jnp.bfloat16), ("shard", "context")).astype(jnp.float32),
        lax.psum(bias_grad.astype(jnp.bfloat16), ("shard", "context")).astype(jnp.float32),
        lax.psum(jnp.sum(gate_pre_back, axis=0).astype(jnp.bfloat16), ("shard", "context")).astype(
            jnp.float32
        ),
        lax.psum(
            jnp.sum(reduce_pre_back, axis=0).astype(jnp.bfloat16), ("shard", "context")
        ).astype(jnp.float32),
        lax.psum(damping_grad.astype(jnp.bfloat16), ("shard", "context")).astype(jnp.float32),
        lax.psum(frequency_grad.astype(jnp.bfloat16), ("shard", "context")).astype(jnp.float32),
        lax.psum(timestep_grad.astype(jnp.bfloat16), ("shard", "context")).astype(jnp.float32),
        lax.psum(mix_real_grad.astype(jnp.bfloat16), ("shard", "context")).astype(jnp.float32),
        lax.psum(mix_imaginary_grad.astype(jnp.bfloat16), ("shard", "context")).astype(jnp.float32),
        lax.psum(jnp.sum(expanded_back, axis=0).astype(jnp.bfloat16), ("shard", "context")).astype(
            jnp.float32
        ),
        lax.psum(jnp.sum(result_back, axis=0).astype(jnp.bfloat16), ("shard", "context")).astype(
            jnp.float32
        ),
    )
    local_grads = (gate_grad, reduce_grad, expand_grad, output_grad)
    paired = (
        lax.psum(local_grads[0].astype(jnp.bfloat16), "context").astype(jnp.float32),
        lax.psum(local_grads[1].astype(jnp.bfloat16), "context").astype(jnp.float32),
        lax.psum(local_grads[2].astype(jnp.bfloat16), "context").astype(jnp.float32),
        lax.psum(local_grads[3].astype(jnp.bfloat16), "context").astype(jnp.float32),
    )
    owned_grads = (
        lax.psum_scatter(paired[0], "shard", scatter_dimension=0, tiled=True),
        lax.psum_scatter(paired[1], "shard", scatter_dimension=0, tiled=True),
        lax.psum_scatter(paired[2], "shard", scatter_dimension=0, tiled=True),
        lax.psum_scatter(paired[3], "shard", scatter_dimension=1, tiled=True),
    )
    return (
        result.astype(jnp.bfloat16),
        loss_value,
        inputs_grad,
        small_sums[0],
        small_sums[1],
        owned_grads[0],
        small_sums[2],
        owned_grads[1],
        small_sums[3],
        small_sums[4],
        small_sums[5],
        small_sums[6],
        small_sums[7],
        small_sums[8],
        owned_grads[2],
        small_sums[9],
        owned_grads[3],
        small_sums[10],
    )


def solution(mesh):
    placed = (
        P(("shard", "context"), None),
        P(("shard", "context"), None),
        P("shard", "context"),
        P("shard", "context"),
        P(),
        P(),
        P("shard", "tensor"),
        P("tensor"),
        P("shard", "tensor"),
        P("tensor"),
        P("tensor", None),
        P("tensor", None),
        P("tensor"),
        P("tensor", None),
        P("tensor", None),
        P("shard", "tensor"),
        P("tensor"),
        P("tensor", "shard"),
        P(),
    )
    return jax.shard_map(
        per_device,
        mesh=mesh,
        in_specs=placed,
        out_specs=(
            P(("shard", "context"), None),
            P(),
            P(("shard", "context"), None),
            P(),
            P(),
            P("shard", "tensor"),
            P("tensor"),
            P("shard", "tensor"),
            P("tensor"),
            P("tensor", None),
            P("tensor", None),
            P("tensor"),
            P("tensor", None),
            P("tensor", None),
            P("shard", "tensor"),
            P("tensor"),
            P("tensor", "shard"),
            P(),
        ),
        check_vma=False,
    )
```

profile of v0, /device:TPU:0, one launch (start us, length us, event | category | flops | bytes accessed | tf_op | source)
XLA Modules:
  0.0 1578.7 jit_solution(11804288709635568111)
XLA Ops:
  20.6 70.1 %fusion.23 = (f32[128,512,65]{1,2,0:T(8,128)S(1)}, f32[128,512,65]{1,2,0:T(8,128)}) fusion(f32[128,512]{1,0:T(8,128)S(1)} %get-tuple-element.1018, f32[65]{0:T(128)S(1)} %iota_convert_fusion, f32[128,512]{1,0:T(8,128)S(1)} %get-tuple-element.1017), kind=kLoop, calls=%fused_computation.53 | loop fusion | flops 17039360 | bytes 34603268 | tf_op jit(solution)/shard_map/jvp()/mul | solution.py:79
  131.2 22.5 %rev.13 = f32[128,512,64]{1,2,0:T(8,128)} reverse(f32[128,512,64]{1,2,0:T(8,128)} %slice.117), dimensions={2} | reverse | bytes 33554432 | tf_op jit(solution)/shard_map/jvp()/rev | solution.py:111
  153.7 22.4 %rev.12 = f32[128,512,64]{1,2,0:T(8,128)} reverse(f32[128,512,64]{1,2,0:T(8,128)} %slice.116), dimensions={2} | reverse | bytes 33554432 | tf_op jit(solution)/shard_map/jvp()/rev | solution.py:110
  204.6 52.2 %while.85 = (s32[]{:T(128)}, f32[128,512]{1,0:T(8,128)S(1)}, f32[128,512]{1,0:T(8,128)S(1)}, f32[8,128,512]{2,1,0:T(8,128)}, f32[8,128,512]{2,1,0:T(8,128)}, /*i...) while((s32[]{:T(128)}, f32[128,512]{1,0:T(8,128)S(1)}, ...), condition=%wide.region_3.4_spmd.clone, body=%wide.region_2.3_spmd.clone.sunk | while | flops 786435 | bytes 4194987 | solution.py:130
  295.5 16.9 %fusion.174 = f32[128,1,64]{2,1,0:T(1,128)S(1)} fusion(f32[128,512,1]{1,0,2:T(8,128)S(1)} %bitcast.279, f32[128,512,65]{1,2,0:T(8,128)} %get-tuple-element.1016), kind=kOutput, calls=%fused_computation.270 | convolution fusion | flops 50331648 | bytes 17072128 | tf_op jit(solution)/shard_map/jvp(hn,hnl->hl)/dot_general | solution.py:94
  337.7 77.3 %fusion.48 = f32[128,8,64]{2,1,0:T(8,128)S(1)} fusion(f32[128,512]{1,0:T(8,128)S(1)} %copy-done.57, f32[128,512]{1,0:T(8,128)S(1)} %get-tuple-element.1018, f32[64]{0:T(128)S(1)} %copy-done.122, f32[128,512]{1,0:T(8,128)S(1)} %get-tuple-element.1017, f32[128,512]{1,0:T(8,128)S(1)} %copy-done.54, f32[7,128,512]{2,0,1:T(8,128)S(1)} %get-tuple-element.1001, ...), kind=kOutput, calls=%fused_computation.95 | convolution fusion | flops 432537600 | bytes 3408128 | tf_op jit(solution)/shard_map/jvp(hnt,khn->kth)/dot_general | solution.py:176
  415.1 78.3 %fusion.133 = bf16[8,64,128]{1,0,2:T(8,128)(2,1)} fusion(f32[128,8,64]{2,1,0:T(8,128)S(1)} %fusion.48, f32[128,512]{1,0:T(8,128)S(1)} %copy-done.57, f32[128,512]{1,0:T(8,128)S(1)} %get-tuple-element.1018, f32[64]{0:T(128)S(1)} %copy-done.122, f32[128,512]{1,0:T(8,128)S(1)} %get-tuple-element.1017, f32[128,512]{1,0:T(8,128)S(1)} %copy-done.54, ...), kind=kOutput, calls=%fused_computation.214 | convolution fusion | flops 432799744 | bytes 3803392 | tf_op jit(solution)/shard_map/jvp(hnt,khn->kth)/dot_general | solution.py:176
  550.0 69.3 %all-reduce.19.cloned.1.call-done = f32[512,1024]{1,0:T(8,128)} async-done(((f32[512,1024]{1,0:T(8,128)}), f32[512,1024]{1,0:T(8,128)}) %all-reduce.19.cloned.1.call-update) | async-done | bytes 2097168 | tf_op jit(solution)/shard_map/psum | solution.py:311
  664.7 72.8 %fusion.107 = f32[8,128,512]{2,0,1:T(8,128)} fusion(f32[128,512]{1,0:T(8,128)S(1)} %copy-done.58, f32[128,512]{1,0:T(8,128)S(1)} %get-tuple-element.1018, f32[64]{0:T(128)S(1)} %copy-done.122, f32[128,512]{1,0:T(8,128)S(1)} %get-tuple-element.1017, f32[128,512]{1,0:T(8,128)S(1)} %copy-done.55, f32[8,64,128]{1,0,2:T(8,128)S(1)} %copy.121, ...), kind=kOutput, calls=%fused_computation.190 | convolution fusion | flops 432078848 | bytes 3410176 | tf_op jit(solution)/shard_map/transpose(jvp(hnt,khn->kth))/dot_general | solution.py:176
  737.5 73.0 %fusion.106 = f32[8,128,512]{2,0,1:T(8,128)} fusion(f32[128,512]{1,0:T(8,128)S(1)} %copy-done.58, f32[128,512]{1,0:T(8,128)S(1)} %get-tuple-element.1018, f32[64]{0:T(128)S(1)} %copy-done.122, f32[128,512]{1,0:T(8,128)S(1)} %get-tuple-element.1017, f32[128,512]{1,0:T(8,128)S(1)} %copy-done.55, f32[8,64,128]{1,0,2:T(8,128)S(1)} %copy.121, ...), kind=kOutput, calls=%fused_computation.189 | convolution fusion | flops 432144384 | bytes 3410176 | tf_op jit(solution)/shard_map/transpose(jvp(hnt,khn->kth))/dot_general | solution.py:176
  873.8 98.9 %fusion.46 = (f32[128,512]{1,0:T(8,128)}, f32[128,512]{1,0:T(8,128)}, f32[128,512]{1,0:T(8,128)S(1)}, f32[128,512]{1,0:T(8,128)S(1)}, f32[128,512]{1,0:T(8,128)S...) fusion(f32[128,512]{1,0:T(8,128)S(1)} %get-tuple-element.1018, ...), kind=kOutput, calls=%fused_computation.83 | convolution fusion | flops 549650432 | bytes 55380224 | tf_op jit(solution)/shard_map/transpose(jvp(hnt,khn->kth))/dot_general | solution.py:176
  987.4 75.9 %while.86 = (s32[]{:T(128)}, f32[128,512]{1,0:T(8,128)}, f32[128,512]{1,0:T(8,128)S(1)}, f32[128,512]{1,0:T(8,128)}, f32[128,512]{1,0:T(8,128)}, /*index=5*/f32[...) while((s32[]{:T(128)}, f32[128,512]{1,0:T(8,128)}, ...), condition=%wide.region_20.21_spmd.clone, body=%wide.region_19.20_spmd.clone.sunk | while | flops 1507332 | bytes 8388884 | solution.py:130
  1063.3 17.7 %fusion.100 = f32[128,8,64]{2,1,0:T(8,128)} fusion(f32[128,512,64]{1,2,0:T(8,128)} %rev.12, f32[128,8,512]{2,0,1:T(8,128)S(1)} %bitcast.268), kind=kOutput, calls=%fused_computation.176 | convolution fusion | flops 402653184 | bytes 19136512 | tf_op jit(solution)/shard_map/transpose(jvp(hns,ksh->khn))/dot_general | solution.py:112
  1098.4 17.5 %fusion.102 = f32[128,512,64]{1,2,0:T(8,128)} fusion(f32[128,8,512]{2,0,1:T(8,128)} %bitcast.270, f32[8,64,128]{1,0,2:T(8,128)S(1)} %copy-done.20, f32[8,64]{1,0:T(8,128)S(1)} %copy-done.82), kind=kOutput, calls=%fused_computation.178 | convolution fusion | flops 402718720 | bytes 19138560 | tf_op jit(solution)/shard_map/transpose(jvp(hns,ksh->khn))/dot_general | solution.py:113
  1115.9 17.8 %fusion.127 = f32[8,64,128]{1,0,2:T(8,128)} fusion(f32[128,8,64]{2,1,0:T(8,128)S(1)} %copy-done.50, f32[128,512,64]{1,2,0:T(8,128)} %rev.13, f32[128,8,512]{2,0,1:T(8,128)S(1)} %bitcast.271, f32[8,128,64]{2,0,1:T(8,128)S(1)} %copy.151, f32[8,64]{1,0:T(8,128)S(1)} %copy-done.82), kind=kOutput, calls=%fused_computation.209 | convolution fusion | flops 402849792 | bytes 19662848 | tf_op jit(solution)/shard_map/transpose(jvp(hns,ksh->khn))/dot_general | solution.py:113
  1136.7 22.3 %rev.15 = f32[128,512,64]{1,2,0:T(8,128)} reverse(f32[128,512,64]{1,2,0:T(8,128)} %fusion.98), dimensions={2} | reverse | bytes 33554432 | tf_op jit(solution)/shard_map/transpose(jvp())/rev | solution.py:110
  1159.1 22.3 %rev.14 = f32[128,512,64]{1,2,0:T(8,128)} reverse(f32[128,512,64]{1,2,0:T(8,128)} %fusion.102), dimensions={2} | reverse | bytes 33554432 | tf_op jit(solution)/shard_map/transpose(jvp())/rev | solution.py:111
  1182.4 82.2 %fusion.36 = (f32[128,512]{1,0:T(8,128)S(1)}, f32[128,512]{1,0:T(8,128)S(1)}) fusion(f32[128,512]{1,0:T(8,128)S(1)} %copy-done.32, f32[65]{0:T(128)S(1)} %copy-done.105, f32[128,512]{1,0:T(8,128)S(1)} %copy-done.30, f32[128,512,64]{1,2,0:T(8,128)} %get-tuple-element.1019, f32[128,512,64]{1,2,0:T(8,128)} %rev.14, f32[128,512,1]{1,2,0:T(1,128)S(1)} %broadcast_in_dim.47, ...), kind=kLoop, calls=%fused_computation.70 | loop fusion | flops 85065728 | bytes 68681984 | tf_op jit(solution)/shard_map/transpose(jvp())/reduce_sum | solution.py:78
  1302.2 23.3 %all-reduce.23.cloned.1.call-done = (bf16[128,512]{1,0:T(8,128)(2,1)}, bf16[128,512]{1,0:T(8,128)(2,1)}, bf16[128,512]{1,0:T(8,128)(2,1)}, bf16[128,512]{1,0:T(8,128)(2,1)}) async-done(((bf16[128,512]{1,0:T(8,128)(2,1)}, bf16[128,512]{1,0:T(8,128)(2,1)}, bf16[128,512]{1,0:T(8,128)(2,1)}, bf16[128,512]{1,0:T(8,128)(2,1)}), (bf16[128,512]{1,0:T(8,128)(2,1)}, bf16[128,512]{1,0:T(8,128)(2,1)}, ...) | async-done | bytes 524304 | tf_op jit(solution)/shard_map/psum | solution.py:387
  1332.1 81.7 %all-reduce.21.cloned.1.call-done = f32[512,1024]{1,0:T(8,128)} async-done(((f32[512,1024]{1,0:T(8,128)}), f32[512,1024]{1,0:T(8,128)}) %all-reduce.21.cloned.1.call-update) | async-done | bytes 2097168 | tf_op jit(solution)/shard_map/psum | solution.py:374
  1417.1 24.1 %all-reduce.10 = (bf16[1024]{0:T(1024)(128)(2,1)S(1)}, bf16[1024]{0:T(1024)(128)(2,1)S(1)}, bf16[768]{0:T(1024)(128)(2,1)S(1)}, bf16[128]{0:T(256)(128)(2,1)S(1)...) all-reduce(bf16[1024]{0:T(1024)(128)(2,1)S(1)} %get-tuple-element.8, ...), channel_id=1, replica_groups=mesh['shard'=4,'context'=2,'tensor'=4] {'shard','context'}, use_global_device_ids=true, to_apply=%region_25.26 | all-reduce | flops 4864 | bytes 19456 | tf_op jit(solution)/shard_map/psum | solution.py:379
  1448.6 27.1 %reduce-scatter.12.cloned.1.call-done = f32[128,768]{1,0:T(8,128)} async-done(((f32[512,768]{1,0:T(8,128)}), f32[128,768]{1,0:T(8,128)}) %reduce-scatter.12.cloned.1.call-update) | async-done | bytes 393232 | tf_op jit(solution)/shard_map/reduce_scatter | solution.py:409
  1475.7 47.4 %reduce-scatter.8.cloned.1.call-done = f32[256,768]{1,0:T(8,128)} async-done(((f32[1024,768]{1,0:T(8,128)}), f32[256,768]{1,0:T(8,128)}) %reduce-scatter.8.cloned.1.call-update) | async-done | bytes 786448 | tf_op jit(solution)/shard_map/reduce_scatter | solution.py:407
  1523.1 47.5 %reduce-scatter.14.cloned.1.call-done = f32[768,256]{1,0:T(8,128)} async-done(((f32[768,1024]{1,0:T(8,128)}), f32[768,256]{1,0:T(8,128)}) %reduce-scatter.14.cloned.1.call-update) | async-done | bytes 786448 | tf_op jit(solution)/shard_map/reduce_scatter | solution.py:410
  (532 shorter events, 514.5 us)
Async XLA Ops:
  7.2 516.9 %all-gather.7.cloned.1.call-start = ((), (), s32[]{:S(2)}) async-start(), calls=%async_computation.5 | async-start | bytes 1966080 | tf_op jit(solution)/shard_map/all_gather | solution.py:259
  7.9 522.0 %all-gather.9.cloned.1.call-start = ((), (), s32[]{:S(2)}) async-start(), calls=%async_computation.6 | async-start | bytes 1966080 | tf_op jit(solution)/shard_map/all_gather | solution.py:262
  8.7 610.7 %all-reduce.19.cloned.1.call-start = ((), (), s32[]{:S(2)}) async-start(), calls=%async_computation.7 | async-start | bytes 4194304 | tf_op jit(solution)/shard_map/psum | solution.py:311
  20.6 257.9 %copy-start.56 = (f32[128,512]{1,0:T(8,128)}, f32[128,512]{1,0:T(8,128)S(1)}, u32[]{:S(2)}) copy-start(f32[128,512]{1,0:T(8,128)S(1)} %get-tuple-element.1008) | copy-start | bytes 786436
  20.6 274.9 %copy-start.53 = (f32[128,512]{1,0:T(8,128)}, f32[128,512]{1,0:T(8,128)S(1)}, u32[]{:S(2)}) copy-start(f32[128,512]{1,0:T(8,128)S(1)} %get-tuple-element.1007) | copy-start | bytes 786436
  20.6 853.1 %copy-start.29 = (f32[128,512]{1,0:T(8,128)}, f32[128,512]{1,0:T(8,128)S(1)}, u32[]{:S(2)}) copy-start(f32[128,512]{1,0:T(8,128)S(1)} %get-tuple-element.1017) | copy-start | bytes 786436
  20.6 853.1 %copy-start.31 = (f32[128,512]{1,0:T(8,128)}, f32[128,512]{1,0:T(8,128)S(1)}, u32[]{:S(2)}) copy-start(f32[128,512]{1,0:T(8,128)S(1)} %get-tuple-element.1018) | copy-start | bytes 786436
  130.9 189.6 %copy-start.44 = (f32[512,128]{1,0:T(8,128)}, f32[512,128]{1,0:T(8,128)S(1)}, u32[]{:S(2)}) copy-start(f32[512,128]{1,0:T(8,128)S(1)} %get-tuple-element.1027) | copy-start | bytes 786436
  331.6 519.6 %copy-start.8 = (f32[128,512]{1,0:T(8,128)}, f32[128,512]{1,0:T(8,128)S(1)}, u32[]{:S(2)}) copy-start(f32[128,512]{1,0:T(8,128)S(1)} %get-tuple-element.615) | copy-start | bytes 786436
  331.6 519.6 %copy-start.10 = (f32[128,512]{1,0:T(8,128)}, f32[128,512]{1,0:T(8,128)S(1)}, u32[]{:S(2)}) copy-start(f32[128,512]{1,0:T(8,128)S(1)} %get-tuple-element.613) | copy-start | bytes 786436
  415.1 109.0 %copy-start.38 = (bf16[512,1024]{1,0:T(8,128)(2,1)S(1)}, bf16[512,1024]{1,0:T(8,128)(2,1)}, u32[]{:S(2)}) copy-start(bf16[512,1024]{1,0:T(8,128)(2,1)} %copy-done.37) | copy-start | bytes 3145732
  415.1 109.0 %copy-start.115 = (f32[768]{0:T(1024)S(1)}, f32[768]{0:T(1024)}, u32[]{:S(2)}) copy-start(f32[768]{0:T(1024)} %param.38) | copy-start | bytes 9220
  534.1 121.2 %reduce-scatter.6.cloned.1.call-start = ((), (), s32[]{:S(2)}) async-start(), calls=%async_computation.8 | async-start | bytes 1310720 | tf_op jit(solution)/shard_map/reduce_scatter | solution.py:331
  629.0 646.3 %all-reduce.25.cloned.1.call-start = ((), (), s32[]{:S(2)}) async-start(), calls=%async_computation.15 | async-start | bytes 8388608 | tf_op jit(solution)/shard_map/psum | solution.py:401
  873.8 98.9 %copy-start.33 = (f32[128,512]{1,0:T(8,128)S(1)}, f32[128,512]{1,0:T(8,128)}, u32[]{:S(2)}) copy-start(f32[128,512]{1,0:T(8,128)} %param.42) | copy-start | bytes 786436
  1181.4 144.2 %all-reduce.23.cloned.1.call-start = ((), (), s32[]{:S(2)}) async-start(), calls=%async_computation.14 | async-start | bytes 1048576 | tf_op jit(solution)/shard_map/psum | solution.py:387
  1271.8 142.0 %all-reduce.21.cloned.1.call-start = ((), (), s32[]{:S(2)}) async-start(), calls=%async_computation.9 | async-start | bytes 4194304 | tf_op jit(solution)/shard_map/psum | solution.py:374
  1275.3 173.4 %reduce-scatter.10.cloned.1.call-start = ((), (), s32[]{:S(2)}) async-start(), calls=%async_computation.11 | async-start | bytes 655360 | tf_op jit(solution)/shard_map/reduce_scatter | solution.py:408
  1277.2 198.5 %reduce-scatter.12.cloned.1.call-start = ((), (), s32[]{:S(2)}) async-start(), calls=%async_computation.12 | async-start | bytes 1966080 | tf_op jit(solution)/shard_map/reduce_scatter | solution.py:409
  1279.7 243.4 %reduce-scatter.8.cloned.1.call-start = ((), (), s32[]{:S(2)}) async-start(), calls=%async_computation.10 | async-start | bytes 3932160 | tf_op jit(solution)/shard_map/reduce_scatter | solution.py:407
  1281.7 288.9 %reduce-scatter.14.cloned.1.call-start = ((), (), s32[]{:S(2)}) async-start(), calls=%async_computation.13 | async-start | bytes 3932160 | tf_op jit(solution)/shard_map/reduce_scatter | solution.py:410
  1285.1 128.7 %copy-start.3 = (bf16[512,1024]{1,0:T(8,128)(2,1)S(1)}, bf16[512,1024]{1,0:T(8,128)(2,1)}, u32[]{:S(2)}) copy-start(bf16[512,1024]{1,0:T(8,128)(2,1)} %param.31) | copy-start | bytes 3145732
  1285.1 128.7 %copy-start.84 = (f32[512]{0:T(512)S(1)}, f32[512]{0:T(512)}, u32[]{:S(2)}) copy-start(f32[512]{0:T(512)} %copy-done.83) | copy-start | bytes 6148
  1285.1 128.7 %copy-start.86 = (f32[1024]{0:T(1024)S(1)}, f32[1024]{0:T(1024)}, u32[]{:S(2)}) copy-start(f32[1024]{0:T(1024)} %param.35) | copy-start | bytes 12292
  (129 other events, 2999.2 us)
Sparse Core Ops, SparseCore 0:
  9.9 33.6 all-gather.6
  45.4 30.8 all-gather.8
  534.2 85.1 all-reduce.18
  629.1 26.0 reduce-scatter.5
  1181.5 27.3 all-reduce.24
  1271.9 53.5 all-reduce.22
  1327.9 85.8 all-reduce.20
  1417.4 23.7 reduce-scatter.9
  1444.7 30.9 reduce-scatter.11
  1479.1 43.9 reduce-scatter.7
  1526.6 43.9 reduce-scatter.13
where the time goes:
time: 1590 us; the launch traced here: 1580 us
  matrix products  595 us (37%)
  waiting for transfers between devices  314 us (20%)
  other arithmetic  304 us (19%)
  local copies, waits for them, and re-layouts  221 us (14%)
  blocking collectives  111 us (7%)
  between operations  22.1 us (1%)
    dot_general x3, matrix products, state_part(): jnp.einsum('hnt,khn->kth', read_real, start_real, precision=PRECISE)  249 us
    dot_general x3, matrix products, state_part(): jnp.einsum('hnt,khn->kth', read_imaginary, start_imaginary, precision=PRE...  168 us
    reduce_sum x1, other arithmetic, powers(): angles = rate_imaginary[..., None] * exponents  82.2 us
    psum x1, waiting for transfers between devices, per_device(): normed_back = lax.psum(normed_part, 'tensor')  81.7 us
    mul x1, other arithmetic, powers(): return (magnitude * jnp.cos(angles), magnitude * jnp.sin(angles))  70.1 us
    psum x1, waiting for transfers between devices, per_device(): lax.psum(jnp.dot(gated_rows, output_full, preferred_element_type=jnp.floa...  69.3 us
    dynamic_slice x40, local copies, waits for them, and re-layouts, intra_part(): lax.scan(advance, (zeros_state, zeros_state), (block_links, added_real, a...  60.7 us
    dot_general x3, matrix products, intra_part(): jnp.einsum('hns,ksh->khn', reverse_imaginary, kept_rows, precision=PRECISE)  47.7 us
  transfers between devices with their start and end apart: 11, of which 7 were waited for; matrix products, arithmetic and copies ran while one was open for 37% of the time, Pallas kernels for 0%

commit v1 on v0

v1 whole, which is shorter than its diff:
```python
from functools import partial

import jax
import jax.numpy as jnp
from jax import lax
from jax.experimental import pallas as pl
from jax.experimental.pallas import tpu as pltpu
from jax.sharding import PartitionSpec as P

BLOCK = 64
REACH = 256
EPSILON = 1e-05
F32 = jnp.float32
BF16 = jnp.bfloat16
VMEM_LIMIT = 50 * 1024 * 1024


def xor_pairs(size, mask):
    return [(i, i ^ mask) for i in range(size)]


def shift_pairs(size, step):
    return [(i, (i + step) % size) for i in range(size)]


def swap_context(x):
    return lax.ppermute(x, "context", [(0, 1), (1, 0)])


def sum_over(x, axis):
    size = lax.axis_size(axis)
    if size == 4:
        first = lax.ppermute(x, axis, xor_pairs(4, 1))
        second = lax.ppermute(x, axis, xor_pairs(4, 2))
        third = lax.ppermute(x, axis, xor_pairs(4, 3))
        return (x + first) + (second + third)
    step = 1
    while step < size:
        x = x + lax.ppermute(x, axis, xor_pairs(size, step))
        step *= 2
    return x


def gather_weight(w, axis):
    if lax.axis_size("shard") != 4 or lax.axis_size("context") != 2:
        return lax.all_gather(w, "shard", axis=axis, tiled=True)
    core = lax.axis_index("context")
    me = lax.axis_index("shard")
    rows, cols = w.shape
    half = rows // 2
    mine = lax.dynamic_slice_in_dim(w, core * half, half, 0)
    near = [lax.ppermute(mine, "shard", xor_pairs(4, k)) for k in (1, 2, 3)]
    far = [swap_context(a) for a in near]
    full = jnp.zeros((4, rows, cols), w.dtype)
    full = lax.dynamic_update_slice(full, w[None], (me, 0, 0))
    for k in (1, 2, 3):
        full = lax.dynamic_update_slice(full, near[k - 1][None], (me ^ k, core * half, 0))
        full = lax.dynamic_update_slice(full, far[k - 1][None], (me ^ k, (1 - core) * half, 0))
    if axis == 0:
        return full.reshape(4 * rows, cols)
    return full.transpose(1, 0, 2).reshape(rows, 4 * cols)


def scatter_grad(grad, axis):
    if lax.axis_size("shard") != 4 or lax.axis_size("context") != 2:
        paired = lax.psum(grad.astype(BF16), "context").astype(F32)
        return lax.psum_scatter(paired, "shard", scatter_dimension=axis, tiled=True)
    core = lax.axis_index("context")
    me = lax.axis_index("shard")
    if axis == 0:
        pieces = grad.reshape(4, 2, grad.shape[0] // 8, grad.shape[1])
    else:
        pieces = grad.reshape(2, grad.shape[0] // 2, 4, grad.shape[1] // 4).transpose(2, 0, 1, 3)
    keep = lax.dynamic_index_in_dim(pieces, core, 1, False)
    give = lax.dynamic_index_in_dim(pieces, 1 - core, 1, False).astype(BF16)
    paired = keep + swap_context(give).astype(F32)
    total = lax.dynamic_index_in_dim(paired, me, 0, False)
    sent = paired.astype(BF16)
    for k in (1, 2, 3):
        piece = lax.dynamic_index_in_dim(sent, me ^ k, 0, False)
        total = total + lax.ppermute(piece, "shard", xor_pairs(4, k)).astype(F32)
    other = swap_context(total)
    both = jnp.where(core == 0, jnp.stack([total, other]), jnp.stack([other, total]))
    return both.reshape(2 * total.shape[0], total.shape[1])


def scatter_rows(x):
    size = lax.axis_size("tensor")
    me = lax.axis_index("tensor")
    pieces = x.reshape(size, x.shape[0] // size, x.shape[1])
    total = lax.dynamic_index_in_dim(pieces, me, 0, False).astype(F32)
    for k in range(1, size):
        piece = lax.dynamic_index_in_dim(pieces, (me + k) % size, 0, False)
        total = total + lax.ppermute(piece, "tensor", shift_pairs(size, k)).astype(F32)
    return total


def gather_rows(x):
    size = lax.axis_size("tensor")
    me = lax.axis_index("tensor")
    full = jnp.zeros((size,) + x.shape, x.dtype)
    full = lax.dynamic_update_slice(full, x[None], (me, 0, 0))
    for k in range(1, size):
        part = lax.ppermute(x, "tensor", shift_pairs(size, k))
        full = lax.dynamic_update_slice(full, part[None], ((me - k) % size, 0, 0))
    return full


def cmul(ar, ai, br, bi):
    return ar * br - ai * bi, ar * bi + ai * br


def modes(damping, frequency, timestep):
    magnitude = jnp.exp(-timestep * damping)
    angle = timestep * frequency
    return magnitude * jnp.cos(angle), magnitude * jnp.sin(angle)


def ratios(damping, frequency, ar, ai):
    minus = ar - 1.0
    inverse = 1.0 / (damping * damping + frequency * frequency)
    return (ai * frequency - minus * damping) * inverse, -(
        minus * frequency + ai * damping
    ) * inverse


def low_powers(ar, ai, count):
    found = [None, (ar, ai)]
    for j in range(2, count):
        found.append(cmul(*found[j // 2], *found[j - j // 2]))
    return found


def taps_kernel(d_ref, f_ref, t_ref, mr_ref, mi_ref, k_ref, rev_ref, ar_s, ai_s, wr_s, wi_s, acc):
    damping, frequency, timestep = d_ref[...], f_ref[...], t_ref[...]
    ar, ai = modes(damping, frequency, timestep)
    qr, qi = ratios(damping, frequency, ar, ai)
    mr, mi = mr_ref[...], mi_ref[...]
    ar_s[...] = ar
    ai_s[...] = ai
    wr_s[...] = mr * qr - mi * qi
    wi_s[...] = mr * qi + mi * qr
    acc[...] = jnp.zeros_like(acc)

    def pair(p, carry):
        rows = pl.ds(pl.multiple_of(16 * p, 16), 16)
        a = (ar_s[rows, :], ai_s[rows, :])
        base = low_powers(*a, 8)
        eight = cmul(*base[4], *base[4])

        def outer(o, w):
            wr, wi = w
            at = pl.multiple_of(64 * o, 64)
            for j in range(8):
                term = wr if j == 0 else wr * base[j][0] - wi * base[j][1]
                acc[pl.ds(at + 8 * j, 8), :] += term[:8] + term[8:]
            return cmul(wr, wi, *eight)

        lax.fori_loop(0, REACH // 8, outer, (wr_s[rows, :], wi_s[rows, :]))
        return carry

    lax.fori_loop(0, ar_s.shape[0] // 16, pair, 0)
    k_ref[...] = jnp.sum(acc[...].reshape(REACH, 8, acc.shape[1]), axis=1)
    for l in range(REACH):
        rev_ref[REACH - 1 - l : REACH - l, :] = k_ref[l : l + 1, :]


def make_taps(damping, frequency, timestep, mix_real, mix_imaginary):
    count, channels = damping.shape
    return pl.pallas_call(
        taps_kernel,
        out_shape=[jax.ShapeDtypeStruct((REACH, channels), F32)] * 2,
        scratch_shapes=[pltpu.VMEM((count, channels), F32)] * 4
        + [pltpu.VMEM((REACH * 8, channels), F32)],
        compiler_params=pltpu.CompilerParams(vmem_limit_bytes=VMEM_LIMIT),
        cost_estimate=pl.CostEstimate(flops=80_000_000, bytes_accessed=2_000_000, transcendentals=200_000),
        name="taps",
    )(damping, frequency, timestep, mix_real, mix_imaginary)


def shifted_copies(source_ref, pad, copies, lead):
    length = copies.shape[1]
    pad[...] = jnp.zeros_like(pad)
    pad[64 : 64 + REACH, :] = source_ref[...]
    for r in range(8):
        start = 64 + lead - r
        copies[r, :, :] = pad[start : start + length, :]


def linked_blocks(seg, first, last, step, bound):
    def more(count):
        at = last + step * count
        edge = 64 * at + (63 if step < 0 else 0)
        mine = 64 * first + (0 if step < 0 else 63)
        return jnp.logical_and(count < bound, seg[jnp.clip(edge, 0, seg.shape[0] - 1)] == seg[mine])

    return lax.while_loop(more, lambda c: c + 1, 0)


def tile(at):
    return pl.ds(pl.multiple_of(8 * at, 8), 8)


def forward_kernel(seg, k_ref, u_ref, s_ref, y_ref, pad, copies, kept):
    channels = u_ref.shape[1]
    blocks = u_ref.shape[0] // 64
    ahead = REACH // 64
    shifted_copies(k_ref, pad, copies, 0)
    for b in range(blocks):
        rows = slice(64 * b, 64 * b + 64)
        kept[rows, :] = jnp.where(s_ref[rows, :] == seg[64 * b + 63], u_ref[rows, :], 0.0)

    def block(i, carry):
        mine = i + ahead
        zero = jnp.zeros((8, channels), F32)
        reach = linked_blocks(seg, mine, mine - 1, -1, ahead)

        def far(d, sums):
            sums = list(sums)
            at = pl.multiple_of(64 * (mine - 1 - d), 64)
            for r in range(8):
                taps = [copies[r, tile(8 * (d + 1) + m), :] for m in range(-7, 8)]
                for q in range(8):
                    u = kept[pl.ds(at + 8 * q + r, 1), :]
                    for t in range(8):
                        sums[t] += taps[t - q + 7] * u
            return tuple(sums)

        sums = lax.fori_loop(0, reach, far, (zero,) * 8)
        base = pl.multiple_of(64 * mine, 64)
        ids = [s_ref[pl.ds(base + 8 * t, 8), :] for t in range(8)]
        sums = [jnp.where(ids[t] == seg[64 * mine], sums[t], 0.0) for t in range(8)]
        for r in range(8):
            taps = [copies[r, 8 * m : 8 * m + 8, :] for m in range(8)]
            for q in range(8):
                u = u_ref[pl.ds(base + 8 * q + r, 1), :]
                own = s_ref[pl.ds(base + 8 * q + r, 1), :]
                for t in range(q, 8):
                    sums[t] += jnp.where(ids[t] == own, taps[t - q], 0.0) * u
        for t in range(0, 8, 2):
            both = jnp.concatenate([sums[t], sums[t + 1]], 0)
            y_ref[pl.ds(pl.multiple_of(64 * i + 8 * t, 16), 16), :] = both.astype(y_ref.dtype)
        return carry

    lax.fori_loop(0, blocks - ahead, block, 0)


SMEM_SPEC = pl.BlockSpec(memory_space=pltpu.SMEM)
VMEM_SPEC = pl.BlockSpec(memory_space=pltpu.VMEM)


def forward_mix(seg, taps, u, ids):
    channels = u.shape[1]
    return pl.pallas_call(
        forward_kernel,
        out_shape=jax.ShapeDtypeStruct((u.shape[0] - REACH, channels), BF16),
        in_specs=[SMEM_SPEC] + [VMEM_SPEC] * 3,
        scratch_shapes=[
            pltpu.VMEM((64 + REACH + 128, channels), F32),
            pltpu.VMEM((8, 64 + REACH, channels), F32),
            pltpu.VMEM(u.shape, F32),
        ],
        compiler_params=pltpu.CompilerParams(vmem_limit_bytes=VMEM_LIMIT),
        cost_estimate=pl.CostEstimate(flops=20_000_000, bytes_accessed=1_000_000, transcendentals=0),
        name="forward_mix",
    )(seg, taps, u, ids)


def backward_kernel(seg, rev_ref, g_ref, s_ref, slope_ref, low_ref, sum_ref, pad, copies, alive):
    channels = g_ref.shape[1]
    blocks = g_ref.shape[0] // 64
    ahead = REACH // 64
    shifted_copies(rev_ref, pad, copies, -57)
    for b in range(blocks):
        rows = slice(64 * b, 64 * b + 64)
        alive[rows, :] = jnp.where(s_ref[rows, :] == seg[64 * b], g_ref[rows, :], 0.0)

    def block(j, total):
        zero = jnp.zeros((8, channels), F32)
        reach = linked_blocks(seg, j, j + 1, 1, ahead)

        def far(d, sums):
            sums = list(sums)
            at = pl.multiple_of(64 * (j + 1 + d), 64)
            for r in range(8):
                taps = [copies[r, tile(39 - (8 * (d + 1) + m)), :] for m in range(-7, 8)]
                for q in range(8):
                    g = alive[pl.ds(at + 8 * q + r, 1), :]
                    for t in range(8):
                        sums[t] += taps[q - t + 7] * g
            return tuple(sums)

        sums = lax.fori_loop(0, reach, far, (zero,) * 8)
        base = pl.multiple_of(64 * j, 64)
        ids = [s_ref[pl.ds(base + 8 * t, 8), :] for t in range(8)]
        last = seg[64 * j + 63]
        sums = [jnp.where(ids[t] == last, sums[t], 0.0) for t in range(8)]
        for r in range(8):
            taps = [copies[r, 8 * (39 - m) : 8 * (39 - m) + 8, :] for m in range(8)]
            for q in range(8):
                g = g_ref[pl.ds(base + 8 * q + r, 1), :]
                own = s_ref[pl.ds(base + 8 * q + r, 1), :]
                for t in range(q + 1):
                    sums[t] += jnp.where(ids[t] == own, taps[q - t], 0.0) * g
        for t in range(0, 8, 2):
            rows = pl.ds(pl.multiple_of(64 * j + 8 * t, 16), 16)
            both = jnp.concatenate([sums[t], sums[t + 1]], 0) * slope_ref[rows, :]
            low_ref[rows, :] = both.astype(low_ref.dtype)
            total = total + both
        return total

    total = lax.fori_loop(0, blocks - ahead, block, jnp.zeros((16, channels), F32))
    sum_ref[...] = jnp.sum(total, axis=0, keepdims=True)


def backward_mix(seg, reversed_taps, g, ids, slope):
    channels = g.shape[1]
    return pl.pallas_call(
        backward_kernel,
        out_shape=[
            jax.ShapeDtypeStruct(slope.shape, BF16),
            jax.ShapeDtypeStruct((1, channels), F32),
        ],
        in_specs=[SMEM_SPEC] + [VMEM_SPEC] * 4,
        scratch_shapes=[
            pltpu.VMEM((64 + REACH + 128, channels), F32),
            pltpu.VMEM((8, 64 + REACH, channels), F32),
            pltpu.VMEM(g.shape, F32),
        ],
        compiler_params=pltpu.CompilerParams(vmem_limit_bytes=VMEM_LIMIT),
        cost_estimate=pl.CostEstimate(flops=20_000_000, bytes_accessed=1_000_000, transcendentals=0),
        name="backward_mix",
    )(seg, reversed_taps, g, ids, slope)


def taps_back_kernel(seg, u_ref, s_ref, g_ref, out_ref, kept, sums, pad):
    channels = u_ref.shape[1]
    blocks = u_ref.shape[0] // 64
    ahead = REACH // 64
    sums[...] = jnp.zeros_like(sums)
    for b in range(blocks):
        rows = slice(64 * b, 64 * b + 64)
        kept[rows, :] = jnp.where(s_ref[rows, :] == seg[64 * b + 63], u_ref[rows, :], 0.0)

    def block(i, carry):
        mine = i + ahead
        reach = linked_blocks(seg, mine, mine - 1, -1, ahead)
        base = pl.multiple_of(64 * mine, 64)
        back = pl.multiple_of(64 * i, 64)
        ids = [s_ref[pl.ds(base + 8 * t, 8), :] for t in range(8)]
        whole = [g_ref[pl.ds(back + 8 * t, 8), :] for t in range(8)]
        alive = [jnp.where(ids[t] == seg[64 * mine], whole[t], 0.0) for t in range(8)]

        def far(d, carried):
            at = pl.multiple_of(64 * (mine - 1 - d), 64)
            for r in range(8):
                found = [None] * 15
                for q in range(8):
                    u = kept[pl.ds(at + 8 * q + r, 1), :]
                    for t in range(8):
                        term = carried[t] * u
                        m = t - q + 7
                        found[m] = term if found[m] is None else found[m] + term
                for m in range(-7, 8):
                    sums[r, tile(8 * (d + 1) + m), :] += found[m + 7]
            return carried

        lax.fori_loop(0, reach, far, tuple(alive))
        for r in range(8):
            found = [None] * 8
            for q in range(8):
                u = u_ref[pl.ds(base + 8 * q + r, 1), :]
                own = s_ref[pl.ds(base + 8 * q + r, 1), :]
                for t in range(q, 8):
                    term = jnp.where(ids[t] == own, whole[t], 0.0) * u
                    m = t - q
                    found[m] = term if found[m] is None else found[m] + term
            for m in range(8):
                sums[r, 8 * m : 8 * m + 8, :] += found[m]
        return carry

    lax.fori_loop(0, blocks - ahead, block, 0)
    total = sums[0, 0:REACH, :]
    for r in range(1, 8):
        total = total + sums[r, r : r + REACH, :]
    out_ref[...] = total


def taps_back(seg, u, ids, g):
    channels = u.shape[1]
    return pl.pallas_call(
        taps_back_kernel,
        out_shape=jax.ShapeDtypeStruct((REACH, channels), F32),
        in_specs=[SMEM_SPEC] + [VMEM_SPEC] * 3,
        scratch_shapes=[
            pltpu.VMEM(u.shape, F32),
            pltpu.VMEM((8, 64 + REACH, channels), F32),
            pltpu.VMEM((8, channels), F32),
        ],
        compiler_params=pltpu.CompilerParams(vmem_limit_bytes=VMEM_LIMIT),
        cost_estimate=pl.CostEstimate(flops=20_000_000, bytes_accessed=1_000_000, transcendentals=0),
        name="taps_back",
    )(seg, u, ids, g)


def modes_back_kernel(
    c_ref, d_ref, f_ref, t_ref, mr_ref, mi_ref, dd_ref, df_ref, dt_ref, dmr_ref, dmi_ref,
    ar_s, ai_s, gr_s, gi_s, hr_s, hi_s, wide, wide_l,
):
    channels = c_ref.shape[1]
    damping, frequency, timestep = d_ref[...], f_ref[...], t_ref[...]
    ar, ai = modes(damping, frequency, timestep)
    ar_s[...] = ar
    ai_s[...] = ai
    for l in range(REACH):
        row = jnp.broadcast_to(c_ref[l : l + 1, :], (8, channels))
        wide[8 * l : 8 * l + 8, :] = row
        wide_l[8 * l : 8 * l + 8, :] = row * float(l)

    def one(p, carry):
        rows = pl.ds(pl.multiple_of(8 * p, 8), 8)
        a = (ar_s[rows, :], ai_s[rows, :])
        base = low_powers(*a, 16)
        jump = cmul(*base[8], *base[8])
        zero = jnp.zeros((8, channels), F32)

        def outer(o, state):
            pr, pi, gr, gi, hr, hi = state
            at = pl.multiple_of(128 * o, 128)
            sr = wide[pl.ds(at, 8), :]
            tr = wide_l[pl.ds(at, 8), :]
            si = zero
            ti = zero
            for j in range(1, 16):
                c = wide[pl.ds(at + 8 * j, 8), :]
                e = wide_l[pl.ds(at + 8 * j, 8), :]
                br, bi = base[j]
                sr += c * br
                si += c * bi
                tr += e * br
                ti += e * bi
            gr += pr * sr - pi * si
            gi += pr * si + pi * sr
            hr += pr * tr - pi * ti
            hi += pr * ti + pi * tr
            pr, pi = cmul(pr, pi, *jump)
            return pr, pi, gr, gi, hr, hi

        one_ = jnp.ones((8, channels), F32)
        _, _, gr, gi, hr, hi = lax.fori_loop(
            0, REACH // 16, outer, (one_, zero, zero, zero, zero, zero)
        )
        gr_s[rows, :] = gr
        gi_s[rows, :] = gi
        hr_s[rows, :] = hr
        hi_s[rows, :] = hi
        return carry

    lax.fori_loop(0, ar_s.shape[0] // 8, one, 0)
    gr, gi, hr, hi = gr_s[...], gi_s[...], hr_s[...], hi_s[...]
    mr, mi = mr_ref[...], mi_ref[...]
    qr, qi = ratios(damping, frequency, ar, ai)
    wr, wi = cmul(mr, mi, qr, qi)
    mixr, mixi = cmul(qr, qi, gr, gi)
    dmr_ref[...] = mixr
    dmi_ref[...] = -mixi
    inverse = 1.0 / (damping * damping + frequency * frequency)
    nr, ni = -damping * inverse, -frequency * inverse
    vr, vi = cmul(*cmul(mr, mi, gr, gi), nr, ni)
    xr, xi = cmul(vr, vi, ar, ai)
    zr, zi = cmul(wr, wi, hr, hi)
    xr, xi = xr + zr, xi + zi
    yr, yi = cmul(vr, vi, qr, qi)
    dd_ref[...] = yr - timestep * xr
    df_ref[...] = yi - timestep * xi
    dt_ref[...] = jnp.sum(-damping * xr - frequency * xi, axis=0, keepdims=True)


def modes_back(c, damping, frequency, timestep, mix_real, mix_imaginary):
    count, channels = damping.shape
    whole = jax.ShapeDtypeStruct((count, channels), F32)
    return pl.pallas_call(
        modes_back_kernel,
        out_shape=[whole, whole, jax.ShapeDtypeStruct((1, channels), F32), whole, whole],
        scratch_shapes=[pltpu.VMEM((count, channels), F32)] * 6
        + [pltpu.VMEM((REACH * 8, channels), F32)] * 2,
        compiler_params=pltpu.CompilerParams(vmem_limit_bytes=VMEM_LIMIT),
        cost_estimate=pl.CostEstimate(flops=160_000_000, bytes_accessed=2_000_000, transcendentals=200_000),
        name="modes_back",
    )(c, damping, frequency, timestep, mix_real, mix_imaginary)


GELU_SCALE = 0.7978845608028654


def gelu_pair(a):
    square = a * a
    bent = jnp.tanh(GELU_SCALE * (a + 0.044715 * (a * square)))
    half = 0.5 * (1.0 + bent)
    slope = half + 0.5 * a * (1.0 - bent * bent) * (GELU_SCALE + 3 * 0.044715 * GELU_SCALE * square)
    return a * half, slope


def dot(a, b):
    return jnp.dot(a, b, preferred_element_type=F32)


def dot_t(a, b):
    return lax.dot_general(a, b, (((1,), (1,)), ((), ())), preferred_element_type=F32)


def t_dot(a, b):
    return lax.dot_general(a, b, (((0,), (0,)), ((), ())), preferred_element_type=F32)


def per_device(
    inputs,
    teacher,
    segment_ids,
    valid_mask,
    norm_gain,
    norm_bias,
    gate_weight,
    gate_bias,
    reduce_weight,
    reduce_bias,
    damping,
    frequency,
    timestep,
    mix_real,
    mix_imaginary,
    expand_weight,
    expand_bias,
    output_weight,
    output_bias,
):
    tokens, width = inputs.shape
    channels = reduce_bias.shape[0]
    tensor_size = lax.axis_size("tensor")
    tensor_at = lax.axis_index("tensor")
    contexts = lax.axis_size("context")
    context_at = lax.axis_index("context")

    mask_row = valid_mask[0].astype(F32)
    counted = jnp.sum(mask_row)
    counted = jnp.broadcast_to(counted, (1, 128))
    counted = sum_over(sum_over(counted, "context"), "shard")[0, 0]

    reduce_full = gather_weight(reduce_weight, 0)
    gate_full = gather_weight(gate_weight, 0)
    expand_full = gather_weight(expand_weight, 0)
    output_full = gather_weight(output_weight, 1)

    rows_in = inputs.astype(F32)
    center = jnp.mean(rows_in, axis=-1, keepdims=True)
    shifted = rows_in - center
    spread = jnp.mean(shifted * shifted, axis=-1, keepdims=True)
    inverse = lax.rsqrt(spread + EPSILON)
    unit = shifted * inverse
    normed = (unit * norm_gain + norm_bias).astype(BF16)

    mode_args = (damping.T, frequency.T, timestep[None, :], mix_real.T, mix_imaginary.T)
    taps, reversed_taps = make_taps(*mode_args)

    segments = segment_ids[0]
    before = [(i, i + 1) for i in range(contexts - 1)]
    after = [(i + 1, i) for i in range(contexts - 1)]
    seg_before = jnp.where(
        context_at > 0, lax.ppermute(segments[tokens - REACH :], "context", before), -1
    )
    seg_after = jnp.where(
        context_at < contexts - 1, lax.ppermute(segments[:REACH], "context", after), -1
    )
    seg_early = jnp.concatenate([seg_before, segments])
    seg_late = jnp.concatenate([segments, seg_after])
    ids_early = jnp.broadcast_to(seg_early[:, None], (tokens + REACH, channels))
    ids_late = jnp.broadcast_to(seg_late[:, None], (tokens + REACH, channels))

    reduced, reduce_slope = gelu_pair(dot(normed, reduce_full) + reduce_bias)
    halo = lax.ppermute(reduced[tokens - REACH :], "context", before)
    u = jnp.concatenate([halo, reduced], 0)
    mixed_rows = forward_mix(seg_early, taps, u, ids_early)

    gate_act, gate_slope = gelu_pair(dot(normed, gate_full) + gate_bias)
    mixed_parts = gather_rows(mixed_rows)
    mixed_full = mixed_parts.transpose(1, 0, 2).reshape(tokens, tensor_size * channels)
    expanded = dot(mixed_full, expand_full) + expand_bias
    gated_rows = (expanded * gate_act).astype(BF16)
    branch_own = scatter_rows(dot(gated_rows, output_full).astype(BF16)).astype(BF16)
    branch = gather_rows(branch_own).reshape(tokens, width).astype(F32)

    result = rows_in + branch + output_bias
    difference = result - teacher.astype(F32)
    errors = jnp.sum(mask_row * jnp.sum(difference * difference, axis=-1))
    tokens_all = tokens * lax.axis_size("shard") * contexts
    result_back = (tokens_all / counted) * mask_row[:, None] * difference
    branch_back = result_back.astype(BF16)
    gated_back = dot_t(branch_back, output_full)
    expanded_back = gated_back * gate_act
    activation_back = gated_back * expanded
    expand_low = expanded_back.astype(BF16)
    mixed_back_part = dot_t(expand_low, expand_full).astype(BF16)
    mixed_back = scatter_rows(
        mixed_back_part.reshape(tokens, tensor_size, channels)
        .transpose(1, 0, 2)
        .reshape(tensor_size * tokens, channels)
    )
    gate_pre_back = gate_slope * activation_back
    gate_low = gate_pre_back.astype(BF16)

    halo_back = lax.ppermute(mixed_back[:REACH], "context", after)
    g_late = jnp.concatenate([mixed_back, halo_back], 0)
    reduce_low, reduce_bias_part = backward_mix(
        seg_late, reversed_taps, g_late, ids_late, reduce_slope
    )
    normed_part = dot_t(gate_low, gate_full) + dot_t(reduce_low, reduce_full)
    normed_own = scatter_rows(normed_part.astype(BF16))

    taps_grad = taps_back(seg_early, u, ids_early, mixed_back)
    taps_grad = sum_over(sum_over(taps_grad, "context"), "shard")
    mode_grads = modes_back(taps_grad, *mode_args)

    own_rows = tokens // tensor_size

    def mine(x):
        return lax.dynamic_slice_in_dim(x, tensor_at * own_rows, own_rows, 0)

    scaled = normed_own * norm_gain
    unit_own = mine(unit)
    rows_back = mine(inverse) * (
        scaled
        - jnp.mean(scaled, axis=-1, keepdims=True)
        - unit_own * jnp.mean(scaled * unit_own, axis=-1, keepdims=True)
    )
    inputs_grad_own = (mine(result_back) + rows_back).astype(BF16)
    inputs_grad = gather_rows(inputs_grad_own).reshape(tokens, width)

    gain_grad = jnp.sum(normed_own * unit_own, axis=0)
    bias_grad = jnp.sum(normed_own, axis=0)
    norm_pack = jnp.concatenate([gain_grad, bias_grad]).reshape(-1, 128)
    norm_pack = sum_over(sum_over(sum_over(norm_pack, "context"), "shard"), "tensor").reshape(-1)

    sizes = (gate_bias.shape[0], expand_bias.shape[0], width, channels, 128)
    pack = jnp.concatenate(
        [
            jnp.sum(gate_pre_back, axis=0),
            jnp.sum(expanded_back, axis=0),
            jnp.sum(result_back, axis=0),
            reduce_bias_part[0],
            jnp.broadcast_to(errors, (128,)),
        ]
    )
    pack = sum_over(sum_over(pack[None, :], "context"), "shard")[0]
    offsets = [sum(sizes[:k]) for k in range(6)]
    gate_bias_grad, expand_bias_grad, output_bias_grad, reduce_bias_grad, error_total = (
        pack[offsets[k] : offsets[k + 1]] for k in range(5)
    )
    loss_value = error_total[0] / (counted * width)

    output_grad = scatter_grad(t_dot(gated_rows, branch_back), 1)
    expand_grad = scatter_grad(t_dot(mixed_full, expand_low), 0)
    gate_grad = scatter_grad(t_dot(normed, gate_low), 0)
    reduce_grad = scatter_grad(t_dot(normed, reduce_low), 0)

    return (
        result.astype(BF16),
        loss_value,
        inputs_grad,
        norm_pack[:width],
        norm_pack[width:],
        gate_grad,
        gate_bias_grad,
        reduce_grad,
        reduce_bias_grad,
        mode_grads[0].T,
        mode_grads[1].T,
        mode_grads[2][0],
        mode_grads[3].T,
        mode_grads[4].T,
        expand_grad,
        expand_bias_grad,
        output_grad,
        output_bias_grad,
    )


def solution(mesh):
    tokens = P(("shard", "context"), None)
    ids = P("shard", "context")
    split = P("shard", "tensor")
    rows = P("tensor", None)
    units = P("tensor")
    return jax.shard_map(
        per_device,
        mesh=mesh,
        in_specs=(
            tokens, tokens, ids, ids, P(), P(), split, units, split, units,
            rows, rows, units, rows, rows, split, units, P("tensor", "shard"), P(),
        ),
        out_specs=(
            tokens, P(), tokens, P(), P(), split, units, split, units,
            rows, rows, units, rows, rows, split, units, P("tensor", "shard"), P(),
        ),
        check_vma=False,
    )
```

time: 1590 us -> 353 us (0.22)
  matrix products: 595 us -> 23.9 us
  other arithmetic: 304 us -> 23.9 us
  waiting for transfers between devices: 314 us -> 69.5 us
  local copies, waits for them, and re-layouts: 221 us -> 72 us
  blocking collectives: 111 us -> 0 us
  starting transfers between devices: 0.45 us -> 98.5 us
  Pallas kernels: 0 us -> 56.7 us
  between operations: 22.1 us -> 3.83 us
    dot_general x30 -> x12, matrix products: 595 us -> 23.9 us  [the longest x4 8.73 us: dot(): return jnp.dot(a, b, preferred_element_type=F32)]
    psum x4 -> x0, waiting for transfers between devices: 174 us -> none  [the longest x1 81.7 us: per_device(): normed_back = lax.psum(normed_part, 'tensor')]
    reduce_scatter x5 -> x0, waiting for transfers between devices: 138 us -> none  [the longest x1 47.5 us: per_device(): lax.psum_scatter(paired[3], 'shard', scatter_dimension=1, tiled=True)]
    reduce_sum x12 -> x6, other arithmetic: 117 us -> 7.47 us  [the longest x1 2.43 us: per_device(): jnp.sum(result_back, axis=0)]
    ppermute x0 -> x85, starting transfers between devices: none -> 98.5 us  [the longest x9 20.2 us: scatter_rows(): lax.ppermute(piece, 'tensor', shift_pairs(size, k)).astype(F32)]
    rev x4 -> x0, local copies, waits for them, and re-layouts: 89.5 us -> none  [the longest x2 44.8 us: intra_part(): reverse_imaginary = power_imaginary[..., :BLOCK][..., ::-1]]
    mul x3 -> x1, other arithmetic: 79.1 us -> 2.13 us  [per_device(): unit = shifted * inverse]
    ppermute x0 -> x85, waiting for transfers between devices: none -> 69.5 us  [the longest x9 25.4 us: scatter_rows(): lax.ppermute(piece, 'tensor', shift_pairs(size, k)).astype(F32)]
  transfers between devices with their start and end apart: 11 -> 85, of which waited for: 7 -> 27; matrix products, arithmetic and copies ran while one was open for 37% -> 27% of each run, Pallas kernels for 0% -> 16%
where the time goes in v1:
time: 353 us; the launch traced here: 348 us
  starting transfers between devices  98.5 us (28%)
  local copies, waits for them, and re-layouts  72 us (20%)
  waiting for transfers between devices  69.5 us (20%)
  Pallas kernels  56.7 us (16%)
  other arithmetic  23.9 us (7%)
  matrix products  23.9 us (7%)
  between operations  3.83 us (1%)
    pallas_call x1, Pallas kernels, modes_back(): pl.pallas_call(modes_back_kernel, out_shape=[whole, whole, jax.ShapeDtype...  28.8 us
    ppermute x9, waiting for transfers between devices, scatter_rows(): lax.ppermute(piece, 'tensor', shift_pairs(size, k)).astype(F32)  25.4 us
    ppermute x9, starting transfers between devices, scatter_rows(): lax.ppermute(piece, 'tensor', shift_pairs(size, k)).astype(F32)  20.2 us
    ppermute x12, starting transfers between devices, gather_weight(): near = [lax.ppermute(mine, 'shard', xor_pairs(4, k)) for k in (1, 2, 3)]  17.6 us
    pallas_call x1, Pallas kernels, make_taps(): pl.pallas_call(taps_kernel, out_shape=[jax.ShapeDtypeStruct((REACH, chann...  16.1 us
    ppermute x9, starting transfers between devices, gather_rows(): part = lax.ppermute(x, 'tensor', shift_pairs(size, k))  16 us
    ppermute x12, waiting for transfers between devices, scatter_grad(): total = total + lax.ppermute(piece, 'shard', xor_pairs(4, k)).astype(F32)  14.1 us
    ppermute x12, starting transfers between devices, scatter_grad(): total = total + lax.ppermute(piece, 'shard', xor_pairs(4, k)).astype(F32)  14.1 us
  transfers between devices with their start and end apart: 85, of which 27 were waited for; matrix products, arithmetic and copies ran while one was open for 27% of the time, Pallas kernels for 16%

profile of v1, /device:TPU:0, one launch (start us, length us, event | category | flops | bytes accessed | tf_op | source)
XLA Modules:
  0.0 348.4 jit_solution(9430056282274755213)
XLA Ops:
  2.4 2.9 collective-permute-start.17
  8.8 3.6 %collective-permute-start = (s32[256]{0:T(256)S(1)}, s32[256]{0:T(256)}, u32[]{:S(2)}, u32[]{:S(2)}) collective-permute-start(s32[256]{0:T(256)S(1)} %bitcast.327), channel_id=1, source_target_pairs={{0,4},{1,5},{2,6},{3,7},{8,12},{9,13},{10,14},{11,15},{16,20},{17,... | collective-permute-start | bytes 3080 | tf_op jit(solution)/shard_map/ppermute | solution.py:569
  24.8 16.1 %taps.1 = (f32[256,128]{1,0:T(8,128)S(1)}, f32[256,128]{1,0:T(8,128)S(1)}) custom-call(f32[512,128]{1,0:T(8,128)S(1)} %bitcast.273, f32[512,128]{1,0:T(8,128)S(1)} %bitcast.275, f32[1,128]{1,0:T(1,128)S(1)} %bitcast.286, f32[512,128]{1,0:T(8,128)S(1)} %bitcast.277, f32[512,128]{1,0:T(8,128)S(1)} %bitcast.279), custom_call_target="tpu_custom_call" | custom-call | flops 80000000 | bytes 2000000 | tf_op jit(solution)/shard_map/taps/pallas_call | solution.py:170
  48.4 3.3 collective-permute-done.5
  61.3 3.8 %forward_mix.1 = bf16[512,128]{1,0:T(8,128)(2,1)S(1)} custom-call(s32[768]{0:T(1024)S(1)} %get-tuple-element.130.seg, f32[256,128]{1,0:T(8,128)S(1)} %get-tuple-element.27.k_ref, f32[768,128]{1,0:T(8,128)S(1)} %pad_maximum_fusion.u_ref, s32[768,128]{1,0:T(8,128)S(1)} %broadcast_in_dim.187.s_ref), custom_call_target="tpu_custom_call" | custom-call | flops 20000000 | bytes 1000000 | tf_op jit(solution)/shard_map/forward_mix/pallas_call | solution.py:254
  114.2 4.8 %collective-permute-start.31 = (bf16[128,1024]{1,0:T(8,128)(2,1)}, bf16[128,1024]{1,0:T(8,128)(2,1)}, u32[]{:S(2)}, u32[]{:S(2)}) collective-permute-start(bf16[128,1024]{1,0:T(8,128)(2,1)} %get-tuple-element.107), channel_id=1, source_target_pairs={{0,3},{1,0},{2,1},{3,2},{4,7},{5,4},{6,5},{7,6},{8,11},{9,8},{10,9... | collective-permute-start | bytes 786440 | tf_op jit(solution)/shard_map/ppermute | solution.py:94
  128.0 13.0 %collective-permute-done.30 = bf16[128,1024]{1,0:T(8,128)(2,1)} collective-permute-done((bf16[128,1024]{1,0:T(8,128)(2,1)}, bf16[128,1024]{1,0:T(8,128)(2,1)}, u32[]{:S(2)}, u32[]{:S(2)}) %collective-permute-start.30) | collective-permute-done | bytes 262176 | tf_op jit(solution)/shard_map/ppermute | solution.py:94
  147.7 2.9 collective-permute-start.34
  150.6 3.2 collective-permute-done.32
  153.8 9.4 %collective-permute-done.33 = bf16[128,1024]{1,0:T(8,128)(2,1)S(1)} collective-permute-done((bf16[128,1024]{1,0:T(8,128)(2,1)S(1)}, bf16[128,1024]{1,0:T(8,128)(2,1)S(1)}, u32[]{:S(2)}, u32[]{:S(2)}) %collective-permute-start.33) | collective-permute-done | bytes 262176 | tf_op jit(solution)/shard_map/ppermute | solution.py:104
  165.7 2.7 fusion.27
  169.5 4.8 %fusion.65 = (f32[768]{0:T(1024)}, bf16[512,768]{1,0:T(8,128)(2,1)S(1)}, f32[768]{0:T(1024)}, bf16[512,768]{1,0:T(8,128)(2,1)}) fusion(f32[512,768]{1,0:T(8,128)S(1)} %copy-done.53, f32[512,768]{1,0:T(8,128)S(1)} %copy-done.54, bf16[768,1024]{0,1:T(8,128)(2,1)} %bitcast.44, f32[512,1024]{1,0:T(8,128)S(1)} %get-tuple-element.90), kind=kOutput, calls=%fused_computation.202 | convolution fusion | flops 814873088 | bytes 8394752 | tf_op jit(solution)/shard_map/dot_general | solution.py:509
  177.3 8.2 %collective-permute-start.42 = (bf16[512,128]{1,0:T(8,128)(2,1)}, bf16[512,128]{1,0:T(8,128)(2,1)}, u32[]{:S(2)}, u32[]{:S(2)}) collective-permute-start(bf16[512,128]{1,0:T(8,128)(2,1)} %bitcast.314), channel_id=1, source_target_pairs={{0,3},{1,0},{2,1},{3,2},{4,7},{5,4},{6,5},{7,6},{8,11},{9,8},{10,9... | collective-permute-start | bytes 393224 | tf_op jit(solution)/shard_map/ppermute | solution.py:94
  196.4 5.2 %reshape.197 = f32[2,384,4,256]{3,2,1,0:T(4,128)} reshape(f32[768,1024]{1,0:T(8,128)} %fusion.27) | data formatting | bytes 6291456 | tf_op jit(solution)/shard_map/reshape | solution.py:73
  201.6 2.9 constant_dynamic-slice_fusion.1
  211.8 3.8 %taps_back.1 = f32[256,128]{1,0:T(8,128)S(1)} custom-call(s32[768]{0:T(1024)S(1)} %get-tuple-element.130.seg, f32[768,128]{1,0:T(8,128)S(1)} %pad_maximum_fusion.u_ref, s32[768,128]{1,0:T(8,128)S(1)} %broadcast_in_dim.187.s_ref, f32[512,128]{1,0:T(8,128)S(1)} %fusion.49.g_ref), custom_call_target="tpu_custom_call" | custom-call | flops 20000000 | bytes 1000000 | tf_op jit(solution)/shard_map/taps_back/pallas_call | solution.py:391
  217.5 4.2 %backward_mix.1 = (bf16[512,128]{1,0:T(8,128)(2,1)S(1)}, f32[1,128]{1,0:T(1,128)S(1)}) custom-call(s32[768]{0:T(1024)S(1)} %get-tuple-element.129.seg, f32[256,128]{1,0:T(8,128)S(1)} %get-tuple-element.28.rev_ref, f32[768,128]{1,0:T(8,128)S(1)} %pad_maximum_fusion.1.g_ref, s32[768,128]{1,0:T(8,128)S(1)} %broadcast_in_dim.221.s_ref, ...), custom_call_target="tpu_custom_call" | custom-call | flops 20000000 | bytes 1000000 | tf_op jit(solution)/shard_map/backward_mix/pallas_call | solution.py:318
  239.2 3.3 collective-permute-start.50
  245.3 28.8 %modes_back.1 = (f32[512,128]{1,0:T(8,128)S(1)}, f32[512,128]{1,0:T(8,128)S(1)}, f32[1,128]{1,0:T(1,128)}, f32[512,128]{1,0:T(8,128)S(1)}, f32[512,128]{1,0:T(8,128)S(1)}) custom-call(f32[256,128]{1,0:T(8,128)S(1)} %add_add_fusion.c_ref, f32[512,128]{1,0:T(8,128)S(1)} %bitcast.274, f32[512,128]{1,0:T(8,128)S(1)} %bitcast.276, f32[1,128]{1,0:T(1,128)S(1)} %bitcast.287, ...), custom_call_target="tpu_custom_call" | custom-call | flops 160000000 | bytes 2000000 | tf_op jit(solution)/shard_map/modes_back/pallas_call | solution.py:482
  286.5 12.4 %collective-permute-done.49 = bf16[128,1024]{1,0:T(8,128)(2,1)S(1)} collective-permute-done((bf16[128,1024]{1,0:T(8,128)(2,1)}, bf16[128,1024]{1,0:T(8,128)(2,1)S(1)}, u32[]{:S(2)}, u32[]{:S(2)}) %collective-permute-start.49) | collective-permute-done | bytes 262176 | tf_op jit(solution)/shard_map/ppermute | solution.py:94
  319.0 2.7 collective-permute-start.53
  329.5 3.5 collective-permute-done.64
  334.1 2.9 collective-permute-done.63
  339.6 4.2 %collective-permute-done.82 = bf16[384,256]{1,0:T(8,128)(2,1)S(1)} collective-permute-done((bf16[384,256]{1,0:T(8,128)(2,1)S(1)}, bf16[384,256]{1,0:T(8,128)(2,1)S(1)}, u32[]{:S(2)}, u32[]{:S(2)}) %collective-permute-start.82) | collective-permute-done | bytes 196640 | tf_op jit(solution)/shard_map/ppermute | solution.py:81
  (414 shorter events, 192.3 us)
Async XLA Ops:
  2.4 62.9 %collective-permute-start.17 = (bf16[128,768]{1,0:T(8,128)(2,1)}, bf16[128,768]{1,0:T(8,128)(2,1)}, u32[]{:S(2)}, u32[]{:S(2)}) collective-permute-start(bf16[128,768]{1,0:T(8,128)(2,1)} %constant_dynamic-slice_fusion.7), channel_id=1, source_target_pairs={{0,8},{8,0},{16,24},{24,16},{1,9},{9,1},{17,25},{25,17},{2,10},{10... | collective-permute-start | bytes 589832 | tf_op jit(solution)/shard_map/ppermute | solution.py:52
  5.3 86.8 %collective-permute-start.19 = (bf16[128,768]{1,0:T(8,128)(2,1)}, bf16[128,768]{1,0:T(8,128)(2,1)}, u32[]{:S(2)}, u32[]{:S(2)}) collective-permute-start(bf16[128,768]{1,0:T(8,128)(2,1)} %constant_dynamic-slice_fusion.7), channel_id=1, source_target_pairs={{0,16},{8,24},{16,0},{24,8},{1,17},{9,25},{17,1},{25,9},{2,18},{10... | collective-permute-start | bytes 589832 | tf_op jit(solution)/shard_map/ppermute | solution.py:52
  6.8 85.8 %collective-permute-start.21 = (bf16[128,768]{1,0:T(8,128)(2,1)}, bf16[128,768]{1,0:T(8,128)(2,1)}, u32[]{:S(2)}, u32[]{:S(2)}) collective-permute-start(bf16[128,768]{1,0:T(8,128)(2,1)} %constant_dynamic-slice_fusion.7), channel_id=1, source_target_pairs={{0,24},{8,16},{16,8},{24,0},{1,25},{9,17},{17,9},{25,1},{2,26},{10... | collective-permute-start | bytes 589832 | tf_op jit(solution)/shard_map/ppermute | solution.py:52
  7.5 33.4 %collective-permute-start.39 = (s32[256]{0:T(256)S(1)}, s32[256]{0:T(256)S(1)}, u32[]{:S(2)}, u32[]{:S(2)}) collective-permute-start(s32[256]{0:T(256)S(1)} %bitcast.328), channel_id=1, source_target_pairs={{4,0},{5,1},{6,2},{7,3},{12,8},{13,9},{14,10},{15,11},{20,16},{21,... | collective-permute-start | bytes 3080 | tf_op jit(solution)/shard_map/ppermute | solution.py:572
  8.8 34.1 %collective-permute-start = (s32[256]{0:T(256)S(1)}, s32[256]{0:T(256)}, u32[]{:S(2)}, u32[]{:S(2)}) collective-permute-start(s32[256]{0:T(256)S(1)} %bitcast.327), channel_id=1, source_target_pairs={{0,4},{1,5},{2,6},{3,7},{8,12},{9,13},{10,14},{11,15},{16,20},{17,... | collective-permute-start | bytes 3080 | tf_op jit(solution)/shard_map/ppermute | solution.py:569
  119.0 22.0 %collective-permute-start.30 = (bf16[128,1024]{1,0:T(8,128)(2,1)}, bf16[128,1024]{1,0:T(8,128)(2,1)}, u32[]{:S(2)}, u32[]{:S(2)}) collective-permute-start(bf16[128,1024]{1,0:T(8,128)(2,1)} %get-tuple-element.108), channel_id=1, source_target_pairs={{0,2},{1,3},{2,0},{3,1},{4,6},{5,7},{6,4},{7,5},{8,10},{9,11},{10,... | collective-permute-start | bytes 786440 | tf_op jit(solution)/shard_map/ppermute | solution.py:94
  119.0 22.0 %collective-permute-start.29 = (bf16[128,1024]{1,0:T(8,128)(2,1)S(1)}, bf16[128,1024]{1,0:T(8,128)(2,1)}, u32[]{:S(2)}, u32[]{:S(2)}) collective-permute-start(bf16[128,1024]{1,0:T(8,128)(2,1)S(1)} %get-tuple-element.106), channel_id=1, source_target_pairs={{0,1},{1,2},{2,3},{3,0},{4,5},{5,6},{6,7},{7,4},{8,9},{9,10},{10,1... | collective-permute-start | bytes 786440 | tf_op jit(solution)/shard_map/ppermute | solution.py:94
  124.5 19.7 %collective-permute-start.37 = (f32[1,128]{1,0:T(1,128)S(1)}, f32[1,128]{1,0:T(1,128)S(1)}, u32[]{:S(2)}, u32[]{:S(2)}) collective-permute-start(f32[1,128]{1,0:T(1,128)S(1)} %broadcast_add_fusion), channel_id=1, source_target_pairs={{0,16},{8,24},{16,0},{24,8},{1,17},{9,25},{17,1},{25,9},{2,18},{10... | collective-permute-start | bytes 1544 | tf_op jit(solution)/shard_map/ppermute | solution.py:34
  125.5 18.7 %collective-permute-start.38 = (f32[1,128]{1,0:T(1,128)S(1)}, f32[1,128]{1,0:T(1,128)S(1)}, u32[]{:S(2)}, u32[]{:S(2)}) collective-permute-start(f32[1,128]{1,0:T(1,128)S(1)} %broadcast_add_fusion), channel_id=1, source_target_pairs={{0,24},{8,16},{16,8},{24,0},{1,25},{9,17},{17,9},{25,1},{2,26},{10... | collective-permute-start | bytes 1544 | tf_op jit(solution)/shard_map/ppermute | solution.py:35
  145.5 17.7 %collective-permute-start.33 = (bf16[128,1024]{1,0:T(8,128)(2,1)S(1)}, bf16[128,1024]{1,0:T(8,128)(2,1)S(1)}, u32[]{:S(2)}, u32[]{:S(2)}) collective-permute-start(bf16[128,1024]{1,0:T(8,128)(2,1)S(1)} %get-tuple-element.96), channel_id=1, source_target_pairs={{0,2},{1,3},{2,0},{3,1},{4,6},{5,7},{6,4},{7,5},{8,10},{9,11},{10,... | collective-permute-start | bytes 786440 | tf_op jit(solution)/shard_map/ppermute | solution.py:104
  177.3 28.9 %collective-permute-start.42 = (bf16[512,128]{1,0:T(8,128)(2,1)}, bf16[512,128]{1,0:T(8,128)(2,1)}, u32[]{:S(2)}, u32[]{:S(2)}) collective-permute-start(bf16[512,128]{1,0:T(8,128)(2,1)} %bitcast.314), channel_id=1, source_target_pairs={{0,3},{1,0},{2,1},{3,2},{4,7},{5,4},{6,5},{7,6},{8,11},{9,8},{10,9... | collective-permute-start | bytes 393224 | tf_op jit(solution)/shard_map/ppermute | solution.py:94
  187.1 19.1 %collective-permute-start.41 = (bf16[512,128]{1,0:T(8,128)(2,1)}, bf16[512,128]{1,0:T(8,128)(2,1)}, u32[]{:S(2)}, u32[]{:S(2)}) collective-permute-start(bf16[512,128]{1,0:T(8,128)(2,1)} %bitcast.315), channel_id=1, source_target_pairs={{0,2},{1,3},{2,0},{3,1},{4,6},{5,7},{6,4},{7,5},{8,10},{9,11},{10,... | collective-permute-start | bytes 393224 | tf_op jit(solution)/shard_map/ppermute | solution.py:94
  187.9 18.3 %collective-permute-start.40 = (bf16[512,128]{1,0:T(8,128)(2,1)}, bf16[512,128]{1,0:T(8,128)(2,1)}, u32[]{:S(2)}, u32[]{:S(2)}) collective-permute-start(bf16[512,128]{1,0:T(8,128)(2,1)} %bitcast.316), channel_id=1, source_target_pairs={{0,1},{1,2},{2,3},{3,0},{4,5},{5,6},{6,7},{7,4},{8,9},{9,10},{10,1... | collective-permute-start | bytes 393224 | tf_op jit(solution)/shard_map/ppermute | solution.py:94
  194.7 127.9 %collective-permute-start.61 = (bf16[4,128,768]{2,1,0:T(8,128)(2,1)}, bf16[4,128,768]{2,1,0:T(8,128)(2,1)}, u32[]{:S(2)}, u32[]{:S(2)}) collective-permute-start(bf16[4,128,768]{2,1,0:T(8,128)(2,1)} %fusion.16), channel_id=1, source_target_pairs={{0,4},{4,0},{1,5},{5,1},{2,6},{6,2},{3,7},{7,3},{8,12},{12,8},{9,1... | collective-permute-start | bytes 2359304 | tf_op jit(solution)/shard_map/ppermute | solution.py:27
  230.3 47.2 %collective-permute-start.75 = (bf16[4,64,768]{2,1,0:T(8,128)(2,1)}, bf16[4,64,768]{2,1,0:T(8,128)(2,1)}, u32[]{:S(2)}, u32[]{:S(2)}) collective-permute-start(bf16[4,64,768]{2,1,0:T(8,128)(2,1)} %fusion.31), channel_id=1, source_target_pairs={{0,4},{4,0},{1,5},{5,1},{2,6},{6,2},{3,7},{7,3},{8,12},{12,8},{9,1... | collective-permute-start | bytes 1179656 | tf_op jit(solution)/shard_map/ppermute | solution.py:27
  239.2 45.5 %collective-permute-start.50 = (bf16[128,1024]{1,0:T(8,128)(2,1)}, bf16[128,1024]{1,0:T(8,128)(2,1)}, u32[]{:S(2)}, u32[]{:S(2)}) collective-permute-start(bf16[128,1024]{1,0:T(8,128)(2,1)} %get-tuple-element.104), channel_id=1, source_target_pairs={{0,3},{1,0},{2,1},{3,2},{4,7},{5,4},{6,5},{7,6},{8,11},{9,8},{10,9... | collective-permute-start | bytes 786440 | tf_op jit(solution)/shard_map/ppermute | solution.py:94
  242.5 37.3 %collective-permute-start.69 = (bf16[128,128]{1,0:T(8,128)(2,1)}, bf16[128,128]{1,0:T(8,128)(2,1)S(1)}, u32[]{:S(2)}, u32[]{:S(2)}) collective-permute-start(bf16[128,128]{1,0:T(8,128)(2,1)} %get-tuple-element.125), channel_id=1, source_target_pairs={{0,24},{8,16},{16,8},{24,0},{1,25},{9,17},{17,9},{25,1},{2,26},{10... | collective-permute-start | bytes 98312 | tf_op jit(solution)/shard_map/ppermute | solution.py:81
  244.3 36.6 %collective-permute-start.68 = (bf16[128,128]{1,0:T(8,128)(2,1)}, bf16[128,128]{1,0:T(8,128)(2,1)S(1)}, u32[]{:S(2)}, u32[]{:S(2)}) collective-permute-start(bf16[128,128]{1,0:T(8,128)(2,1)} %get-tuple-element.126), channel_id=1, source_target_pairs={{0,16},{8,24},{16,0},{24,8},{1,17},{9,25},{17,1},{25,9},{2,18},{10... | collective-permute-start | bytes 98312 | tf_op jit(solution)/shard_map/ppermute | solution.py:81
  279.7 19.2 %collective-permute-start.49 = (bf16[128,1024]{1,0:T(8,128)(2,1)}, bf16[128,1024]{1,0:T(8,128)(2,1)S(1)}, u32[]{:S(2)}, u32[]{:S(2)}) collective-permute-start(bf16[128,1024]{1,0:T(8,128)(2,1)} %get-tuple-element.105), channel_id=1, source_target_pairs={{0,2},{1,3},{2,0},{3,1},{4,6},{5,7},{6,4},{7,5},{8,10},{9,11},{10,... | collective-permute-start | bytes 786440 | tf_op jit(solution)/shard_map/ppermute | solution.py:94
  281.0 19.2 %collective-permute-start.48 = (bf16[128,1024]{1,0:T(8,128)(2,1)}, bf16[128,1024]{1,0:T(8,128)(2,1)S(1)}, u32[]{:S(2)}, u32[]{:S(2)}) collective-permute-start(bf16[128,1024]{1,0:T(8,128)(2,1)} %get-tuple-element.103), channel_id=1, source_target_pairs={{0,1},{1,2},{2,3},{3,0},{4,5},{5,6},{6,7},{7,4},{8,9},{9,10},{10,1... | collective-permute-start | bytes 786440 | tf_op jit(solution)/shard_map/ppermute | solution.py:94
  283.9 41.5 %collective-permute-start.80 = (bf16[4,384,256]{2,1,0:T(8,128)(2,1)S(1)}, bf16[4,384,256]{2,1,0:T(8,128)(2,1)S(1)}, u32[]{:S(2)}, u32[]{:S(2)}) collective-permute-start(bf16[4,384,256]{2,1,0:T(8,128)(2,1)S(1)} %bitcast.302), channel_id=1, source_target_pairs={{0,4},{4,0},{1,5},{5,1},{2,6},{6,2},{3,7},{7,3},{8,12},{12,8},{9,1... | collective-permute-start | bytes 2359304 | tf_op jit(solution)/shard_map/ppermute | solution.py:27
  284.7 17.8 %collective-permute-start.78 = (bf16[64,768]{1,0:T(8,128)(2,1)S(1)}, bf16[64,768]{1,0:T(8,128)(2,1)S(1)}, u32[]{:S(2)}, u32[]{:S(2)}) collective-permute-start(bf16[64,768]{1,0:T(8,128)(2,1)S(1)} %get-tuple-element.120), channel_id=1, source_target_pairs={{0,24},{8,16},{16,8},{24,0},{1,25},{9,17},{17,9},{25,1},{2,26},{10... | collective-permute-start | bytes 294920 | tf_op jit(solution)/shard_map/ppermute | solution.py:81
  317.3 27.3 %collective-permute-start.52 = (bf16[128,1024]{1,0:T(8,128)(2,1)S(1)}, bf16[128,1024]{1,0:T(8,128)(2,1)S(1)}, u32[]{:S(2)}, u32[]{:S(2)}) collective-permute-start(bf16[128,1024]{1,0:T(8,128)(2,1)S(1)} %get-tuple-element.87), channel_id=1, source_target_pairs={{0,2},{1,3},{2,0},{3,1},{4,6},{5,7},{6,4},{7,5},{8,10},{9,11},{10,... | collective-permute-start | bytes 786440 | tf_op jit(solution)/shard_map/ppermute | solution.py:104
  319.0 25.7 %collective-permute-start.53 = (bf16[128,1024]{1,0:T(8,128)(2,1)S(1)}, bf16[128,1024]{1,0:T(8,128)(2,1)S(1)}, u32[]{:S(2)}, u32[]{:S(2)}) collective-permute-start(bf16[128,1024]{1,0:T(8,128)(2,1)S(1)} %get-tuple-element.87), channel_id=1, source_target_pairs={{0,3},{1,0},{2,1},{3,2},{4,7},{5,4},{6,5},{7,6},{8,11},{9,8},{10,9... | collective-permute-start | bytes 786440 | tf_op jit(solution)/shard_map/ppermute | solution.py:104
  (116 other events, 815.8 us)

commit v2 on v1

v2 whole, which is shorter than its diff:
```python
import math
from functools import partial

import jax
import jax.numpy as jnp
from jax import lax
from jax.experimental import pallas as pl
from jax.experimental.pallas import tpu as pltpu
from jax.sharding import PartitionSpec as P

REACH = 256
EPSILON = 1e-05
EARLY, PAIR, LATE, TAPS_BACK, MODES_BACK, TAPS = 0.2,0.2,1,6,13,9
GELU_SCALE = 0.7978845608028654
F32 = jnp.float32
BF16 = jnp.bfloat16
SMEM_SPEC = pl.BlockSpec(memory_space=pltpu.SMEM)
VMEM_SPEC = pl.BlockSpec(memory_space=pltpu.VMEM)


def call(body, name, outs, args, scalars=1, scratch=(), micros=2, ties=()):
    held = [(a.shape, a.dtype) for a in args[scalars:]] + list(outs)
    held += [entry for entry in scratch if isinstance(entry, tuple)]
    room = 0
    for shape, kind in held:
        shape = (8,) * (2 - len(shape)) + tuple(shape)
        room += math.prod(shape[:-2] + (max(shape[-2], 8), max(shape[-1], 128))) * jnp.dtype(kind).itemsize
    count = len(args)

    def kernel(*refs):
        body(*refs[:count], *refs[count + len(ties) :])

    return pl.pallas_call(
        kernel,
        out_shape=[jax.ShapeDtypeStruct(shape, kind) for shape, kind in outs],
        in_specs=[SMEM_SPEC] * scalars
        + [VMEM_SPEC] * (len(args) - scalars)
        + [pl.BlockSpec(memory_space=pl.ANY)] * len(ties),
        out_specs=[VMEM_SPEC] * len(outs),
        scratch_shapes=[
            pltpu.VMEM(*entry) if isinstance(entry, tuple) else entry for entry in scratch
        ],
        compiler_params=pltpu.CompilerParams(vmem_limit_bytes=room + room // 16 + (3 << 20)),
        cost_estimate=pl.CostEstimate(
            flops=int(micros * 0.3e9), bytes_accessed=int(micros * 1e5), transcendentals=0
        ),
        name=name,
    )(*args, *ties)


def dot(a, b):
    return jnp.dot(a, b, preferred_element_type=F32)


def dot_t(a, b):
    return lax.dot_general(a, b, (((1,), (1,)), ((), ())), preferred_element_type=F32)


def t_dot(a, b):
    return lax.dot_general(a, b, (((0,), (0,)), ((), ())), preferred_element_type=F32)


def at(start, size, unit=None):
    return pl.ds(pl.multiple_of(start, unit or size), size)


def gelu_pair(a):
    square = a * a
    bent = jnp.tanh(GELU_SCALE * (a + 0.044715 * (a * square)))
    half = 0.5 * (1.0 + bent)
    slope = half + 0.5 * a * (1.0 - bent * bent) * (GELU_SCALE + 3 * 0.044715 * GELU_SCALE * square)
    return a * half, slope


def xor_pairs(size, mask):
    return [(i, i ^ mask) for i in range(size)]


def shift_pairs(size, step):
    return [(i, (i + step) % size) for i in range(size)]


def swap_context(x):
    return lax.ppermute(x, "context", [(0, 1), (1, 0)])


def sum_over(x, axis):
    size = lax.axis_size(axis)
    if size == 4:
        first = lax.ppermute(x, axis, xor_pairs(4, 1))
        second = lax.ppermute(x, axis, xor_pairs(4, 2))
        third = lax.ppermute(x, axis, xor_pairs(4, 3))
        return (x + first) + (second + third)
    step = 1
    while step < size:
        x = x + lax.ppermute(x, axis, xor_pairs(size, step))
        step *= 2
    return x


def copy_kernel(x_ref, out_ref):
    out_ref[...] = x_ref[...]


def add_kernel(x_ref, y_ref, out_ref):
    out_ref[...] = (x_ref[...].astype(F32) + y_ref[...].astype(F32)).astype(out_ref.dtype)


def toward(place, k, size):
    return place[2] ^ k if size == 4 else lax.rem(place[2] + k, size)


def origin(place, k, size):
    return place[2] ^ k if size == 4 else lax.rem(place[2] + size - k, size)


def spread_tensor(x):
    size = lax.axis_size("tensor")
    if size == 4:
        near = lax.ppermute(x, "tensor", xor_pairs(4, 1))
        far = lax.ppermute(x, "tensor", xor_pairs(4, 2))
        (again,) = call(copy_kernel, "again", [(x.shape, x.dtype)], (far,), scalars=0, micros=0.5, ties=(near,))
        return [near, far, lax.ppermute(again, "tensor", xor_pairs(4, 1))]
    return [lax.ppermute(x, "tensor", shift_pairs(size, k)) for k in range(1, size)]


def deliver_tensor(pieces):
    size = lax.axis_size("tensor")
    if size == 4:
        passed = lax.ppermute(pieces[2], "tensor", xor_pairs(4, 1))
        near = lax.ppermute(pieces[0], "tensor", xor_pairs(4, 1))
        (joined,) = call(
            add_kernel, "joined", [(passed.shape, BF16)], (pieces[1], passed), scalars=0, micros=0.5, ties=(near,)
        )
        return [near, lax.ppermute(joined, "tensor", xor_pairs(4, 2))]
    return [lax.ppermute(x, "tensor", shift_pairs(size, k + 1)) for k, x in enumerate(pieces)]


def cmul(ar, ai, br, bi):
    return ar * br - ai * bi, ar * bi + ai * br


def modes(damping, frequency, timestep):
    magnitude = jnp.exp(-timestep * damping)
    angle = timestep * frequency
    return magnitude * jnp.cos(angle), magnitude * jnp.sin(angle)


def ratios(damping, frequency, ar, ai):
    minus = ar - 1.0
    inverse = 1.0 / (damping * damping + frequency * frequency)
    return (ai * frequency - minus * damping) * inverse, -(
        minus * frequency + ai * damping
    ) * inverse


def low_powers(ar, ai, count):
    found = [None, (ar, ai)]
    for j in range(2, count):
        found.append(cmul(*found[j // 2], *found[j - j // 2]))
    return found


def taps_kernel(place, d_ref, f_ref, t_ref, mr_ref, mi_ref, k_ref, ar_s, ai_s, wr_s, wi_s, acc, lags):
    damping, frequency, timestep = d_ref[...].T, f_ref[...].T, t_ref[...][None, :]
    ar, ai = modes(damping, frequency, timestep)
    qr, qi = ratios(damping, frequency, ar, ai)
    mr, mi = mr_ref[...].T, mi_ref[...].T
    wr, wi = mr * qr - mi * qi, mr * qi + mi * qr
    ar_s[...] = ar
    ai_s[...] = ai
    if lags < REACH:
        power = (ar, ai)
        for _ in range(lags.bit_length() - 1):
            power = cmul(*power, *power)
        later = place[1] > 0
        vr, vi = cmul(wr, wi, *power)
        wr, wi = jnp.where(later, vr, wr), jnp.where(later, vi, wi)
    wr_s[...] = wr
    wi_s[...] = wi
    acc[...] = jnp.zeros_like(acc)

    def pair(p, carry):
        rows = at(16 * p, 16)
        a = (ar_s[rows, :], ai_s[rows, :])
        base = low_powers(*a, 8)
        eight = cmul(*base[4], *base[4])

        def outer(o, w):
            wr, wi = w
            start = pl.multiple_of(64 * o, 64)
            for j in range(8):
                term = wr if j == 0 else wr * base[j][0] - wi * base[j][1]
                acc[pl.ds(start + 8 * j, 8), :] += term[:8] + term[8:]
            return cmul(wr, wi, *eight)

        lax.fori_loop(0, lags // 8, outer, (wr_s[rows, :], wi_s[rows, :]), unroll=2)
        return carry

    lax.fori_loop(0, ar_s.shape[0] // 16, pair, 0)
    k_ref[...] = jnp.sum(acc[...].reshape(lags, 8, acc.shape[1]), axis=1)


def make_taps(place, damping, frequency, timestep, mix_real, mix_imaginary, lags):
    channels, count = damping.shape
    return call(
        partial(taps_kernel, lags=lags),
        "taps",
        [((lags, channels), F32)],
        (place, damping, frequency, timestep, mix_real, mix_imaginary),
        scratch=[((count, channels), F32)] * 4 + [((lags * 8, channels), F32)],
        micros=TAPS,
    )[0]


def shifted_copies(pad, copies, lead):
    length = copies.shape[1]
    for r in range(8):
        start = 64 + lead - r
        copies[r, :, :] = pad[start : start + length, :]


def linked_blocks(edges, first, step, bound):
    blocks = edges.shape[0] // 2
    mine = edges[first] if step < 0 else edges[blocks + first]

    def more(count):
        there = jnp.clip(first + step * (count + 1), 0, blocks - 1)
        edge = edges[blocks + there] if step < 0 else edges[there]
        return jnp.logical_and(count < bound, edge == mine)

    return lax.while_loop(more, lambda c: c + 1, 0)


def tile(index):
    return at(8 * index, 8)


def fill_ids(place, own, other, own_row, other_row, edges, ids, early):
    length, channels = ids.shape
    tokens = own_row.shape[1]
    valid = place[1] > 0 if early else place[1] == 0
    near = slice(tokens - REACH, tokens) if early else slice(0, REACH)
    halo = jnp.where(valid, other_row[:, near].astype(F32), -1.0)
    mine = own_row[...].astype(F32)
    at_halo, at_own = (0, REACH) if early else (tokens, 0)
    ids[at_halo : at_halo + REACH, :] = jnp.broadcast_to(halo, (channels, REACH)).T
    ids[at_own : at_own + tokens, :] = jnp.broadcast_to(mine, (channels, tokens)).T
    blocks = length // 64
    for b in range(blocks):
        for edge, offset in ((0, 0), (blocks, 63)):
            position = 64 * b + offset
            if at_own <= position < at_own + tokens:
                edges[edge + b] = own[0, position - at_own]
            else:
                value = other[0, position - at_halo + near.start]
                edges[edge + b] = jnp.where(valid, value, -1)


def fill_taps(place, pad, mine_ref, other_ref, flip):
    mine, other = mine_ref[...], other_ref[...]
    first = jnp.where(place[1] == 0, mine, other)
    second = jnp.where(place[1] == 0, other, mine)
    half = mine.shape[0]
    pad[...] = jnp.zeros_like(pad)
    if not flip:
        pad[64 : 64 + half, :] = first
        pad[64 + half : 64 + 2 * half, :] = second
        return
    end = 64 + 2 * half
    for l in range(half):
        pad[end - 1 - l : end - l, :] = first[l : l + 1]
        pad[end - half - 1 - l : end - half - l, :] = second[l : l + 1]


def fill_rows(whole, pieces):
    start = 0
    for piece in pieces:
        whole[start : start + piece.shape[0], :] = piece[...]
        start += piece.shape[0]


def forward_kernel(
    place, own, other, own_row, other_row, k0_ref, k1_ref, halo_ref, lo_ref, hi_ref, y_ref,
    edges, pad, copies, kept, u_s, s_ref,
):
    channels = lo_ref.shape[1]
    blocks = u_s.shape[0] // 64
    ahead = REACH // 64
    fill_ids(place, own, other, own_row, other_row, edges, s_ref, True)
    fill_taps(place, pad, k0_ref, k1_ref, False)
    shifted_copies(pad, copies, 0)
    fill_rows(u_s, (halo_ref, lo_ref, hi_ref))
    for b in range(blocks):
        rows = slice(64 * b, 64 * b + 64)
        edge = edges[blocks + b].astype(F32)
        kept[rows, :] = jnp.where(s_ref[rows, :] == edge, u_s[rows, :], 0.0)

    def block(i, carry):
        mine = i + ahead
        zero = jnp.zeros((8, channels), F32)
        reach = linked_blocks(edges, mine, -1, ahead)

        def far(d, sums):
            sums = list(sums)
            start = pl.multiple_of(64 * (mine - 1 - d), 64)
            for r in range(8):
                taps = [copies[r, tile(8 * (d + 1) + m), :] for m in range(-7, 8)]
                for q in range(8):
                    u = kept[pl.ds(start + 8 * q + r, 1), :]
                    for t in range(8):
                        sums[t] += taps[t - q + 7] * u
            return tuple(sums)

        sums = lax.fori_loop(0, reach, far, (zero,) * 8)
        base = pl.multiple_of(64 * mine, 64)
        ids = [s_ref[pl.ds(base + 8 * t, 8), :] for t in range(8)]
        first = edges[mine].astype(F32)
        sums = [jnp.where(ids[t] == first, sums[t], 0.0) for t in range(8)]
        for r in range(8):
            taps = [copies[r, 8 * m : 8 * m + 8, :] for m in range(8)]
            for q in range(8):
                u = u_s[pl.ds(base + 8 * q + r, 1), :]
                own = s_ref[pl.ds(base + 8 * q + r, 1), :]
                for t in range(q, 8):
                    sums[t] += jnp.where(ids[t] == own, taps[t - q], 0.0) * u
        for t in range(0, 8, 2):
            both = jnp.concatenate([sums[t], sums[t + 1]], 0)
            y_ref[at(64 * i + 8 * t, 16), :] = both.astype(y_ref.dtype)
        return carry

    lax.fori_loop(0, blocks - ahead, block, 0)


def forward_mix(place, ids, taps, halo, low, high):
    channels = low.shape[1]
    length = halo.shape[0] + low.shape[0] + high.shape[0]
    return call(
        forward_kernel,
        "forward_mix",
        [((length - REACH, channels), BF16)],
        (place, *ids, *ids, *taps, halo, low, high),
        scalars=3,
        scratch=[
            pltpu.SMEM((2 * length // 64,), jnp.int32),
            ((64 + REACH + 128, channels), F32),
            ((8, 64 + REACH, channels), F32),
            ((length, channels), F32),
            ((length, channels), F32),
            ((length, channels), F32),
        ],
        micros=5,
    )[0]


def backward_kernel(
    place, own, other, own_row, other_row, k0_ref, k1_ref, lo_ref, hi_ref, halo_ref, slope_ref,
    part_ref, w_ref, low_ref, sum_ref, own_ref, *rest,
):
    *sends, edges, pad, copies, alive, g_s, s_ref = rest
    channels = lo_ref.shape[1]
    blocks = g_s.shape[0] // 64
    ahead = REACH // 64
    fill_ids(place, own, other, own_row, other_row, edges, s_ref, False)
    fill_taps(place, pad, k0_ref, k1_ref, True)
    shifted_copies(pad, copies, -57)
    fill_rows(g_s, (lo_ref, hi_ref, halo_ref))
    for b in range(blocks):
        rows = slice(64 * b, 64 * b + 64)
        edge = edges[b].astype(F32)
        alive[rows, :] = jnp.where(s_ref[rows, :] == edge, g_s[rows, :], 0.0)

    def block(j, total):
        zero = jnp.zeros((8, channels), F32)
        reach = linked_blocks(edges, j, 1, ahead)

        def far(d, sums):
            sums = list(sums)
            start = pl.multiple_of(64 * (j + 1 + d), 64)
            for r in range(8):
                taps = [copies[r, tile(39 - (8 * (d + 1) + m)), :] for m in range(-7, 8)]
                for q in range(8):
                    g = alive[pl.ds(start + 8 * q + r, 1), :]
                    for t in range(8):
                        sums[t] += taps[q - t + 7] * g
            return tuple(sums)

        sums = lax.fori_loop(0, reach, far, (zero,) * 8)
        base = pl.multiple_of(64 * j, 64)
        ids = [s_ref[pl.ds(base + 8 * t, 8), :] for t in range(8)]
        last = edges[blocks + j].astype(F32)
        sums = [jnp.where(ids[t] == last, sums[t], 0.0) for t in range(8)]
        for r in range(8):
            taps = [copies[r, 8 * (39 - m) : 8 * (39 - m) + 8, :] for m in range(8)]
            for q in range(8):
                g = g_s[pl.ds(base + 8 * q + r, 1), :]
                own = s_ref[pl.ds(base + 8 * q + r, 1), :]
                for t in range(q + 1):
                    sums[t] += jnp.where(ids[t] == own, taps[q - t], 0.0) * g
        for t in range(0, 8, 2):
            rows = at(64 * j + 8 * t, 16)
            both = jnp.concatenate([sums[t], sums[t + 1]], 0) * slope_ref[rows, :]
            low_ref[rows, :] = both.astype(low_ref.dtype)
            total = total + both
        return total

    total = lax.fori_loop(0, blocks - ahead, block, jnp.zeros((16, channels), F32))
    sum_ref[...] = jnp.sum(total, axis=0, keepdims=True)
    size = len(sends) + 1
    height = own_ref.shape[0]
    for k in range(size):
        rows = at(height * toward(place, k, size), height)
        piece = part_ref[rows, :] + dot_t(low_ref[rows, :], w_ref[...])
        if k == 0:
            own_ref[...] = piece
        else:
            sends[k - 1][...] = piece.astype(BF16)


def backward_mix(place, ids, taps, low, high, halo, slope, part, weight, size):
    channels = low.shape[1]
    length = halo.shape[0] + low.shape[0] + high.shape[0]
    piece = (part.shape[0] // size, part.shape[1])
    return call(
        backward_kernel,
        "backward_mix",
        [(slope.shape, BF16), ((1, channels), F32), (piece, F32)] + [(piece, BF16)] * (size - 1),
        (place, *ids, *ids, *taps, low, high, halo, slope, part, weight),
        scalars=3,
        scratch=[
            pltpu.SMEM((2 * length // 64,), jnp.int32),
            ((64 + REACH + 128, channels), F32),
            ((8, 64 + REACH, channels), F32),
            ((length, channels), F32),
            ((length, channels), F32),
            ((length, channels), F32),
        ],
        micros=6,
    )


def put_row(out_ref, start, row):
    width = out_ref.shape[1]
    for i in range(row.shape[1] // width):
        out_ref[start + i : start + i + 1, :] = row[:, width * i : width * (i + 1)]
    return start + row.shape[1] // width


def taps_back_kernel(
    place, own_id, other_id, own_row, other_row, halo_ref, ulo_ref, uhi_ref, lo_ref, hi_ref,
    out_ref, edges, kept, u_s, g_s, s_ref, sums,
):
    channels = ulo_ref.shape[1]
    blocks = u_s.shape[0] // 64
    ahead = REACH // 64
    fill_ids(place, own_id, other_id, own_row, other_row, edges, s_ref, True)
    fill_rows(u_s, (halo_ref, ulo_ref, uhi_ref))
    fill_rows(g_s, (lo_ref, hi_ref))
    sums[...] = jnp.zeros_like(sums)
    for b in range(blocks):
        rows = slice(64 * b, 64 * b + 64)
        edge = edges[blocks + b].astype(F32)
        kept[rows, :] = jnp.where(s_ref[rows, :] == edge, u_s[rows, :], 0.0)

    def block(i, carry):
        mine = i + ahead
        reach = linked_blocks(edges, mine, -1, ahead)
        base = pl.multiple_of(64 * mine, 64)
        back = pl.multiple_of(64 * i, 64)
        ids = [s_ref[pl.ds(base + 8 * t, 8), :] for t in range(8)]
        whole = [g_s[pl.ds(back + 8 * t, 8), :] for t in range(8)]
        first = edges[mine].astype(F32)
        alive = [jnp.where(ids[t] == first, whole[t], 0.0) for t in range(8)]

        def far(d, carried):
            start = pl.multiple_of(64 * (mine - 1 - d), 64)
            for r in range(8):
                found = [None] * 15
                for q in range(8):
                    u = kept[pl.ds(start + 8 * q + r, 1), :]
                    for t in range(8):
                        term = carried[t] * u
                        m = t - q + 7
                        found[m] = term if found[m] is None else found[m] + term
                for m in range(-7, 8):
                    sums[r, tile(8 * (d + 1) + m), :] += found[m + 7]
            return carried

        lax.fori_loop(0, reach, far, tuple(alive))
        for r in range(8):
            found = [None] * 8
            for q in range(8):
                u = u_s[pl.ds(base + 8 * q + r, 1), :]
                own = s_ref[pl.ds(base + 8 * q + r, 1), :]
                for t in range(q, 8):
                    term = jnp.where(ids[t] == own, whole[t], 0.0) * u
                    m = t - q
                    found[m] = term if found[m] is None else found[m] + term
            for m in range(8):
                sums[r, 8 * m : 8 * m + 8, :] += found[m]
        return carry

    lax.fori_loop(0, blocks - ahead, block, 0)
    total = sums[0, 0:REACH, :]
    for r in range(1, 8):
        total = total + sums[r, r : r + REACH, :]
    out_ref[...] = total


def gain_kernel(place, x_ref, own_ref, *rest, vectors):
    out_ref = rest[-1]
    sends = rest[: -1 - vectors]
    start = 0
    for ref in rest[-1 - vectors : -1]:
        start = put_row(out_ref, start, ref[...])
    size = len(sends) + 1
    height = own_ref.shape[0]
    gain = jnp.zeros((8, x_ref.shape[1]), F32)
    bias = gain
    step = min(64, height)
    for k in range(size):
        source = own_ref if k == 0 else sends[k - 1]

        def rows_step(i, state, source=source, k=k):
            gain, bias = state
            unit, _ = unit_rows(x_ref[at(height * toward(place, k, size) + step * i, step), :])
            part = source[at(step * i, step), :].astype(F32)
            scaled = part * unit
            for j in range(0, step, 8):
                gain = gain + scaled[j : j + 8]
                bias = bias + part[j : j + 8]
            return gain, bias

        gain, bias = lax.fori_loop(0, height // step, rows_step, (gain, bias))
    start = put_row(out_ref, start, jnp.sum(gain, axis=0, keepdims=True))
    put_row(out_ref, start, jnp.sum(bias, axis=0, keepdims=True))


def gain_sums(place, channels, rows, own, sends, vectors, ties):
    count = (sum(v.shape[1] for v in vectors) + 2 * rows.shape[1]) // channels
    return call(
        partial(gain_kernel, vectors=len(vectors)),
        "gain",
        [((count, channels), F32)],
        (place, rows, own, *sends, *vectors),
        micros=0.2,
        ties=ties,
    )[0]


def taps_back(place, ids, halo, u_low, u_high, low, high, ties):
    channels = low.shape[1]
    length = halo.shape[0] + low.shape[0] + high.shape[0]
    return call(
        taps_back_kernel,
        "taps_back",
        [((REACH, channels), F32)],
        (place, *ids, *ids, halo, u_low, u_high, low, high),
        scalars=3,
        ties=ties,
        scratch=[
            pltpu.SMEM((2 * length // 64,), jnp.int32),
            ((length, channels), F32),
            ((length, channels), F32),
            ((length - REACH, channels), F32),
            ((length, channels), F32),
            ((8, 64 + REACH, channels), F32),
        ],
        micros=TAPS_BACK,
    )[0]


def modes_back_kernel(
    place, c_ref, d_ref, f_ref, t_ref, mr_ref, mi_ref, out_ref,
    ar_s, ai_s, gr_s, gi_s, hr_s, hi_s, wide, wide_l,
):
    channels = c_ref.shape[1]
    count = ar_s.shape[0]
    half = at(count * place[1], count)
    damping, frequency, timestep = d_ref[:, half].T, f_ref[:, half].T, t_ref[...][None, :]
    ar, ai = modes(damping, frequency, timestep)
    ar_s[...] = ar
    ai_s[...] = ai
    for l in range(REACH):
        row = jnp.broadcast_to(c_ref[l : l + 1, :], (8, channels))
        wide[8 * l : 8 * l + 8, :] = row
        wide_l[8 * l : 8 * l + 8, :] = row * float(l)

    def one(p, carry):
        rows = at(8 * p, 8)
        a = (ar_s[rows, :], ai_s[rows, :])
        base = low_powers(*a, 16)
        jump = cmul(*base[8], *base[8])
        zero = jnp.zeros((8, channels), F32)

        def outer(o, state):
            pr, pi, gr, gi, hr, hi = state
            start = pl.multiple_of(128 * o, 128)
            sr = wide[pl.ds(start, 8), :]
            tr = wide_l[pl.ds(start, 8), :]
            si = zero
            ti = zero
            for j in range(1, 16):
                c = wide[pl.ds(start + 8 * j, 8), :]
                e = wide_l[pl.ds(start + 8 * j, 8), :]
                br, bi = base[j]
                sr += c * br
                si += c * bi
                tr += e * br
                ti += e * bi
            gr += pr * sr - pi * si
            gi += pr * si + pi * sr
            hr += pr * tr - pi * ti
            hi += pr * ti + pi * tr
            pr, pi = cmul(pr, pi, *jump)
            return pr, pi, gr, gi, hr, hi

        one_ = jnp.ones((8, channels), F32)
        _, _, gr, gi, hr, hi = lax.fori_loop(
            0, REACH // 16, outer, (one_, zero, zero, zero, zero, zero), unroll=2
        )
        gr_s[rows, :] = gr
        gi_s[rows, :] = gi
        hr_s[rows, :] = hr
        hi_s[rows, :] = hi
        return carry

    lax.fori_loop(0, ar_s.shape[0] // 8, one, 0)
    gr, gi, hr, hi = gr_s[...], gi_s[...], hr_s[...], hi_s[...]
    mr, mi = mr_ref[:, half].T, mi_ref[:, half].T
    qr, qi = ratios(damping, frequency, ar, ai)
    wr, wi = cmul(mr, mi, qr, qi)
    mixr, mixi = cmul(qr, qi, gr, gi)
    inverse = 1.0 / (damping * damping + frequency * frequency)
    nr, ni = -damping * inverse, -frequency * inverse
    vr, vi = cmul(*cmul(mr, mi, gr, gi), nr, ni)
    xr, xi = cmul(vr, vi, ar, ai)
    zr, zi = cmul(wr, wi, hr, hi)
    xr, xi = xr + zr, xi + zi
    yr, yi = cmul(vr, vi, qr, qi)
    grads = (yr - timestep * xr, yi - timestep * xi, mixr, -mixi)
    for i, grad in enumerate(grads):
        out_ref[channels * i : channels * (i + 1), :] = grad.T
    out_ref[4 * channels :, 0:channels] = jnp.broadcast_to(
        jnp.sum(-damping * xr - frequency * xi, axis=0, keepdims=True), (8, channels)
    )


def modes_back(place, c, damping, frequency, timestep, mix_real, mix_imaginary):
    channels, count = damping.shape
    count = count // 2
    return call(
        modes_back_kernel,
        "modes_back",
        [((4 * channels + 8, count), F32)],
        (place, c, damping, frequency, timestep, mix_real, mix_imaginary),
        scratch=[((count, channels), F32)] * 6 + [((REACH * 8, channels), F32)] * 2,
        micros=MODES_BACK,
    )[0]


def unit_rows(x):
    x = x.astype(F32)
    shifted = x - jnp.mean(x, axis=-1, keepdims=True)
    inverse = lax.rsqrt(jnp.mean(shifted * shifted, axis=-1, keepdims=True) + EPSILON)
    return shifted * inverse, inverse


def norm_kernel(x_ref, gain_ref, bias_ref, out_ref):
    def step(i, carry):
        rows = at(128 * i, 128)
        unit, _ = unit_rows(x_ref[rows, :])
        out_ref[rows, :] = (unit * gain_ref[...][None, :] + bias_ref[...][None, :]).astype(BF16)
        return carry

    lax.fori_loop(0, x_ref.shape[0] // 128, step, 0)


def reduce_kernel(place, x_ref, b_ref, *rest, count):
    pieces = rest[:count]
    lo_ref, hi_ref, slope_ref, full_ref = rest[count:]
    depth = pieces[0].shape[0]
    for k in range(count):
        full_ref[at(depth * (place[0] ^ k if count > 1 else 0), depth), :] = pieces[k][...]
    half = lo_ref.shape[0]
    for part, out in enumerate((lo_ref, hi_ref)):
        rows = slice(half * part, half * part + half)
        act, slope = gelu_pair(dot(x_ref[rows, :], full_ref[...]) + b_ref[...][None, :])
        out[...] = act
        slope_ref[rows, :] = slope


def gate_kernel(x_ref, w_ref, b_ref, act_ref, slope_ref):
    def step(i, carry):
        rows = at(128 * i, 128)
        act, slope = gelu_pair(dot(x_ref[rows, :], w_ref[...]) + b_ref[...][None, :])
        act_ref[rows, :] = act.astype(BF16)
        slope_ref[rows, :] = slope.astype(BF16)
        return carry

    lax.fori_loop(0, x_ref.shape[0] // 128, step, 0)


def pack_kernel(place, gate_ref, expand_ref, output_ref, mine_ref, rest_ref):
    rows = gate_ref.shape[0]
    some = expand_ref.shape[0] // 2

    def store(first_ref, second_ref):
        first_ref[0:rows, :] = gate_ref[...]
        first_ref[rows:, :] = expand_ref[0:some, :]
        second_ref[0:rows, :] = output_ref[...].T
        second_ref[rows:, :] = expand_ref[some:, :]

    @pl.when(place[1] == 0)
    def _():
        store(mine_ref, rest_ref)

    @pl.when(place[1] != 0)
    def _():
        store(rest_ref, mine_ref)


def stack_kernel(*refs):
    for k, ref in enumerate(refs[:-1]):
        refs[-1][k] = ref[...]


def unpack_kernel(place, mine_ref, rest_ref, near_ref, far_ref, gate_ref, expand_ref, output_ref):
    mines = [mine_ref] + [near_ref.at[k] for k in range(3)]
    rests = [rest_ref] + [far_ref.at[k] for k in range(3)]
    rows = gate_ref.shape[0] // 4
    some = expand_ref.shape[0] // 8

    def store(firsts, seconds):
        for k in range(4):
            s = place[0] ^ k
            gate_ref[at(rows * s, rows), :] = firsts[k][0:rows, :]
            output_ref[at(rows * s, rows), :] = seconds[k][0:rows, :]
            expand_ref[at(2 * some * s, some), :] = firsts[k][rows:, :]
            expand_ref[at(2 * some * s + some, some), :] = seconds[k][rows:, :]

    @pl.when(place[1] == 0)
    def _():
        store(mines, rests)

    @pl.when(place[1] != 0)
    def _():
        store(rests, mines)


def expand_kernel(place, act_ref, slope_ref, we_ref, b_ref, wo_ref, *rest, size):
    pieces, rest = rest[:size], rest[size:]
    gated_ref, coef_ref, own_ref, *sends = rest
    height = own_ref.shape[0]
    channels = pieces[0].shape[1]
    for k in range(size):
        rows = at(height * toward(place, k, size), height)
        expanded = b_ref[...][None, :]
        for j in range(size):
            source = origin(place, j, size)
            expanded = expanded + dot(pieces[j][rows, :], we_ref[at(channels * source, channels), :])
        coef_ref[rows, :] = (slope_ref[rows, :].astype(F32) * expanded).astype(BF16)
        gated = (expanded * act_ref[rows, :].astype(F32)).astype(BF16)
        gated_ref[rows, :] = gated
        piece = dot_t(gated, wo_ref[...])
        if k == 0:
            own_ref[...] = piece
        else:
            sends[k - 1][...] = piece.astype(BF16)


def loss_kernel(
    place, x_ref, t_ref, mask_ref, b_ref, act_ref, coef_ref, wo_ref, we_ref, *rest, size
):
    pieces, rest = rest[:size], rest[size:]
    out_ref, back_ref, keep_ref, low_ref, gate_ref, ob_ref, eb_ref, gb_ref, err_ref, own_ref, *rest = rest
    sends, mask_s = rest[:-1], rest[-1]
    height = pieces[0].shape[0]
    channels = own_ref.shape[1]
    mask_s[...] = jnp.broadcast_to(mask_ref[...].astype(F32), (mask_s.shape[1], mask_s.shape[0])).T
    outb = jnp.zeros_like(ob_ref)
    expb = jnp.zeros_like(eb_ref)
    gatb = jnp.zeros_like(gb_ref)
    errors = jnp.zeros((1, 1), F32)
    for j in range(size):
        rows = at(height * origin(place, j, size), height)
        result = x_ref[rows, :].astype(F32) + pieces[j][...].astype(F32) + b_ref[...][None, :]
        out_ref[rows, :] = result.astype(BF16)
        back = (result - t_ref[rows, :].astype(F32)) * mask_s[rows, 0:1]
        low = back.astype(BF16)
        back_ref[rows, :] = low
        if j == 0:
            keep_ref[...] = back
        outb = outb + jnp.sum(back, axis=0, keepdims=True)
        errors = errors + jnp.sum(jnp.sum(back * back, axis=0, keepdims=True), axis=1, keepdims=True)
        gated_back = dot(low, wo_ref[...])
        expanded_back = gated_back * act_ref[rows, :].astype(F32)
        expb = expb + jnp.sum(expanded_back, axis=0, keepdims=True)
        expand_low = expanded_back.astype(BF16)
        low_ref[rows, :] = expand_low
        gate_back = gated_back * coef_ref[rows, :].astype(F32)
        gatb = gatb + jnp.sum(gate_back, axis=0, keepdims=True)
        gate_ref[rows, :] = gate_back.astype(BF16)
        for k in range(size):
            target = toward(place, k, size)
            part = dot_t(expand_low, we_ref[at(channels * target, channels), :])
            if k == 0:
                own_ref[rows, :] = part
            else:
                sends[k - 1][rows, :] = part.astype(BF16)
    ob_ref[...] = outb
    eb_ref[...] = expb
    gb_ref[...] = gatb
    count = jnp.sum(mask_ref[...].astype(F32), axis=1, keepdims=True)
    half = err_ref.shape[1] // 2
    err_ref[...] = jnp.concatenate(
        [jnp.broadcast_to(errors, (1, half)), jnp.broadcast_to(count, (1, half))], 1
    )


def sum_kernel(own_ref, *rest):
    *pieces, lo_ref, hi_ref = rest
    total = own_ref[...]
    for piece in pieces:
        total = total + piece[...].astype(F32)
    half = lo_ref.shape[0]
    lo_ref[...] = total[:half]
    hi_ref[...] = total[half:]


def scale_of(total_ref, scale):
    row, tokens_all = scale
    return tokens_all / total_ref[row : row + 1, 0:1]


EXTRA = 16


def rows_kernel(place, x_ref, gain_ref, keep_ref, total_ref, own_ref, *rest, scale):
    *pieces, out_ref = rest
    height, features = own_ref.shape
    step = 32
    factor = scale_of(total_ref, scale)
    gain = gain_ref[...][None, :]

    def one(i, carry):
        rows = at(step * i, step)
        total = own_ref[rows, :]
        for piece in pieces:
            total = total + piece[rows, :].astype(F32)
        unit, inverse = unit_rows(x_ref[at(height * place[2] + step * i, step), :])
        scaled = total * gain
        back = inverse * (
            scaled
            - jnp.mean(scaled, axis=-1, keepdims=True)
            - unit * jnp.mean(scaled * unit, axis=-1, keepdims=True)
        )
        out_ref[rows, :] = (factor * (keep_ref[rows, :] + back)).astype(BF16)
        return carry

    lax.fori_loop(0, height // step, one, 0, unroll=2)
    width = total_ref.shape[1]
    count = features // width
    start = total_ref.shape[0] - 2 * count
    both = []
    for v in range(2):
        first = start + count * v
        both.append(
            jnp.concatenate(
                [total_ref[first + i : first + i + 1, :] for i in range(count)], axis=1
            )
        )
    both.append(jnp.zeros((EXTRA - 2, features), F32))
    out_ref[height:, :] = (factor * jnp.concatenate(both, 0)).astype(BF16)


def join_kernel(place, *rest):
    *pieces, out_ref, norm_ref, parts = rest
    size = len(pieces)
    height = pieces[0].shape[0] - EXTRA
    for k in range(size):
        source = origin(place, k, size)
        out_ref[at(height * source, height), :] = pieces[k][0:height, :]
        parts[source] = pieces[k][height:, :].astype(F32)
    total = parts[0]
    for k in range(1, size):
        total = total + parts[k]
    norm_ref[...] = total


def finish_kernel(place, sum_ref, mine_ref, other_ref, *outs, starts, scale):
    dd_ref, df_ref, dmr_ref, dmi_ref, dt_ref, loss_ref, *vectors = outs
    channels, count = dd_ref.shape
    count = count // 2
    counted = sum_ref[scale[0] : scale[0] + 1, 0:1]
    loss_ref[...] = sum_ref[scale[0] - 1 : scale[0], 0:1] / (counted * scale[2])
    scale = scale_of(sum_ref, scale[:2])
    for i, out in enumerate((dd_ref, df_ref, dmr_ref, dmi_ref)):
        rows = slice(channels * i, channels * (i + 1))
        out[:, at(count * place[1], count)] = mine_ref[rows, :] * scale
        out[:, at(count * (1 - place[1]), count)] = other_ref[rows, :] * scale
    row = slice(4 * channels, 4 * channels + 1)
    dt_ref[...] = (mine_ref[row, 0:channels] + other_ref[row, 0:channels]) * scale
    width = sum_ref.shape[1]
    for out, start in zip(vectors, starts):
        for i in range(out.shape[1] // width):
            out[:, width * i : width * (i + 1)] = sum_ref[start + i : start + i + 1, :] * scale


def early_kernel(place, gated_ref, back_ref, low_ref, *rest, size):
    pieces, (keep_ref, give_ref, mixed_s) = rest[:size], rest[size:]
    core = place[1]
    channels = pieces[0].shape[1]
    for j in range(size):
        source = origin(place, j, size)
        mixed_s[:, at(channels * source, channels)] = pieces[j][...]
    half = back_ref.shape[1] // 8
    some = mixed_s.shape[1] // 8
    for s in range(4):
        k = s
        keep_ref[k, 0:half, :] = t_dot(back_ref[:, at((2 * s + core) * half, half)], gated_ref[...])
        give_ref[k, 0:half, :] = t_dot(
            back_ref[:, at((2 * s + 1 - core) * half, half)], gated_ref[...]
        ).astype(BF16)
        both = t_dot(mixed_s[:, at(2 * some * s, 2 * some)], low_ref[...])
        keep_ref[k, half:, :] = jnp.where(core == 0, both[:some], both[some:])
        give_ref[k, half:, :] = jnp.where(core == 0, both[some:], both[:some]).astype(BF16)


def late_kernel(place, x_ref, gate_ref, reduce_ref, keep_ref, give_ref):
    core = place[1]
    half = x_ref.shape[1] // 8
    units = gate_ref.shape[1]
    for s in range(4):
        k = s
        mine = x_ref[:, at((2 * s + core) * half, half)]
        keep_ref[k, :, 0:units] = t_dot(mine, gate_ref[...])
        keep_ref[k, :, units:] = t_dot(mine, reduce_ref[...])
        other = x_ref[:, at((2 * s + 1 - core) * half, half)]
        give_ref[k, :, 0:units] = t_dot(other, gate_ref[...]).astype(BF16)
        give_ref[k, :, units:] = t_dot(other, reduce_ref[...]).astype(BF16)


def pair_kernel(place, keep_ref, got_ref, own_ref, *sends):
    s = place[0]
    own_ref[...] = keep_ref[s] + got_ref[s].astype(F32)
    for k in (1, 2, 3):
        sends[k - 1][...] = (keep_ref[s ^ k] + got_ref[s ^ k].astype(F32)).astype(BF16)


def early_out_kernel(place, own_ref, other_ref, total_ref, output_ref, expand_ref, *, scale):
    scale = scale_of(total_ref, scale)
    mine, other = own_ref[...].astype(F32) * scale, other_ref[...].astype(F32) * scale
    first = jnp.where(place[1] == 0, mine, other)
    second = jnp.where(place[1] == 0, other, mine)
    half = output_ref.shape[1] // 2
    some = expand_ref.shape[0] // 2
    output_ref[...] = jnp.concatenate([first[:half], second[:half]], 0).T
    expand_ref[0:some, :] = first[half:]
    expand_ref[some:, :] = second[half:]


def late_out_kernel(place, own_ref, other_ref, total_ref, gate_ref, reduce_ref, *, scale):
    scale = scale_of(total_ref, scale)
    mine, other = own_ref[...].astype(F32) * scale, other_ref[...].astype(F32) * scale
    first = jnp.where(place[1] == 0, mine, other)
    second = jnp.where(place[1] == 0, other, mine)
    half = gate_ref.shape[0] // 2
    units = gate_ref.shape[1]
    gate_ref[0:half, :] = first[:, :units]
    gate_ref[half:, :] = second[:, :units]
    reduce_ref[0:half, :] = first[:, units:]
    reduce_ref[half:, :] = second[:, units:]


def pair_grads(place, keep, give):
    shape = keep.shape[1:]
    return call(
        pair_kernel,
        "pair",
        [(shape, F32)] + [(shape, BF16)] * 3,
        (place, keep, swap_context(give)),
        micros=PAIR,
    )


def send_grads(pieces):
    own, *sends = pieces
    for k in (1, 2, 3):
        own = own + lax.ppermute(sends[k - 1], "shard", xor_pairs(4, k)).astype(F32)
    return own, swap_context(own)


def plain_grad(grad, scale, axis):
    paired = lax.psum(grad.astype(BF16), "context").astype(F32)
    return scale * lax.psum_scatter(paired, "shard", scatter_dimension=axis, tiled=True)


def per_device(
    inputs,
    teacher,
    segment_ids,
    valid_mask,
    norm_gain,
    norm_bias,
    gate_weight,
    gate_bias,
    reduce_weight,
    reduce_bias,
    damping,
    frequency,
    timestep,
    mix_real,
    mix_imaginary,
    expand_weight,
    expand_bias,
    output_weight,
    output_bias,
):
    tokens, width = inputs.shape
    channels = reduce_bias.shape[0]
    units = gate_bias.shape[0]
    size = lax.axis_size("tensor")
    shards = lax.axis_size("shard")
    contexts = lax.axis_size("context")
    core = lax.axis_index("context")
    shard = lax.axis_index("shard")
    tensor = lax.axis_index("tensor")
    fast = shards == 4 and contexts == 2 and size == 4
    height = tokens // size
    place = jnp.stack([shard, core, tensor]).astype(jnp.int32)

    ids = (segment_ids, swap_context(segment_ids))
    if fast:
        found = [lax.ppermute(reduce_weight, "shard", xor_pairs(4, k)) for k in (1, 2, 3)]
        reduce_pieces = [reduce_weight] + found
        some = expand_weight.shape[0] // 2
        shape = (gate_weight.shape[0] + some, units)
        mine, rest = call(
            pack_kernel, "pack", [(shape, BF16)] * 2, (place, gate_weight, expand_weight, output_weight)
        )
        nears = [lax.ppermute(mine, "shard", xor_pairs(4, k)) for k in (1, 2, 3)]
    else:
        reduce_pieces = [lax.all_gather(reduce_weight, "shard", axis=0, tiled=True)]
        gate_full = lax.all_gather(gate_weight, "shard", axis=0, tiled=True)
        expand_full = lax.all_gather(expand_weight, "shard", axis=0, tiled=True)
        output_full = lax.all_gather(output_weight.T, "shard", axis=0, tiled=True)

    (normed,) = call(
        norm_kernel,
        "norm",
        [(inputs.shape, BF16)],
        (inputs, norm_gain, norm_bias),
        scalars=0,
    )
    mode_args = (damping, frequency, timestep, mix_real, mix_imaginary)
    taps_mine = make_taps(place, *mode_args, REACH // 2)
    taps = (taps_mine, swap_context(taps_mine))
    half_rows = (tokens // 2, channels)
    u_low, u_high, reduce_slope, reduce_full = call(
        partial(reduce_kernel, count=len(reduce_pieces)),
        "reduce",
        [(half_rows, F32), (half_rows, F32), ((tokens, channels), F32), ((width, channels), BF16)],
        (place, normed, reduce_bias, *reduce_pieces),
    )
    before = [(i, i + 1) for i in range(contexts - 1)]
    after = [(i + 1, i) for i in range(contexts - 1)]
    halo = lax.ppermute(u_high[tokens // 2 - REACH :], "context", before)
    mixed_own = forward_mix(place, ids, taps, halo, u_low, u_high)
    mixed = [mixed_own] + spread_tensor(mixed_own)
    if fast:
        shape = (3,) + mine.shape
        (near,) = call(stack_kernel, "stack", [(shape, BF16)], nears, scalars=0, ties=(mixed_own,))
        gate_full, expand_full, output_full = call(
            unpack_kernel,
            "unpack",
            [
                ((4 * gate_weight.shape[0], units), BF16),
                ((4 * expand_weight.shape[0], units), BF16),
                ((width, units), BF16),
            ],
            (place, mine, rest, near, swap_context(near)),
            micros=1,
        )
    gate_act, gate_slope = call(
        gate_kernel,
        "gate",
        [((tokens, units), BF16)] * 2,
        (normed, gate_full, gate_bias),
        scalars=0,
        micros=4,
    )
    piece = (height, width)
    gated, coef, branch_part, *branch_sends = call(
        partial(expand_kernel, size=size),
        "expand",
        [((tokens, units), BF16), ((tokens, units), BF16), (piece, F32)] + [(piece, BF16)] * (size - 1),
        (place, gate_act, gate_slope, expand_full, expand_bias, output_full, *mixed),
        micros=4,
    )
    for got in deliver_tensor(branch_sends):
        branch_part = branch_part + got.astype(F32)
    branch_own = branch_part.astype(BF16)
    branch = [branch_own] + spread_tensor(branch_own)

    output, branch_back, keep_back, expand_low, gate_low, *rest = call(
        partial(loss_kernel, size=size),
        "loss",
        [
            (inputs.shape, BF16),
            (inputs.shape, BF16),
            (piece, F32),
            ((tokens, units), BF16),
            ((tokens, units), BF16),
            ((1, width), F32),
            ((1, units), F32),
            ((1, units), F32),
            ((1, 2 * channels), F32),
            ((tokens, channels), F32),
        ]
        + [((tokens, channels), BF16)] * (size - 1),
        (
            place,
            inputs,
            teacher,
            valid_mask,
            output_bias,
            gate_act,
            coef,
            output_full,
            expand_full,
            *branch,
        ),
        scratch=[((tokens, 128), F32)],
        micros=8,
    )
    output_sum, expand_sum, gate_sum, error_row, back_part, *back_sends = rest
    back_got = deliver_tensor(back_sends)
    ties = ()
    if fast:
        shape = (4, (gate_weight.shape[0] + expand_weight.shape[0]) // 2, units)
        early = call(
            partial(early_kernel, size=size),
            "early",
            [(shape, F32), (shape, BF16)],
            (place, gated, branch_back, expand_low, *mixed),
            scratch=[((tokens, size * channels), BF16)],
            micros=EARLY,
            ties=(),
        )
        early = pair_grads(place, *early)
        ties = ()
    g_low, g_high = call(
        sum_kernel,
        "sum",
        [(half_rows, F32)] * 2,
        (back_part, *back_got),
        scalars=0,
        ties=ties,
    )
    halo_back = lax.ppermute(g_low[:REACH], "context", after)
    gate_part = dot_t(gate_low, gate_full)
    reduce_low, reduce_sum, normed_part, *normed_sends = backward_mix(
        place, ids, taps, g_low, g_high, halo_back, reduce_slope, gate_part, reduce_full, size
    )
    normed_got = deliver_tensor(normed_sends)

    vectors = (gate_sum, expand_sum, output_sum, reduce_sum, error_row)
    pack = gain_sums(place, channels, inputs, normed_part, normed_sends, vectors, ())
    norm_at = pack.shape[0] - 2 * width // channels
    total = sum_over(sum_over(pack, "context"), "shard")
    error_at = norm_at - 2
    taps_grad = taps_back(place, ids, halo, u_low, u_high, g_low, g_high, ())
    taps_grad = sum_over(sum_over(taps_grad, "context"), "shard")
    tokens_all = float(tokens * shards * contexts)

    scale = (error_at + 1, tokens_all)

    (rows_own,) = call(
        partial(rows_kernel, scale=scale),
        "rows",
        [((height + EXTRA, width), BF16)],
        (place, inputs, norm_gain, keep_back, total, normed_part, *normed_got),
        micros=3,
    )
    inputs_grad, norm_grads = call(
        join_kernel,
        "join",
        [(inputs.shape, BF16), ((EXTRA, width), F32)],
        (place, rows_own, *spread_tensor(rows_own)),
        scratch=[((size, EXTRA, width), F32)],
    )
    mode_mine = modes_back(place, taps_grad, *mode_args)
    mode_other = swap_context(mode_mine)

    if fast:
        output_grad, expand_grad = call(
            partial(early_out_kernel, scale=scale),
            "early_out",
            [(output_weight.shape, F32), (expand_weight.shape, F32)],
            (place, *send_grads(early), total),
        )
        shape = (4, gate_weight.shape[0] // 2, units + channels)
        late = call(
            late_kernel,
            "late",
            [(shape, F32), (shape, BF16)],
            (place, normed, gate_low, reduce_low),
            micros=LATE,
            ties=(),
        )
        gate_grad, reduce_grad = call(
            partial(late_out_kernel, scale=scale),
            "late_out",
            [(gate_weight.shape, F32), (reduce_weight.shape, F32)],
            (place, *send_grads(pair_grads(place, *late)), total),
        )
    else:
        factor = tokens_all / total[error_at + 1, 0]
        mixed_full = lax.all_gather(mixed_own, "tensor", axis=1, tiled=True)
        output_grad = plain_grad(t_dot(gated, branch_back), factor, 1)
        expand_grad = plain_grad(t_dot(mixed_full, expand_low), factor, 0)
        gate_grad = plain_grad(t_dot(normed, gate_low), factor, 0)
        reduce_grad = plain_grad(t_dot(normed, reduce_low), factor, 0)

    counts = [v.shape[1] // channels for v in vectors]
    offsets = [sum(counts[:i]) for i in range(4)]
    whole = (damping.shape, F32)
    *mode_grads, timestep_grad, loss_value, gate_bias_grad, expand_bias_grad, output_bias_grad, reduce_bias_grad = call(
        partial(finish_kernel, starts=offsets, scale=scale + (float(width),)),
        "finish",
        [whole] * 4 + [((1, n), F32) for n in (channels, 1, units, units, width, channels)],
        (place, total, mode_mine, mode_other),
    )
    return (
        output,
        loss_value.reshape(()),
        inputs_grad,
        norm_grads[0],
        norm_grads[1],
        gate_grad,
        gate_bias_grad[0],
        reduce_grad,
        reduce_bias_grad[0],
        mode_grads[0],
        mode_grads[1],
        timestep_grad[0],
        mode_grads[2],
        mode_grads[3],
        expand_grad,
        expand_bias_grad[0],
        output_grad,
        output_bias_grad[0],
    )


def solution(mesh):
    tokens = P(("shard", "context"), None)
    ids = P("shard", "context")
    split = P("shard", "tensor")
    rows = P("tensor", None)
    units = P("tensor")
    return jax.shard_map(
        per_device,
        mesh=mesh,
        in_specs=(
            tokens, tokens, ids, ids, P(), P(), split, units, split, units,
            rows, rows, units, rows, rows, split, units, P("tensor", "shard"), P(),
        ),
        out_specs=(
            tokens, P(), tokens, P(), P(), split, units, split, units,
            rows, rows, units, rows, rows, split, units, P("tensor", "shard"), P(),
        ),
        check_vma=False,
    )
```

time: 353 us -> 212 us (0.60); the launches traced: 348 us -> 211 us
  local copies, waits for them, and re-layouts: 72 us -> 3.6 us
  starting transfers between devices: 98.5 us -> 46 us
  waiting for transfers between devices: 69.5 us -> 93.9 us
  matrix products: 23.9 us -> 1.01 us
  other arithmetic: 23.9 us -> 1.68 us
  Pallas kernels: 56.7 us -> 63.8 us
    ppermute x46 -> x32, starting transfers between devices: 76 us -> 38.4 us  [the longest x3 5.37 us: spread_tensor(): near = lax.ppermute(x, 'tensor', xor_pairs(4, 1))]
    ppermute x46 -> x32, waiting for transfers between devices: 61 us -> 88.5 us  [the longest x3 26.1 us: spread_tensor(): far = lax.ppermute(x, 'tensor', xor_pairs(4, 2))]
    dynamic_update_slice x38 -> x0, local copies, waits for them, and re-layouts: 24.4 us -> none  [the longest x12 12.6 us: gather_weight(): lax.dynamic_update_slice(full, near[k - 1][None], (me ^ k, core * half, 0))]
    dot_general x8 -> x0, matrix products: 15.7 us -> none  [the longest x4 8.73 us: dot(): return jnp.dot(a, b, preferred_element_type=F32)]
    another operation x8 -> x0, local copies, waits for them, and re-layouts: 9.21 us -> none
    broadcast_in_dim x13 -> x0, local copies, waits for them, and re-layouts: 7.93 us -> none  [the longest x3 3.68 us: gather_rows(): full = lax.dynamic_update_slice(full, part[None], ((me - k) % size, 0, 0))]
    unnamed x125 -> x38, local copies, waits for them, and re-layouts: 10.9 us -> 3 us
    reduce_sum x6 -> x0, other arithmetic: 7.47 us -> none  [the longest x1 2.43 us: per_device(): jnp.sum(result_back, axis=0)]
  transfers between devices with their start and end apart: 85 -> 48, of which waited for: 27 -> 23; matrix products, arithmetic and copies ran while one was open for 27% -> 2% of each run, Pallas kernels for 16% -> 25%
where the time goes in v2:
time: 212 us; the launch traced here: 211 us
  waiting for transfers between devices  93.9 us (44%)
  Pallas kernels  63.8 us (30%)
  starting transfers between devices  46 us (22%)
  local copies, waits for them, and re-layouts  3.6 us (2%)
    pallas_call x30, Pallas kernels, call(): pl.pallas_call(kernel, out_shape=[jax.ShapeDtypeStruct(shape, kind) for s...  63.8 us
    ppermute x3, waiting for transfers between devices, spread_tensor(): far = lax.ppermute(x, 'tensor', xor_pairs(4, 2))  26.1 us
    ppermute x3, waiting for transfers between devices, deliver_tensor(): return [near, lax.ppermute(joined, 'tensor', xor_pairs(4, 2))]  20.4 us
    ppermute x6, waiting for transfers between devices, send_grads(): own = own + lax.ppermute(sends[k - 1], 'shard', xor_pairs(4, k)).astype(F32)  10.7 us
    ppermute x3, waiting for transfers between devices, deliver_tensor(): near = lax.ppermute(pieces[0], 'tensor', xor_pairs(4, 1))  10.2 us
    ppermute x3, waiting for transfers between devices, deliver_tensor(): passed = lax.ppermute(pieces[2], 'tensor', xor_pairs(4, 1))  9.96 us
    ppermute x3, waiting for transfers between devices, spread_tensor(): return [near, far, lax.ppermute(again, 'tensor', xor_pairs(4, 1))]  7.77 us
    ppermute x3, starting transfers between devices, spread_tensor(): near = lax.ppermute(x, 'tensor', xor_pairs(4, 1))  5.37 us
  transfers between devices with their start and end apart: 48, of which 23 were waited for; matrix products, arithmetic and copies ran while one was open for 2% of the time, Pallas kernels for 25%

profile of v2, /device:TPU:0, one launch (start us, length us, event | category | flops | bytes accessed | tf_op | source)
XLA Modules:
  0.0 211.2 jit_solution(10084022647070542055)
XLA Ops:
  0.7 3.0 %collective-permute-start.6 = (bf16[256,128]{1,0:T(8,128)(2,1)}, bf16[256,128]{1,0:T(8,128)(2,1)S(1)}, u32[]{:S(2)}, u32[]{:S(2)}) collective-permute-start(bf16[256,128]{1,0:T(8,128)(2,1)} %refs_3_.10), channel_id=1, source_target_pairs={{0,16},{8,24},{16,0},{24,8},{1,17},{9,25},{17,1},{25,9},{2,18},{10... | collective-permute-start | bytes 196616 | tf_op jit(solution)/shard_map/ppermute | solution.py:1035
  17.3 8.5 %taps.1.refs_5_ = f32[128,128]{1,0:T(8,128)S(1)} custom-call(s32[3]{0:T(128)S(1)} %pad_add_fusion.refs_0_, f32[128,512]{1,0:T(8,128)S(1)} %copy-done.5, f32[128,512]{1,0:T(8,128)S(1)} %copy-done.6, f32[128]{0:T(128)S(1)} %copy-done.18, f32[128,512]{1,0:T(8,128)S(1)} %copy-done.7, f32[128,512]{1,0:T(8,128)S(1)} %copy-done.8), custom_call_target="tpu_custom_call" | custom-call | flops 2700000000 | bytes 900000 | tf_op jit(solution)/shard_map/taps/pallas_call | solution.py:33
  27.2 3.6 %forward_mix.1.refs_3_.refs_6_.refs_4_ = bf16[512,128]{1,0:T(8,128)(2,1)S(1)} custom-call(s32[3]{0:T(128)S(1)} %pad_add_fusion.refs_0_, s32[1,512]{1,0:T(1,128)S(1)} %copy-done.16, s32[1,512]{1,0:T(1,128)S(1)} %collective-permute-done.3.refs_2_.refs_4_, s32[1,512]{1,0:T(1,128)S(1)} %copy-done.16, s32[1,512]{1,0:T(1,128)S(1)} %collective-permute-done.3.refs_2_.refs_4_, ...), custom_call_target="tpu_custom_call" | custom-call | flops 1500000000 | bytes 500000 | tf_op jit(solution)/shard_map/forward_mix/pallas_call | solution.py:33
  37.5 5.5 %collective-permute-done.11.refs_0_.refs_8_.refs_6_ = bf16[512,128]{1,0:T(8,128)(2,1)S(1)} collective-permute-done((bf16[512,128]{1,0:T(8,128)(2,1)S(1)}, bf16[512,128]{1,0:T(8,128)(2,1)S(1)}, u32[]{:S(2)}, u32[]{:S(2)}) %collective-permute-start.11) | collective-permute-done | bytes 131104 | tf_op jit(solution)/shard_map/ppermute | solution.py:121
  48.3 3.8 %expand.1 = (bf16[512,768]{1,0:T(8,128)(2,1)S(1)}, bf16[512,768]{1,0:T(8,128)(2,1)S(1)}, f32[128,1024]{1,0:T(8,128)S(1)}, bf16[128,1024]{1,0:T(8,128)(2,1)S(1)},...) custom-call(s32[3]{0:T(128)S(1)} %pad_add_fusion.refs_0_, ...), custom_call_target="tpu_custom_call" | custom-call | flops 1200000000 | bytes 400000 | tf_op jit(solution)/shard_map/expand/pallas_call | solution.py:33
  54.2 7.2 %collective-permute-done.13.refs_2_ = bf16[128,1024]{1,0:T(8,128)(2,1)S(1)} collective-permute-done((bf16[128,1024]{1,0:T(8,128)(2,1)S(1)}, bf16[128,1024]{1,0:T(8,128)(2,1)S(1)}, u32[]{:S(2)}, u32[]{:S(2)}) %collective-permute-start.13) | collective-permute-done | bytes 262176 | tf_op jit(solution)/shard_map/ppermute | solution.py:131
  61.4 3.5 %collective-permute-done.14.refs_1_ = bf16[128,1024]{1,0:T(8,128)(2,1)S(1)} collective-permute-done((bf16[128,1024]{1,0:T(8,128)(2,1)S(1)}, bf16[128,1024]{1,0:T(8,128)(2,1)S(1)}, u32[]{:S(2)}, u32[]{:S(2)}) %collective-permute-start.14) | collective-permute-done | bytes 262176 | tf_op jit(solution)/shard_map/ppermute | solution.py:130
  65.1 3.2 %collective-permute-start.15 = (bf16[128,1024]{1,0:T(8,128)(2,1)S(1)}, bf16[128,1024]{1,0:T(8,128)(2,1)S(1)}, u32[]{:S(2)}, u32[]{:S(2)}) collective-permute-start(bf16[128,1024]{1,0:T(8,128)(2,1)S(1)} %joined.3), channel_id=1, source_target_pairs={{0,2},{1,3},{2,0},{3,1},{4,6},{5,7},{6,4},{7,5},{8,10},{9,11},{10,... | collective-permute-start | bytes 786440 | tf_op jit(solution)/shard_map/ppermute | solution.py:135
  68.2 10.7 %collective-permute-done.15 = bf16[128,1024]{1,0:T(8,128)(2,1)S(1)} collective-permute-done((bf16[128,1024]{1,0:T(8,128)(2,1)S(1)}, bf16[128,1024]{1,0:T(8,128)(2,1)S(1)}, u32[]{:S(2)}, u32[]{:S(2)}) %collective-permute-start.15) | collective-permute-done | bytes 262176 | tf_op jit(solution)/shard_map/ppermute | solution.py:135
  79.1 3.7 %collective-permute-start.16 = (bf16[128,1024]{1,0:T(8,128)(2,1)S(1)}, bf16[128,1024]{1,0:T(8,128)(2,1)S(1)}, u32[]{:S(2)}, u32[]{:S(2)}) collective-permute-start(bf16[128,1024]{1,0:T(8,128)(2,1)S(1)} %add_convert_fusion.refs_9_), channel_id=1, source_target_pairs={{0,1},{1,0},{2,3},{3,2},{4,5},{5,4},{6,7},{7,6},{8,9},{9,8},{10,11... | collective-permute-start | bytes 786440 | tf_op jit(solution)/shard_map/ppermute | solution.py:120
  82.8 10.5 %collective-permute-done.17.refs_0_.refs_11_ = bf16[128,1024]{1,0:T(8,128)(2,1)S(1)} collective-permute-done((bf16[128,1024]{1,0:T(8,128)(2,1)S(1)}, bf16[128,1024]{1,0:T(8,128)(2,1)S(1)}, u32[]{:S(2)}, u32[]{:S(2)}) %collective-permute-start.17) | collective-permute-done | bytes 262176 | tf_op jit(solution)/shard_map/ppermute | solution.py:121
  93.5 7.3 %collective-permute-done.18.refs_12_ = bf16[128,1024]{1,0:T(8,128)(2,1)S(1)} collective-permute-done((bf16[128,1024]{1,0:T(8,128)(2,1)S(1)}, bf16[128,1024]{1,0:T(8,128)(2,1)S(1)}, u32[]{:S(2)}, u32[]{:S(2)}) %collective-permute-start.18) | collective-permute-done | bytes 262176 | tf_op jit(solution)/shard_map/ppermute | solution.py:123
  100.9 4.4 %loss.1 = (bf16[512,1024]{1,0:T(8,128)(2,1)}, bf16[512,1024]{1,0:T(8,128)(2,1)S(1)}, f32[128,1024]{1,0:T(8,128)S(1)}, bf16[512,768]{1,0:T(8,128)(2,1)S(1)}, bf16...) custom-call(s32[3]{0:T(128)S(1)} %pad_add_fusion.refs_0_, ...), custom_call_target="tpu_custom_call" | custom-call | flops 2400000000 | bytes 800000 | tf_op jit(solution)/shard_map/loss/pallas_call | solution.py:33
  107.3 3.0 %collective-permute-done.19.refs_2_.refs_1_ = bf16[512,128]{1,0:T(8,128)(2,1)S(1)} collective-permute-done((bf16[512,128]{1,0:T(8,128)(2,1)S(1)}, bf16[512,128]{1,0:T(8,128)(2,1)S(1)}, u32[]{:S(2)}, u32[]{:S(2)}) %collective-permute-start.19) | collective-permute-done | bytes 131104 | tf_op jit(solution)/shard_map/ppermute | solution.py:131
  115.1 4.0 %collective-permute-done.21.refs_2_ = bf16[512,128]{1,0:T(8,128)(2,1)S(1)} collective-permute-done((bf16[512,128]{1,0:T(8,128)(2,1)S(1)}, bf16[512,128]{1,0:T(8,128)(2,1)S(1)}, u32[]{:S(2)}, u32[]{:S(2)}) %collective-permute-start.21) | collective-permute-done | bytes 131104 | tf_op jit(solution)/shard_map/ppermute | solution.py:135
  122.4 4.7 %backward_mix.1 = (bf16[512,128]{1,0:T(8,128)(2,1)S(1)}, f32[1,128]{1,0:T(1,128)S(1)}, f32[128,1024]{1,0:T(8,128)S(1)}, bf16[128,1024]{1,0:T(8,128)(2,1)S(1)}, b...) custom-call(s32[3]{0:T(128)S(1)} %pad_add_fusion.refs_0_, s32[1,512]{1,0:T(1,128)S(1)} %copy-done.16, ...), custom_call_target="tpu_custom_call" | custom-call | flops 1800000000 | bytes 600000 | tf_op jit(solution)/shard_map/backward_mix/pallas_call | solution.py:33
  129.2 3.6 %taps_back.1 = f32[256,128]{1,0:T(8,128)S(1)} custom-call(s32[3]{0:T(128)S(1)} %pad_add_fusion.refs_0_, s32[1,512]{1,0:T(1,128)S(1)} %copy-done.16, s32[1,512]{1,0:T(1,128)S(1)} %collective-permute-done.3.refs_2_.refs_4_, s32[1,512]{1,0:T(1,128)S(1)} %copy-done.16, s32[1,512]{1,0:T(1,128)S(1)} %collective-permute-done.3.refs_2_.refs_4_, ...), custom_call_target="tpu_custom_call" | custom-call | flops 1800000000 | bytes 600000 | tf_op jit(solution)/shard_map/taps_back/pallas_call | solution.py:33
  136.4 5.0 %collective-permute-done.33.refs_1_ = bf16[128,1024]{1,0:T(8,128)(2,1)S(1)} collective-permute-done((bf16[128,1024]{1,0:T(8,128)(2,1)S(1)}, bf16[128,1024]{1,0:T(8,128)(2,1)S(1)}, u32[]{:S(2)}, u32[]{:S(2)}) %collective-permute-start.33) | collective-permute-done | bytes 262176 | tf_op jit(solution)/shard_map/ppermute | solution.py:130
  150.2 5.7 %collective-permute-done.34.refs_7_ = bf16[128,1024]{1,0:T(8,128)(2,1)S(1)} collective-permute-done((bf16[128,1024]{1,0:T(8,128)(2,1)S(1)}, bf16[128,1024]{1,0:T(8,128)(2,1)S(1)}, u32[]{:S(2)}, u32[]{:S(2)}) %collective-permute-start.34) | collective-permute-done | bytes 262176 | tf_op jit(solution)/shard_map/ppermute | solution.py:135
  157.2 4.1 %collective-permute-done.28 = f32[256,128]{1,0:T(8,128)S(1)} collective-permute-done((f32[256,128]{1,0:T(8,128)S(1)}, f32[256,128]{1,0:T(8,128)S(1)}, u32[]{:S(2)}, u32[]{:S(2)}) %collective-permute-start.28) | collective-permute-done | bytes 131104 | tf_op jit(solution)/shard_map/ppermute | solution.py:90
  162.6 10.1 %collective-permute-done.36.refs_0_.refs_3_ = bf16[144,1024]{1,0:T(8,128)(2,1)S(1)} collective-permute-done((bf16[144,1024]{1,0:T(8,128)(2,1)S(1)}, bf16[144,1024]{1,0:T(8,128)(2,1)S(1)}, u32[]{:S(2)}, u32[]{:S(2)}) %collective-permute-start.36) | collective-permute-done | bytes 294944 | tf_op jit(solution)/shard_map/ppermute | solution.py:121
  173.6 12.9 %modes_back.1.refs_2_ = f32[520,256]{1,0:T(8,128)S(1)} custom-call(s32[3]{0:T(128)S(1)} %pad_add_fusion.refs_0_, f32[256,128]{1,0:T(8,128)S(1)} %add_add_fusion.refs_1_, f32[128,512]{1,0:T(8,128)S(1)} %copy-done.5, f32[128,512]{1,0:T(8,128)S(1)} %copy-done.6, f32[128]{0:T(128)S(1)} %copy-done.18, f32[128,512]{1,0:T(8,128)S(1)} %copy-done.7, ...), custom_call_target="tpu_custom_call" | custom-call | flops 3900000000 | bytes 1300000 | tf_op jit(solution)/shard_map/modes_back/pallas_call | solution.py:33
  191.5 4.4 %collective-permute-done.39 = bf16[128,896]{1,0:T(8,128)(2,1)S(1)} collective-permute-done((bf16[128,896]{1,0:T(8,128)(2,1)S(1)}, bf16[128,896]{1,0:T(8,128)(2,1)S(1)}, u32[]{:S(2)}, u32[]{:S(2)}) %collective-permute-start.39) | collective-permute-done | bytes 229408 | tf_op jit(solution)/shard_map/ppermute | solution.py:990
  196.0 4.4 %collective-permute-done.40 = bf16[128,896]{1,0:T(8,128)(2,1)S(1)} collective-permute-done((bf16[128,896]{1,0:T(8,128)(2,1)S(1)}, bf16[128,896]{1,0:T(8,128)(2,1)S(1)}, u32[]{:S(2)}, u32[]{:S(2)}) %collective-permute-start.40) | collective-permute-done | bytes 229408 | tf_op jit(solution)/shard_map/ppermute | solution.py:990
  (152 shorter events, 72.8 us)
Async XLA Ops:
  0.7 12.9 %collective-permute-start.6 = (bf16[256,128]{1,0:T(8,128)(2,1)}, bf16[256,128]{1,0:T(8,128)(2,1)S(1)}, u32[]{:S(2)}, u32[]{:S(2)}) collective-permute-start(bf16[256,128]{1,0:T(8,128)(2,1)} %refs_3_.10), channel_id=1, source_target_pairs={{0,16},{8,24},{16,0},{24,8},{1,17},{9,25},{17,1},{25,9},{2,18},{10... | collective-permute-start | bytes 196616 | tf_op jit(solution)/shard_map/ppermute | solution.py:1035
  9.0 21.8 %collective-permute-start.2 = (bf16[320,768]{1,0:T(8,128)(2,1)S(1)}, bf16[320,768]{1,0:T(8,128)(2,1)S(1)}, u32[]{:S(2)}, u32[]{:S(2)}) collective-permute-start(bf16[320,768]{1,0:T(8,128)(2,1)S(1)} %get-tuple-element.84.refs_1_), channel_id=1, source_target_pairs={{0,24},{8,16},{16,8},{24,0},{1,25},{9,17},{17,9},{25,1},{2,26},{10... | collective-permute-start | bytes 1474568 | tf_op jit(solution)/shard_map/ppermute | solution.py:1042
  11.9 21.0 %collective-permute-start.1 = (bf16[320,768]{1,0:T(8,128)(2,1)S(1)}, bf16[320,768]{1,0:T(8,128)(2,1)S(1)}, u32[]{:S(2)}, u32[]{:S(2)}) collective-permute-start(bf16[320,768]{1,0:T(8,128)(2,1)S(1)} %get-tuple-element.84.refs_1_), channel_id=1, source_target_pairs={{0,16},{8,24},{16,0},{24,8},{1,17},{9,25},{17,1},{25,9},{2,18},{10... | collective-permute-start | bytes 1474568 | tf_op jit(solution)/shard_map/ppermute | solution.py:1042
  13.6 19.6 %collective-permute-start = (bf16[320,768]{1,0:T(8,128)(2,1)S(1)}, bf16[320,768]{1,0:T(8,128)(2,1)S(1)}, u32[]{:S(2)}, u32[]{:S(2)}) collective-permute-start(bf16[320,768]{1,0:T(8,128)(2,1)S(1)} %get-tuple-element.84.refs_1_), channel_id=1, source_target_pairs={{0,8},{8,0},{16,24},{24,16},{1,9},{9,1},{17,25},{25,17},{2,10},{10... | collective-permute-start | bytes 1474568 | tf_op jit(solution)/shard_map/ppermute | solution.py:1042
  13.8 12.1 %collective-permute-start.3 = (s32[1,512]{1,0:T(1,128)S(1)}, s32[1,512]{1,0:T(1,128)S(1)}, u32[]{:S(2)}, u32[]{:S(2)}) collective-permute-start(s32[1,512]{1,0:T(1,128)S(1)} %copy-done.16), channel_id=1, source_target_pairs={{0,4},{4,0},{1,5},{5,1},{2,6},{6,2},{3,7},{7,3},{8,12},{12,8},{9,1... | collective-permute-start | bytes 6152 | tf_op jit(solution)/shard_map/ppermute | solution.py:84
  14.9 12.3 %collective-permute-start.8 = (f32[256,128]{1,0:T(8,128)S(1)}, f32[256,128]{1,0:T(8,128)S(1)}, u32[]{:S(2)}, u32[]{:S(2)}) collective-permute-start(f32[256,128]{1,0:T(8,128)S(1)} %get-tuple-element.86.refs_9_.refs_7_), channel_id=1, source_target_pairs={{0,4},{1,5},{2,6},{3,7},{8,12},{9,13},{10,14},{11,15},{16,20},{17,... | collective-permute-start | bytes 393224 | tf_op jit(solution)/shard_map/ppermute | solution.py:1068
  33.2 11.5 %collective-permute-start.9 = (bf16[3,320,768]{2,1,0:T(8,128)(2,1)S(1)}, bf16[3,320,768]{2,1,0:T(8,128)(2,1)S(1)}, u32[]{:S(2)}, u32[]{:S(2)}) collective-permute-start(bf16[3,320,768]{2,1,0:T(8,128)(2,1)S(1)} %stack.17.refs_3_), channel_id=1, source_target_pairs={{0,4},{4,0},{1,5},{5,1},{2,6},{6,2},{3,7},{7,3},{8,12},{12,8},{9,1... | collective-permute-start | bytes 4423688 | tf_op jit(solution)/shard_map/ppermute | solution.py:84
  65.1 13.9 %collective-permute-start.15 = (bf16[128,1024]{1,0:T(8,128)(2,1)S(1)}, bf16[128,1024]{1,0:T(8,128)(2,1)S(1)}, u32[]{:S(2)}, u32[]{:S(2)}) collective-permute-start(bf16[128,1024]{1,0:T(8,128)(2,1)S(1)} %joined.3), channel_id=1, source_target_pairs={{0,2},{1,3},{2,0},{3,1},{4,6},{5,7},{6,4},{7,5},{8,10},{9,11},{10,... | collective-permute-start | bytes 786440 | tf_op jit(solution)/shard_map/ppermute | solution.py:135
  79.0 14.3 %collective-permute-start.17 = (bf16[128,1024]{1,0:T(8,128)(2,1)S(1)}, bf16[128,1024]{1,0:T(8,128)(2,1)S(1)}, u32[]{:S(2)}, u32[]{:S(2)}) collective-permute-start(bf16[128,1024]{1,0:T(8,128)(2,1)S(1)} %add_convert_fusion.refs_9_), channel_id=1, source_target_pairs={{0,2},{1,3},{2,0},{3,1},{4,6},{5,7},{6,4},{7,5},{8,10},{9,11},{10,... | collective-permute-start | bytes 786440 | tf_op jit(solution)/shard_map/ppermute | solution.py:121
  79.1 14.3 %collective-permute-start.16 = (bf16[128,1024]{1,0:T(8,128)(2,1)S(1)}, bf16[128,1024]{1,0:T(8,128)(2,1)S(1)}, u32[]{:S(2)}, u32[]{:S(2)}) collective-permute-start(bf16[128,1024]{1,0:T(8,128)(2,1)S(1)} %add_convert_fusion.refs_9_), channel_id=1, source_target_pairs={{0,1},{1,0},{2,3},{3,2},{4,5},{5,4},{6,7},{7,6},{8,9},{9,8},{10,11... | collective-permute-start | bytes 786440 | tf_op jit(solution)/shard_map/ppermute | solution.py:120
  115.0 46.4 %collective-permute-start.43 = (bf16[4,192,768]{2,1,0:T(8,128)(2,1)S(1)}, bf16[4,192,768]{2,1,0:T(8,128)(2,1)S(1)}, u32[]{:S(2)}, u32[]{:S(2)}) collective-permute-start(bf16[4,192,768]{2,1,0:T(8,128)(2,1)S(1)} %get-tuple-element.141), channel_id=1, source_target_pairs={{0,4},{4,0},{1,5},{5,1},{2,6},{6,2},{3,7},{7,3},{8,12},{12,8},{9,1... | collective-permute-start | bytes 3538952 | tf_op jit(solution)/shard_map/ppermute | solution.py:84
  127.2 14.3 %collective-permute-start.33 = (bf16[128,1024]{1,0:T(8,128)(2,1)S(1)}, bf16[128,1024]{1,0:T(8,128)(2,1)S(1)}, u32[]{:S(2)}, u32[]{:S(2)}) collective-permute-start(bf16[128,1024]{1,0:T(8,128)(2,1)S(1)} %get-tuple-element.111.refs_5_), channel_id=1, source_target_pairs={{0,1},{1,0},{2,3},{3,2},{4,5},{5,4},{6,7},{7,6},{8,9},{9,8},{10,11... | collective-permute-start | bytes 786440 | tf_op jit(solution)/shard_map/ppermute | solution.py:130
  141.5 14.4 %collective-permute-start.34 = (bf16[128,1024]{1,0:T(8,128)(2,1)S(1)}, bf16[128,1024]{1,0:T(8,128)(2,1)S(1)}, u32[]{:S(2)}, u32[]{:S(2)}) collective-permute-start(bf16[128,1024]{1,0:T(8,128)(2,1)S(1)} %joined.5), channel_id=1, source_target_pairs={{0,2},{1,3},{2,0},{3,1},{4,6},{5,7},{6,4},{7,5},{8,10},{9,11},{10,... | collective-permute-start | bytes 786440 | tf_op jit(solution)/shard_map/ppermute | solution.py:135
  150.2 36.5 %collective-permute-start.38 = (bf16[4,128,896]{2,1,0:T(8,128)(2,1)S(1)}, bf16[4,128,896]{2,1,0:T(8,128)(2,1)S(1)}, u32[]{:S(2)}, u32[]{:S(2)}) collective-permute-start(bf16[4,128,896]{2,1,0:T(8,128)(2,1)S(1)} %get-tuple-element.123), channel_id=1, source_target_pairs={{0,4},{4,0},{1,5},{5,1},{2,6},{6,2},{3,7},{7,3},{8,12},{12,8},{9,1... | collective-permute-start | bytes 2752520 | tf_op jit(solution)/shard_map/ppermute | solution.py:84
  157.2 15.6 %collective-permute-start.36 = (bf16[144,1024]{1,0:T(8,128)(2,1)S(1)}, bf16[144,1024]{1,0:T(8,128)(2,1)S(1)}, u32[]{:S(2)}, u32[]{:S(2)}) collective-permute-start(bf16[144,1024]{1,0:T(8,128)(2,1)S(1)} %rows.1.refs_1_), channel_id=1, source_target_pairs={{0,2},{1,3},{2,0},{3,1},{4,6},{5,7},{6,4},{7,5},{8,10},{9,11},{10,... | collective-permute-start | bytes 884744 | tf_op jit(solution)/shard_map/ppermute | solution.py:121
  161.4 25.2 %collective-permute-start.35 = (bf16[144,1024]{1,0:T(8,128)(2,1)S(1)}, bf16[144,1024]{1,0:T(8,128)(2,1)S(1)}, u32[]{:S(2)}, u32[]{:S(2)}) collective-permute-start(bf16[144,1024]{1,0:T(8,128)(2,1)S(1)} %rows.1.refs_1_), channel_id=1, source_target_pairs={{0,1},{1,0},{2,3},{3,2},{4,5},{5,4},{6,7},{7,6},{8,9},{9,8},{10,11... | collective-permute-start | bytes 884744 | tf_op jit(solution)/shard_map/ppermute | solution.py:120
  162.2 25.3 %collective-permute-start.44 = (bf16[192,768]{1,0:T(8,128)(2,1)S(1)}, bf16[192,768]{1,0:T(8,128)(2,1)S(1)}, u32[]{:S(2)}, u32[]{:S(2)}) collective-permute-start(bf16[192,768]{1,0:T(8,128)(2,1)S(1)} %get-tuple-element.143), channel_id=1, source_target_pairs={{0,8},{8,0},{16,24},{24,16},{1,9},{9,1},{17,25},{25,17},{2,10},{10... | collective-permute-start | bytes 884744 | tf_op jit(solution)/shard_map/ppermute | solution.py:990
  162.6 25.8 %collective-permute-start.45 = (bf16[192,768]{1,0:T(8,128)(2,1)S(1)}, bf16[192,768]{1,0:T(8,128)(2,1)S(1)}, u32[]{:S(2)}, u32[]{:S(2)}) collective-permute-start(bf16[192,768]{1,0:T(8,128)(2,1)S(1)} %get-tuple-element.144), channel_id=1, source_target_pairs={{0,16},{8,24},{16,0},{24,8},{1,17},{9,25},{17,1},{25,9},{2,18},{10... | collective-permute-start | bytes 884744 | tf_op jit(solution)/shard_map/ppermute | solution.py:990
  172.7 17.4 %collective-permute-start.46 = (bf16[192,768]{1,0:T(8,128)(2,1)S(1)}, bf16[192,768]{1,0:T(8,128)(2,1)S(1)}, u32[]{:S(2)}, u32[]{:S(2)}) collective-permute-start(bf16[192,768]{1,0:T(8,128)(2,1)S(1)} %get-tuple-element.145), channel_id=1, source_target_pairs={{0,24},{8,16},{16,8},{24,0},{1,25},{9,17},{17,9},{25,1},{2,26},{10... | collective-permute-start | bytes 884744 | tf_op jit(solution)/shard_map/ppermute | solution.py:990
  186.6 15.8 %collective-permute-start.31 = (f32[520,256]{1,0:T(8,128)S(1)}, f32[520,256]{1,0:T(8,128)S(1)}, u32[]{:S(2)}, u32[]{:S(2)}) collective-permute-start(f32[520,256]{1,0:T(8,128)S(1)} %modes_back.1.refs_2_), channel_id=1, source_target_pairs={{0,4},{4,0},{1,5},{5,1},{2,6},{6,2},{3,7},{7,3},{8,12},{12,8},{9,1... | collective-permute-start | bytes 1597448 | tf_op jit(solution)/shard_map/ppermute | solution.py:84
  186.7 18.5 %collective-permute-start.37 = (bf16[144,1024]{1,0:T(8,128)(2,1)S(1)}, bf16[144,1024]{1,0:T(8,128)(2,1)}, u32[]{:S(2)}, u32[]{:S(2)}) collective-permute-start(bf16[144,1024]{1,0:T(8,128)(2,1)S(1)} %again.5), channel_id=1, source_target_pairs={{0,1},{1,0},{2,3},{3,2},{4,5},{5,4},{6,7},{7,6},{8,9},{9,8},{10,11... | collective-permute-start | bytes 884744 | tf_op jit(solution)/shard_map/ppermute | solution.py:123
  188.4 12.0 %collective-permute-start.40 = (bf16[128,896]{1,0:T(8,128)(2,1)S(1)}, bf16[128,896]{1,0:T(8,128)(2,1)S(1)}, u32[]{:S(2)}, u32[]{:S(2)}) collective-permute-start(bf16[128,896]{1,0:T(8,128)(2,1)S(1)} %get-tuple-element.126), channel_id=1, source_target_pairs={{0,16},{8,24},{16,0},{24,8},{1,17},{9,25},{17,1},{25,9},{2,18},{10... | collective-permute-start | bytes 688136 | tf_op jit(solution)/shard_map/ppermute | solution.py:990
  190.1 12.1 %collective-permute-start.41 = (bf16[128,896]{1,0:T(8,128)(2,1)S(1)}, bf16[128,896]{1,0:T(8,128)(2,1)S(1)}, u32[]{:S(2)}, u32[]{:S(2)}) collective-permute-start(bf16[128,896]{1,0:T(8,128)(2,1)S(1)} %get-tuple-element.127), channel_id=1, source_target_pairs={{0,24},{8,16},{16,8},{24,0},{1,25},{9,17},{17,9},{25,1},{2,26},{10... | collective-permute-start | bytes 688136 | tf_op jit(solution)/shard_map/ppermute | solution.py:990
  196.0 13.5 %collective-permute-start.47 = (f32[192,768]{1,0:T(8,128)S(1)}, f32[192,768]{1,0:T(8,128)S(1)}, u32[]{:S(2)}, u32[]{:S(2)}) collective-permute-start(f32[192,768]{1,0:T(8,128)S(1)} %convert_add_fusion.refs_1_), channel_id=1, source_target_pairs={{0,4},{4,0},{1,5},{5,1},{2,6},{6,2},{3,7},{7,3},{8,12},{12,8},{9,1... | collective-permute-start | bytes 1769480 | tf_op jit(solution)/shard_map/ppermute | solution.py:84
  (43 other events, 337.8 us)

commit v3 on v2

--- a/solution.py
+++ b/solution.py
@@ -10,7 +10,7 @@
 
 REACH = 256
 EPSILON = 1e-05
-EARLY, PAIR, LATE, TAPS_BACK, MODES_BACK, TAPS = 0.2,0.2,1,6,13,9
+EARLY, PAIR, LATE, TAPS_BACK, MODES_BACK, TAPS = 2, 1, 2, 4, 4, 9
 GELU_SCALE = 0.7978845608028654
 F32 = jnp.float32
 BF16 = jnp.bfloat16
@@ -42,7 +42,7 @@
         ],
         compiler_params=pltpu.CompilerParams(vmem_limit_bytes=room + room // 16 + (3 << 20)),
         cost_estimate=pl.CostEstimate(
-            flops=int(micros * 0.3e9), bytes_accessed=int(micros * 1e5), transcendentals=0
+            flops=int(micros * 0.2e9), bytes_accessed=int(micros * 1e5), transcendentals=0
         ),
         name=name,
     )(*args, *ties)
@@ -102,8 +102,9 @@
     out_ref[...] = x_ref[...]
 
 
-def add_kernel(x_ref, y_ref, out_ref):
-    out_ref[...] = (x_ref[...].astype(F32) + y_ref[...].astype(F32)).astype(out_ref.dtype)
+def add_kernel(x_ref, y_ref, z_ref, sum_ref, copy_ref):
+    sum_ref[...] = (x_ref[...].astype(F32) + y_ref[...].astype(F32)).astype(BF16)
+    copy_ref[...] = z_ref[...]
 
 
 def toward(place, k, size):
@@ -114,12 +115,75 @@
     return place[2] ^ k if size == 4 else lax.rem(place[2] + size - k, size)
 
 
-def spread_tensor(x):
+def tensor_pairs(size, k):
+    return xor_pairs(size, k) if size == 4 else shift_pairs(size, k)
+
+
+def exchange_tensor(pieces):
+    size = lax.axis_size("tensor")
+    return [lax.ppermute(x, "tensor", tensor_pairs(size, k + 1)) for k, x in enumerate(pieces)]
+
+
+def stage_kernel(x_ref, y_ref, z_ref, w_ref, sum_ref, copy_ref, next_ref):
+    sum_ref[...] = (x_ref[...].astype(F32) + y_ref[...].astype(F32)).astype(BF16)
+    copy_ref[...] = z_ref[...]
+    next_ref[...] = w_ref[...]
+
+
+def sum_tensor(owns, sends):
+    size = lax.axis_size("tensor")
+    if size != 4:
+        found = []
+        for own, pieces in zip(owns, sends):
+            for got in exchange_tensor(pieces):
+                own = own + got.astype(F32)
+            own = own.astype(BF16)
+            found.append([own] + exchange_tensor([own] * (size - 1)))
+        return found
+    near_pairs, far_pairs = xor_pairs(4, 1), xor_pairs(4, 2)
+
+    def stage(pieces, passed, after):
+        return call(
+            stage_kernel,
+            "stage",
+            [(passed.shape, BF16)] * 3,
+            (pieces[1], passed, pieces[0], after),
+            scalars=0,
+            micros=0.5,
+        )
+
+    first, second = sends
+    passed = lax.ppermute(first[2], "tensor", near_pairs)
+    joined, near, after = stage(first, passed, second[2])
+    first_far = lax.ppermute(joined, "tensor", far_pairs)
+    passed = lax.ppermute(after, "tensor", near_pairs)
+    first_near = lax.ppermute(near, "tensor", near_pairs)
+    joined, near, _ = stage(second, passed, second[0])
+    second_far = lax.ppermute(joined, "tensor", far_pairs)
+    second_near = lax.ppermute(near, "tensor", near_pairs)
+    found = []
+    for own, far, near in ((owns[0], first_far, first_near), (owns[1], second_far, second_near)):
+        total = (own + (far.astype(F32) + near.astype(F32))).astype(BF16)
+        away = lax.ppermute(total, "tensor", far_pairs)
+        beside = lax.ppermute(total, "tensor", near_pairs)
+        found.append([total, beside, away, lax.ppermute(away, "tensor", near_pairs)])
+    return found
+
+
+def spread_tensor(x, ties=()):
     size = lax.axis_size("tensor")
     if size == 4:
         near = lax.ppermute(x, "tensor", xor_pairs(4, 1))
         far = lax.ppermute(x, "tensor", xor_pairs(4, 2))
-        (again,) = call(copy_kernel, "again", [(x.shape, x.dtype)], (far,), scalars=0, micros=0.5, ties=(near,))
+        (again,) = call(
+            copy_kernel,
+            "again",
+            [(x.shape, x.dtype)],
+            (far,),
+            scalars=0,
+            micros=0.5,
+            ties=(near,) + ties,
+        )
         return [near, far, lax.ppermute(again, "tensor", xor_pairs(4, 1))]
     return [lax.ppermute(x, "tensor", shift_pairs(size, k)) for k in range(1, size)]
 
@@ -128,12 +192,21 @@
     size = lax.axis_size("tensor")
     if size == 4:
         passed = lax.ppermute(pieces[2], "tensor", xor_pairs(4, 1))
-        near = lax.ppermute(pieces[0], "tensor", xor_pairs(4, 1))
-        (joined,) = call(
-            add_kernel, "joined", [(passed.shape, BF16)], (pieces[1], passed), scalars=0, micros=0.5, ties=(near,)
+        joined, near = call(
+            add_kernel,
+            "joined",
+            [(passed.shape, BF16)] * 2,
+            (pieces[1], passed, pieces[0]),
+            scalars=0,
+            micros=0.5,
         )
-        return [near, lax.ppermute(joined, "tensor", xor_pairs(4, 2))]
-    return [lax.ppermute(x, "tensor", shift_pairs(size, k + 1)) for k, x in enumerate(pieces)]
+        found = [
+            lax.ppermute(near, "tensor", xor_pairs(4, 1)),
+            lax.ppermute(joined, "tensor", xor_pairs(4, 2)),
+        ]
+        return found, joined
+    found = [lax.ppermute(x, "tensor", shift_pairs(size, k + 1)) for k, x in enumerate(pieces)]
+    return found, found[0]
 
 
 def cmul(ar, ai, br, bi):
@@ -194,7 +267,7 @@
                 acc[pl.ds(start + 8 * j, 8), :] += term[:8] + term[8:]
             return cmul(wr, wi, *eight)
 
-        lax.fori_loop(0, lags // 8, outer, (wr_s[rows, :], wi_s[rows, :]), unroll=2)
+        lax.fori_loop(0, lags // 8, outer, (wr_s[rows, :], wi_s[rows, :]), unroll=4)
         return carry
 
     lax.fori_loop(0, ar_s.shape[0] // 16, pair, 0)
@@ -507,10 +580,11 @@
     out_ref[...] = total
 
 
-def gain_kernel(place, x_ref, own_ref, *rest, vectors):
+def gain_kernel(place, taps_ref, x_ref, own_ref, *rest, vectors):
     out_ref = rest[-1]
     sends = rest[: -1 - vectors]
-    start = 0
+    start = taps_ref.shape[0]
+    out_ref[0:start, :] = taps_ref[...]
     for ref in rest[-1 - vectors : -1]:
         start = put_row(out_ref, start, ref[...])
     size = len(sends) + 1
@@ -523,7 +597,7 @@
 
         def rows_step(i, state, source=source, k=k):
             gain, bias = state
-            unit, _ = unit_rows(x_ref[at(height * toward(place, k, size) + step * i, step), :])
+            unit = x_ref[at(height * toward(place, k, size) + step * i, step), :].astype(F32)
             part = source[at(step * i, step), :].astype(F32)
             scaled = part * unit
             for j in range(0, step, 8):
@@ -536,15 +610,15 @@
     put_row(out_ref, start, jnp.sum(bias, axis=0, keepdims=True))
 
 
-def gain_sums(place, channels, rows, own, sends, vectors, ties):
-    count = (sum(v.shape[1] for v in vectors) + 2 * rows.shape[1]) // channels
+def gain_sums(place, taps, rows, own, sends, vectors):
+    count, channels = taps.shape
+    count += (sum(v.shape[1] for v in vectors) + 2 * rows.shape[1]) // channels
     return call(
         partial(gain_kernel, vectors=len(vectors)),
         "gain",
         [((count, channels), F32)],
-        (place, rows, own, *sends, *vectors),
-        micros=0.2,
-        ties=ties,
+        (place, taps, rows, own, *sends, *vectors),
+        micros=2,
     )[0]
 
 
@@ -617,7 +691,7 @@
 
         one_ = jnp.ones((8, channels), F32)
         _, _, gr, gi, hr, hi = lax.fori_loop(
-            0, REACH // 16, outer, (one_, zero, zero, zero, zero, zero), unroll=2
+            0, REACH // 16, outer, (one_, zero, zero, zero, zero, zero), unroll=4
         )
         gr_s[rows, :] = gr
         gi_s[rows, :] = gi
@@ -646,7 +720,7 @@
     )
 
 
-def modes_back(place, c, damping, frequency, timestep, mix_real, mix_imaginary):
+def modes_back(place, c, damping, frequency, timestep, mix_real, mix_imaginary, ties):
     channels, count = damping.shape
     count = count // 2
     return call(
@@ -656,6 +730,7 @@
         (place, c, damping, frequency, timestep, mix_real, mix_imaginary),
         scratch=[((count, channels), F32)] * 6 + [((REACH * 8, channels), F32)] * 2,
         micros=MODES_BACK,
+        ties=ties,
     )[0]
 
 
@@ -666,11 +741,12 @@
     return shifted * inverse, inverse
 
 
-def norm_kernel(x_ref, gain_ref, bias_ref, out_ref):
+def norm_kernel(x_ref, gain_ref, bias_ref, out_ref, unit_ref):
     def step(i, carry):
         rows = at(128 * i, 128)
         unit, _ = unit_rows(x_ref[rows, :])
         out_ref[rows, :] = (unit * gain_ref[...][None, :] + bias_ref[...][None, :]).astype(BF16)
+        unit_ref[rows, :] = unit.astype(BF16)
         return carry
 
     lax.fori_loop(0, x_ref.shape[0] // 128, step, 0)
@@ -748,31 +824,56 @@
         store(rests, mines)
 
 
-def expand_kernel(place, act_ref, slope_ref, we_ref, b_ref, wo_ref, *rest, size):
-    pieces, rest = rest[:size], rest[size:]
-    gated_ref, coef_ref, own_ref, *sends = rest
-    height = own_ref.shape[0]
+def expand_rows(place, k, refs, pieces, size):
+    act_ref, slope_ref, we_ref, b_ref, wo_ref = refs
+    height = pieces[0].shape[0] // size
     channels = pieces[0].shape[1]
-    for k in range(size):
-        rows = at(height * toward(place, k, size), height)
-        expanded = b_ref[...][None, :]
-        for j in range(size):
-            source = origin(place, j, size)
-            expanded = expanded + dot(pieces[j][rows, :], we_ref[at(channels * source, channels), :])
-        coef_ref[rows, :] = (slope_ref[rows, :].astype(F32) * expanded).astype(BF16)
-        gated = (expanded * act_ref[rows, :].astype(F32)).astype(BF16)
+    rows = at(height * toward(place, k, size), height)
+    expanded = b_ref[...][None, :]
+    for j in range(size):
+        source = origin(place, j, size)
+        expanded = expanded + dot(pieces[j][rows, :], we_ref[at(channels * source, channels), :])
+    coef = (slope_ref[rows, :].astype(F32) * expanded).astype(BF16)
+    gated = (expanded * act_ref[rows, :].astype(F32)).astype(BF16)
+    half = wo_ref.shape[0] // 2
+    return rows, gated, coef, [dot_t(gated, wo_ref[half * h : half * (h + 1), :]) for h in range(2)]
+
+
+def expand_first_kernel(place, *rest, size):
+    refs, pieces, (gated_ref, coef_ref, *sends) = rest[:5], rest[5 : 5 + size], rest[5 + size :]
+    _, gated_ref[...], coef_ref[...], parts = expand_rows(place, size - 1, refs, pieces, size)
+    for send, part in zip(sends, parts):
+        send[...] = part.astype(BF16)
+
+
+def expand_kernel(place, *rest, size):
+    refs, pieces, rest = rest[:5], rest[5 : 5 + size], rest[5 + size :]
+    last_gated_ref, last_coef_ref, gated_ref, coef_ref, *rest = rest
+    owns, sends = rest[:2], rest[2:]
+    for k in range(size - 1):
+        rows, gated, coef, parts = expand_rows(place, k, refs, pieces, size)
         gated_ref[rows, :] = gated
-        piece = dot_t(gated, wo_ref[...])
-        if k == 0:
-            own_ref[...] = piece
-        else:
-            sends[k - 1][...] = piece.astype(BF16)
+        coef_ref[rows, :] = coef
+        for h, part in enumerate(parts):
+            if k == 0:
+                owns[h][...] = part
+            else:
+                sends[(size - 2) * h + k - 1][...] = part.astype(BF16)
+    height = last_gated_ref.shape[0]
+    rows = at(height * toward(place, size - 1, size), height)
+    gated_ref[rows, :] = last_gated_ref[...]
+    coef_ref[rows, :] = last_coef_ref[...]
+
+
+def halves(x):
+    high = x.astype(BF16).astype(F32)
+    return high, x - high
 
 
 def loss_kernel(
     place, x_ref, t_ref, mask_ref, b_ref, act_ref, coef_ref, wo_ref, we_ref, *rest, size
 ):
-    pieces, rest = rest[:size], rest[size:]
+    pieces, others, rest = rest[:size], rest[size : 2 * size], rest[2 * size :]
     out_ref, back_ref, keep_ref, low_ref, gate_ref, ob_ref, eb_ref, gb_ref, err_ref, own_ref, *rest = rest
     sends, mask_s = rest[:-1], rest[-1]
     height = pieces[0].shape[0]
@@ -784,7 +885,8 @@
     errors = jnp.zeros((1, 1), F32)
     for j in range(size):
         rows = at(height * origin(place, j, size), height)
-        result = x_ref[rows, :].astype(F32) + pieces[j][...].astype(F32) + b_ref[...][None, :]
+        branch = jnp.concatenate([pieces[j][...], others[j][...]], 1).astype(F32)
+        result = x_ref[rows, :].astype(F32) + branch + b_ref[...][None, :]
         out_ref[rows, :] = result.astype(BF16)
         back = (result - t_ref[rows, :].astype(F32)) * mask_s[rows, 0:1]
         low = back.astype(BF16)
@@ -812,10 +914,18 @@
     eb_ref[...] = expb
     gb_ref[...] = gatb
     count = jnp.sum(mask_ref[...].astype(F32), axis=1, keepdims=True)
-    half = err_ref.shape[1] // 2
-    err_ref[...] = jnp.concatenate(
-        [jnp.broadcast_to(errors, (1, half)), jnp.broadcast_to(count, (1, half))], 1
-    )
+    half = err_ref.shape[1] // 4
+    high, low = halves(
+        jnp.concatenate([jnp.broadcast_to(errors, (1, half)), jnp.broadcast_to(count, (1, half))], 1)
+    )
+    err_ref[...] = jnp.concatenate([high, low], 1)
+
+
+def gate_back_kernel(low_ref, w_ref, out_ref):
+    height = 128
+    for i in range(low_ref.shape[0] // height):
+        rows = slice(height * i, height * (i + 1))
+        out_ref[rows, :] = dot_t(low_ref[rows, :], w_ref[...])
 
 
 def sum_kernel(own_ref, *rest):
@@ -830,13 +940,13 @@
 
 def scale_of(total_ref, scale):
     row, tokens_all = scale
-    return tokens_all / total_ref[row : row + 1, 0:1]
+    return tokens_all / (total_ref[row : row + 1, 0:1] + total_ref[row + 2 : row + 3, 0:1])
 
 
 EXTRA = 16
 
 
-def rows_kernel(place, x_ref, gain_ref, keep_ref, total_ref, own_ref, *rest, scale):
+def rows_kernel(place, x_ref, gain_ref, keep_ref, total_ref, own_ref, *rest, scale, norm_at):
     *pieces, out_ref = rest
     height, features = own_ref.shape
     step = 32
@@ -861,7 +971,7 @@
     lax.fori_loop(0, height // step, one, 0, unroll=2)
     width = total_ref.shape[1]
     count = features // width
-    start = total_ref.shape[0] - 2 * count
+    start = norm_at
     both = []
     for v in range(2):
         first = start + count * v
@@ -875,7 +985,7 @@
 
 
 def join_kernel(place, *rest):
-    *pieces, out_ref, norm_ref, parts = rest
+    *pieces, out_ref, gain_ref, bias_ref, parts = rest
     size = len(pieces)
     height = pieces[0].shape[0] - EXTRA
     for k in range(size):
@@ -885,16 +995,18 @@
     total = parts[0]
     for k in range(1, size):
         total = total + parts[k]
-    norm_ref[...] = total
+    gain_ref[...] = total[0:1]
+    bias_ref[...] = total[1:2]
 
 
 def finish_kernel(place, sum_ref, mine_ref, other_ref, *outs, starts, scale):
     dd_ref, df_ref, dmr_ref, dmi_ref, dt_ref, loss_ref, *vectors = outs
     channels, count = dd_ref.shape
     count = count // 2
-    counted = sum_ref[scale[0] : scale[0] + 1, 0:1]
-    loss_ref[...] = sum_ref[scale[0] - 1 : scale[0], 0:1] / (counted * scale[2])
-    scale = scale_of(sum_ref, scale[:2])
+    row, tokens_all, features = scale
+    errors = sum_ref[row - 1 : row, 0:1] + sum_ref[row + 1 : row + 2, 0:1]
+    scale = scale_of(sum_ref, (row, tokens_all))
+    loss_ref[...] = errors * scale * (1.0 / (tokens_all * features))
     for i, out in enumerate((dd_ref, df_ref, dmr_ref, dmi_ref)):
         rows = slice(channels * i, channels * (i + 1))
         out[:, at(count * place[1], count)] = mine_ref[rows, :] * scale
@@ -927,18 +1039,72 @@
         give_ref[k, half:, :] = jnp.where(core == 0, both[some:], both[:some]).astype(BF16)
 
 
-def late_kernel(place, x_ref, gate_ref, reduce_ref, keep_ref, give_ref):
+PACK_ROWS = 80
+
+
+def late_kernel(place, x_ref, gate_ref, reduce_ref, pack_ref, keep_ref, give_ref, pack_s):
     core = place[1]
     half = x_ref.shape[1] // 8
     units = gate_ref.shape[1]
     for s in range(4):
-        k = s
+        lines = slice(half * s, half * (s + 1))
         mine = x_ref[:, at((2 * s + core) * half, half)]
-        keep_ref[k, :, 0:units] = t_dot(mine, gate_ref[...])
-        keep_ref[k, :, units:] = t_dot(mine, reduce_ref[...])
+        keep_ref[lines, 0:units] = t_dot(mine, gate_ref[...])
+        keep_ref[lines, units:] = t_dot(mine, reduce_ref[...])
         other = x_ref[:, at((2 * s + 1 - core) * half, half)]
-        give_ref[k, :, 0:units] = t_dot(other, gate_ref[...]).astype(BF16)
-        give_ref[k, :, units:] = t_dot(other, reduce_ref[...]).astype(BF16)
+        give_ref[lines, 0:units] = t_dot(other, gate_ref[...]).astype(BF16)
+        give_ref[lines, units:] = t_dot(other, reduce_ref[...]).astype(BF16)
+    pack_s[...] = jnp.zeros_like(pack_s)
+    sums = pack_ref.shape[0]
+    high, low = halves(pack_ref[0:REACH, :])
+    pack_s[0:REACH, :] = high
+    pack_s[REACH:sums, :] = pack_ref[REACH:, :]
+    pack_s[sums : sums + REACH, :] = low
+    width = pack_s.shape[1]
+    for b in range(pack_s.shape[0] // PACK_ROWS):
+        part = pack_s[PACK_ROWS * b : PACK_ROWS * (b + 1), :].astype(BF16)
+        lanes = slice(width * b, width * (b + 1))
+        give_ref[4 * half :, lanes] = part
+        keep_ref[4 * half :, lanes] = part.astype(F32)
+
+
+def pack_of(sums, pack_ref):
+    width = pack_ref.shape[1]
+    for b in range(pack_ref.shape[0] // PACK_ROWS):
+        pack_ref[PACK_ROWS * b : PACK_ROWS * (b + 1), :] = sums[:, width * b : width * (b + 1)]
+
+
+def late_pair_kernel(place, keep_ref, got_ref, own_ref, mine_ref, *rest, error_at, sums):
+    *sends, pack_s = rest
+    s = place[0]
+    half = own_ref.shape[0]
+    lines = at(half * s, half)
+    own_ref[...] = keep_ref[lines, :] + got_ref[lines, :].astype(F32)
+    pack_of(keep_ref[4 * half :, :] + got_ref[4 * half :, :].astype(F32), pack_s)
+    high, low = halves(pack_s[error_at : error_at + 2, :] + pack_s[error_at + 2 : error_at + 4, :])
+    pack_s[error_at : error_at + 2, :] = high
+    pack_s[error_at + 2 : error_at + 4, :] = low
+    high, low = halves(pack_s[0:REACH, :] + pack_s[sums : sums + REACH, :])
+    pack_s[0:REACH, :] = high
+    pack_s[sums : sums + REACH, :] = low
+    width = pack_s.shape[1]
+    for b in range(pack_s.shape[0] // PACK_ROWS):
+        part = pack_s[PACK_ROWS * b : PACK_ROWS * (b + 1), :].astype(BF16)
+        mine_ref[:, width * b : width * (b + 1)] = part
+    for k in (1, 2, 3):
+        lines = at(half * (s ^ k), half)
+        sends[k - 1][0:half, :] = (keep_ref[lines, :] + got_ref[lines, :].astype(F32)).astype(BF16)
+        sends[k - 1][half:, :] = mine_ref[...]
+
+
+def late_sum_kernel(own_ref, mine_ref, first_ref, second_ref, third_ref, out_ref, total_ref, *, sums):
+    half = own_ref.shape[0]
+    first, second, third = (ref[...].astype(F32) for ref in (first_ref, second_ref, third_ref))
+    out_ref[...] = (own_ref[...] + first[:half]) + (second[:half] + third[:half])
+    pack_of(
+        (mine_ref[...].astype(F32) + first[half:]) + (second[half:] + third[half:]), total_ref
+    )
+    total_ref[0:REACH, :] += total_ref[sums : sums + REACH, :]
 
 
 def pair_kernel(place, keep_ref, got_ref, own_ref, *sends):
@@ -973,22 +1139,25 @@
     reduce_ref[half:, :] = second[:, units:]
 
 
-def pair_grads(place, keep, give):
-    shape = keep.shape[1:]
-    return call(
-        pair_kernel,
-        "pair",
-        [(shape, F32)] + [(shape, BF16)] * 3,
+def send_late(place, keep, give, channels, error_at, sums, ties):
+    half = (keep.shape[0] - PACK_ROWS) // 4
+    shape = (half, keep.shape[1])
+    sent = (half + PACK_ROWS, keep.shape[1])
+    pack = (PACK_ROWS * (keep.shape[1] // channels), channels)
+    own, mine, *sends = call(
+        partial(late_pair_kernel, error_at=error_at, sums=sums),
+        "pair_late",
+        [(shape, F32), ((PACK_ROWS, keep.shape[1]), BF16)] + [(sent, BF16)] * 3,
         (place, keep, swap_context(give)),
+        scratch=[(pack, F32)],
         micros=PAIR,
-    )
-
-
-def send_grads(pieces):
-    own, *sends = pieces
-    for k in (1, 2, 3):
-        own = own + lax.ppermute(sends[k - 1], "shard", xor_pairs(4, k)).astype(F32)
-    return own, swap_context(own)
+        ties=ties,
+    )
+    got = [lax.ppermute(sends[k - 1], "shard", xor_pairs(4, k)) for k in (1, 2, 3)]
+    own, total = call(
+        partial(late_sum_kernel, sums=sums), "late_sum", [(shape, F32), (pack, F32)], (own, mine, *got), scalars=0, micros=1
+    )
+    return own, swap_context(own), total
 
 
 def plain_grad(grad, scale, axis):
@@ -1034,22 +1203,16 @@
     if fast:
         found = [lax.ppermute(reduce_weight, "shard", xor_pairs(4, k)) for k in (1, 2, 3)]
         reduce_pieces = [reduce_weight] + found
-        some = expand_weight.shape[0] // 2
-        shape = (gate_weight.shape[0] + some, units)
-        mine, rest = call(
-            pack_kernel, "pack", [(shape, BF16)] * 2, (place, gate_weight, expand_weight, output_weight)
-        )
-        nears = [lax.ppermute(mine, "shard", xor_pairs(4, k)) for k in (1, 2, 3)]
     else:
         reduce_pieces = [lax.all_gather(reduce_weight, "shard", axis=0, tiled=True)]
         gate_full = lax.all_gather(gate_weight, "shard", axis=0, tiled=True)
         expand_full = lax.all_gather(expand_weight, "shard", axis=0, tiled=True)
         output_full = lax.all_gather(output_weight.T, "shard", axis=0, tiled=True)
 
-    (normed,) = call(
+    normed, unit = call(
         norm_kernel,
         "norm",
-        [(inputs.shape, BF16)],
+        [(inputs.shape, BF16)] * 2,
         (inputs, norm_gain, norm_bias),
         scalars=0,
     )
@@ -1063,11 +1226,19 @@
         [(half_rows, F32), (half_rows, F32), ((tokens, channels), F32), ((width, channels), BF16)],
         (place, normed, reduce_bias, *reduce_pieces),
     )
+    if fast:
+        some = expand_weight.shape[0] // 2
+        shape = (gate_weight.shape[0] + some, units)
+        mine, rest = call(
+            pack_kernel, "pack", [(shape, BF16)] * 2, (place, gate_weight, expand_weight, output_weight),
+            ties=(u_high,),
+        )
+        nears = [lax.ppermute(mine, "shard", xor_pairs(4, k)) for k in (1, 2, 3)]
     before = [(i, i + 1) for i in range(contexts - 1)]
     after = [(i + 1, i) for i in range(contexts - 1)]
     halo = lax.ppermute(u_high[tokens // 2 - REACH :], "context", before)
     mixed_own = forward_mix(place, ids, taps, halo, u_low, u_high)
-    mixed = [mixed_own] + spread_tensor(mixed_own)
+    mixed = [mixed_own] + exchange_tensor([mixed_own] * (size - 1))
     if fast:
         shape = (3,) + mine.shape
         (near,) = call(stack_kernel, "stack", [(shape, BF16)], nears, scalars=0, ties=(mixed_own,))
@@ -1091,17 +1262,27 @@
         micros=4,
     )
     piece = (height, width)
-    gated, coef, branch_part, *branch_sends = call(
+    half_piece = (height, width // 2)
+    expand_args = (gate_act, gate_slope, expand_full, expand_bias, output_full, *mixed)
+    last_gated, last_coef, *last_sends = call(
+        partial(expand_first_kernel, size=size),
+        "expand_first",
+        [((height, units), BF16)] * 2 + [(half_piece, BF16)] * 2,
+        (place, *expand_args),
+        micros=1,
+    )
+    gated, coef, first_part, second_part, *branch_sends = call(
         partial(expand_kernel, size=size),
         "expand",
-        [((tokens, units), BF16), ((tokens, units), BF16), (piece, F32)] + [(piece, BF16)] * (size - 1),
-        (place, gate_act, gate_slope, expand_full, expand_bias, output_full, *mixed),
-        micros=4,
-    )
-    for got in deliver_tensor(branch_sends):
-        branch_part = branch_part + got.astype(F32)
-    branch_own = branch_part.astype(BF16)
-    branch = [branch_own] + spread_tensor(branch_own)
+        [((tokens, units), BF16)] * 2 + [(half_piece, F32)] * 2 + [(half_piece, BF16)] * (2 * size - 4),
+        (place, *expand_args, last_gated, last_coef),
+        micros=3,
+    )
+    count = size - 2
+    branch = sum_tensor(
+        (first_part, second_part),
+        (branch_sends[:count] + last_sends[:1], branch_sends[count:] + last_sends[1:]),
+    )
 
     output, branch_back, keep_back, expand_low, gate_low, *rest = call(
         partial(loss_kernel, size=size),
@@ -1115,7 +1296,7 @@
             ((1, width), F32),
             ((1, units), F32),
             ((1, units), F32),
-            ((1, 2 * channels), F32),
+            ((1, 4 * channels), F32),
             ((tokens, channels), F32),
         ]
         + [((tokens, channels), BF16)] * (size - 1),
@@ -1129,13 +1310,13 @@
             coef,
             output_full,
             expand_full,
-            *branch,
+            *branch[0],
+            *branch[1],
         ),
         scratch=[((tokens, 128), F32)],
         micros=8,
     )
     output_sum, expand_sum, gate_sum, error_row, back_part, *back_sends = rest
-    back_got = deliver_tensor(back_sends)
     ties = ()
     if fast:
         shape = (4, (gate_weight.shape[0] + expand_weight.shape[0]) // 2, units)
@@ -1146,10 +1327,29 @@
             (place, gated, branch_back, expand_low, *mixed),
             scratch=[((tokens, size * channels), BF16)],
             micros=EARLY,
-            ties=(),
         )
-        early = pair_grads(place, *early)
-        ties = ()
+        early, *early_sends = call(
+            pair_kernel,
+            "pair_early",
+            [(shape[1:], F32)] + [(shape[1:], BF16)] * 3,
+            (place, early[0], swap_context(early[1])),
+            micros=PAIR,
+        )
+        ties = (early,)
+        early_got = [
+            lax.ppermute(early_sends[k - 1], "shard", xor_pairs(4, k)).astype(F32) for k in (1, 2, 3)
+        ]
+        early = (early + early_got[0]) + (early_got[1] + early_got[2])
+    back_got = exchange_tensor(back_sends)
+    (gate_part,) = call(
+        gate_back_kernel,
+        "gate_back",
+        [((tokens, width), F32)],
+        (gate_low, gate_full),
+        scalars=0,
+        micros=1,
+    )
+    ties = ties + (gate_part,)
     g_low, g_high = call(
         sum_kernel,
         "sum",
@@ -1159,38 +1359,51 @@
         ties=ties,
     )
     halo_back = lax.ppermute(g_low[:REACH], "context", after)
-    gate_part = dot_t(gate_low, gate_full)
     reduce_low, reduce_sum, normed_part, *normed_sends = backward_mix(
         place, ids, taps, g_low, g_high, halo_back, reduce_slope, gate_part, reduce_full, size
     )
-    normed_got = deliver_tensor(normed_sends)
+    normed_got, _ = deliver_tensor(normed_sends)
 
     vectors = (gate_sum, expand_sum, output_sum, reduce_sum, error_row)
-    pack = gain_sums(place, channels, inputs, normed_part, normed_sends, vectors, ())
+    taps_part = taps_back(
+        place, ids, halo, u_low, u_high, g_low, g_high, ()
+    )
+    pack = gain_sums(place, taps_part, unit, normed_part, normed_sends, vectors)
     norm_at = pack.shape[0] - 2 * width // channels
-    total = sum_over(sum_over(pack, "context"), "shard")
-    error_at = norm_at - 2
-    taps_grad = taps_back(place, ids, halo, u_low, u_high, g_low, g_high, ())
-    taps_grad = sum_over(sum_over(taps_grad, "context"), "shard")
+    error_at = norm_at - 4
+    if fast:
+        shape = (2 * gate_weight.shape[0] + PACK_ROWS, units + channels)
+        late = call(
+            late_kernel,
+            "late",
+            [(shape, F32), (shape, BF16)],
+            (place, normed, gate_low, reduce_low, pack),
+            ties=(early,),
+            scratch=[((PACK_ROWS * (shape[1] // channels), channels), F32)],
+            micros=LATE,
+        )
+        *late, total = send_late(place, *late, channels, error_at, pack.shape[0], ())
+    else:
+        total = sum_over(sum_over(pack, "context"), "shard")
     tokens_all = float(tokens * shards * contexts)
 
     scale = (error_at + 1, tokens_all)
 
     (rows_own,) = call(
-        partial(rows_kernel, scale=scale),
+        partial(rows_kernel, scale=scale, norm_at=norm_at),
         "rows",
         [((height + EXTRA, width), BF16)],
         (place, inputs, norm_gain, keep_back, total, normed_part, *normed_got),
         micros=3,
     )
-    inputs_grad, norm_grads = call(
+    mode_mine = modes_back(place, total, *mode_args, ties=(rows_own,))
+    inputs_grad, gain_grad, bias_grad = call(
         join_kernel,
         "join",
-        [(inputs.shape, BF16), ((EXTRA, width), F32)],
-        (place, rows_own, *spread_tensor(rows_own)),
+        [(inputs.shape, BF16), ((1, width), F32), ((1, width), F32)],
+        (place, rows_own, *spread_tensor(rows_own, (mode_mine,))),
         scratch=[((size, EXTRA, width), F32)],
     )
-    mode_mine = modes_back(place, taps_grad, *mode_args)
     mode_other = swap_context(mode_mine)
 
     if fast:
@@ -1198,22 +1411,13 @@
             partial(early_out_kernel, scale=scale),
             "early_out",
             [(output_weight.shape, F32), (expand_weight.shape, F32)],
-            (place, *send_grads(early), total),
-        )
-        shape = (4, gate_weight.shape[0] // 2, units + channels)
-        late = call(
-            late_kernel,
-            "late",
-            [(shape, F32), (shape, BF16)],
-            (place, normed, gate_low, reduce_low),
-            micros=LATE,
-            ties=(),
+            (place, early, swap_context(early), total),
         )
         gate_grad, reduce_grad = call(
             partial(late_out_kernel, scale=scale),
             "late_out",
             [(gate_weight.shape, F32), (reduce_weight.shape, F32)],
-            (place, *send_grads(pair_grads(place, *late)), total),
+            (place, *late, total),
         )
     else:
         factor = tokens_all / total[error_at + 1, 0]
@@ -1224,7 +1428,7 @@
         reduce_grad = plain_grad(t_dot(normed, reduce_low), factor, 0)
 
     counts = [v.shape[1] // channels for v in vectors]
-    offsets = [sum(counts[:i]) for i in range(4)]
+    offsets = [REACH + sum(counts[:i]) for i in range(4)]
     whole = (damping.shape, F32)
     *mode_grads, timestep_grad, loss_value, gate_bias_grad, expand_bias_grad, output_bias_grad, reduce_bias_grad = call(
         partial(finish_kernel, starts=offsets, scale=scale + (float(width),)),
@@ -1236,8 +1440,8 @@
         output,
         loss_value.reshape(()),
         inputs_grad,
-        norm_grads[0],
-        norm_grads[1],
+        gain_grad[0],
+        bias_grad[0],
         gate_grad,
         gate_bias_grad[0],
         reduce_grad,

time: 212 us -> 180 us (0.85)
  waiting for transfers between devices: 93.9 us -> 58.3 us
  starting transfers between devices: 46 us -> 49.3 us
  Pallas kernels: 63.8 us -> 66.2 us
    ppermute x3 -> x1, waiting for transfers between devices: 26.1 us -> 0.01 us  [spread_tensor(): far = lax.ppermute(x, 'tensor', xor_pairs(4, 2))]
    ppermute x20 -> x26, starting transfers between devices: 19.5 us -> 28.9 us  [the longest x6 8.89 us: exchange_tensor(): lax.ppermute(x, 'tensor', tensor_pairs(size, k + 1))]
    ppermute x3 -> x1, waiting for transfers between devices: 9.96 us -> 2.07 us  [deliver_tensor(): passed = lax.ppermute(pieces[2], 'tensor', xor_pairs(4, 1))]
    ppermute x3 -> x1, waiting for transfers between devices: 7.77 us -> 2.09 us  [spread_tensor(): return [near, far, lax.ppermute(again, 'tensor', xor_pairs(4, 1))]]
    ppermute x3 -> x1, starting transfers between devices: 5.37 us -> 1.32 us  [spread_tensor(): near = lax.ppermute(x, 'tensor', xor_pairs(4, 1))]
    ppermute x20 -> x26, waiting for transfers between devices: 45.5 us -> 48 us  [the longest x3 11.1 us: send_late(): lax.ppermute(sends[k - 1], 'shard', xor_pairs(4, k))]
    pallas_call x30 -> x31, Pallas kernels: 63.8 us -> 66.2 us  [call(): pl.pallas_call(kernel, out_shape=[jax.ShapeDtypeStruct(shape, kind) for s...]
    ppermute x8, starting transfers between devices: 0.36 us -> 2.6 us  [swap_context(): return lax.ppermute(x, 'context', [(0, 1), (1, 0)])]
  transfers between devices with their start and end apart: 48 -> 46, of which waited for: 23 -> 18; matrix products, arithmetic and copies ran while one was open for 2% -> 1% of each run, Pallas kernels for 25% -> 29%
where the time goes in v3:
time: 180 us; the launch traced here: 179 us
  Pallas kernels  66.2 us (37%)
  waiting for transfers between devices  58.3 us (32%)
  starting transfers between devices  49.3 us (27%)
  local copies, waits for them, and re-layouts  2.69 us (1%)
    pallas_call x31, Pallas kernels, call(): pl.pallas_call(kernel, out_shape=[jax.ShapeDtypeStruct(shape, kind) for s...  66.2 us
    ppermute x3, waiting for transfers between devices, send_late(): lax.ppermute(sends[k - 1], 'shard', xor_pairs(4, k))  11.1 us
    ppermute x6, waiting for transfers between devices, exchange_tensor(): lax.ppermute(x, 'tensor', tensor_pairs(size, k + 1))  9.87 us
    ppermute x6, starting transfers between devices, exchange_tensor(): lax.ppermute(x, 'tensor', tensor_pairs(size, k + 1))  8.89 us
    ppermute x1, waiting for transfers between devices, sum_tensor(): second_far = lax.ppermute(joined, 'tensor', far_pairs)  8.11 us
    ppermute x1, waiting for transfers between devices, sum_tensor(): passed = lax.ppermute(after, 'tensor', near_pairs)  6.42 us
    ppermute x2, waiting for transfers between devices, sum_tensor(): lax.ppermute(away, 'tensor', near_pairs)  4.77 us
    ppermute x3, starting transfers between devices, per_device(): lax.ppermute(reduce_weight, 'shard', xor_pairs(4, k))  4.57 us
  transfers between devices with their start and end apart: 46, of which 18 were waited for; matrix products, arithmetic and copies ran while one was open for 1% of the time, Pallas kernels for 29%

profile of v3, /device:TPU:0, one launch (start us, length us, event | category | flops | bytes accessed | tf_op | source)
XLA Modules:
  0.0 179.2 jit_solution(5971270057565371315)
XLA Ops:
  0.7 3.0 %collective-permute-start.1 = (bf16[256,128]{1,0:T(8,128)(2,1)}, bf16[256,128]{1,0:T(8,128)(2,1)S(1)}, u32[]{:S(2)}, u32[]{:S(2)}) collective-permute-start(bf16[256,128]{1,0:T(8,128)(2,1)} %refs_3_.8), channel_id=1, source_target_pairs={{0,16},{8,24},{16,0},{24,8},{1,17},{9,25},{17,1},{25,9},{2,18},{10... | collective-permute-start | bytes 196616 | tf_op jit(solution)/shard_map/ppermute | solution.py:1204
  16.0 2.4 %collective-permute-start.8 = (f32[256,128]{1,0:T(8,128)S(1)}, f32[256,128]{1,0:T(8,128)S(1)}, u32[]{:S(2)}, u32[]{:S(2)}) collective-permute-start(f32[256,128]{1,0:T(8,128)S(1)} %get-tuple-element.104.refs_4_.refs_9_.refs_7_), channel_id=1, source_target_pairs={{0,4},{1,5},{2,6},{3,7},{8,12},{9,13},{10,14},{11,15},{16,20},{17,... | collective-permute-start | bytes 393224 | tf_op jit(solution)/shard_map/ppermute | solution.py:1239
  18.4 8.1 %taps.1.refs_5_ = f32[128,128]{1,0:T(8,128)S(1)} custom-call(s32[3]{0:T(128)S(1)} %pad_add_fusion.refs_0_, f32[128,512]{1,0:T(8,128)S(1)} %copy-done.10, f32[128,512]{1,0:T(8,128)S(1)} %copy-done.11, f32[128]{0:T(128)S(1)} %copy-done.20, f32[128,512]{1,0:T(8,128)S(1)} %copy-done.12, f32[128,512]{1,0:T(8,128)S(1)} %copy-done.13), custom_call_target="tpu_custom_call" | custom-call | flops 1800000000 | bytes 900000 | tf_op jit(solution)/shard_map/taps/pallas_call | solution.py:33
  27.9 3.9 %forward_mix.1.refs_3_.refs_6_.refs_4_ = bf16[512,128]{1,0:T(8,128)(2,1)S(1)} custom-call(s32[3]{0:T(128)S(1)} %pad_add_fusion.refs_0_, s32[1,512]{1,0:T(1,128)S(1)} %copy-done.18, s32[1,512]{1,0:T(1,128)S(1)} %collective-permute-done.6.refs_2_.refs_4_, s32[1,512]{1,0:T(1,128)S(1)} %copy-done.18, s32[1,512]{1,0:T(1,128)S(1)} %collective-permute-done.6.refs_2_.refs_4_, ...), custom_call_target="tpu_custom_call" | custom-call | flops 1000000000 | bytes 500000 | tf_op jit(solution)/shard_map/forward_mix/pallas_call | solution.py:33
  31.8 3.3 %collective-permute-done.4.refs_1_ = bf16[320,768]{1,0:T(8,128)(2,1)S(1)} collective-permute-done((bf16[320,768]{1,0:T(8,128)(2,1)S(1)}, bf16[320,768]{1,0:T(8,128)(2,1)S(1)}, u32[]{:S(2)}, u32[]{:S(2)}) %collective-permute-start.4) | collective-permute-done | bytes 491552 | tf_op jit(solution)/shard_map/ppermute | solution.py:1236
  35.4 3.7 %collective-permute-start.12 = (bf16[512,128]{1,0:T(8,128)(2,1)S(1)}, bf16[512,128]{1,0:T(8,128)(2,1)S(1)}, u32[]{:S(2)}, u32[]{:S(2)}) collective-permute-start(bf16[512,128]{1,0:T(8,128)(2,1)S(1)} %forward_mix.1.refs_3_.refs_6_.refs_4_), channel_id=1, source_target_pairs={{0,3},{1,2},{2,1},{3,0},{4,7},{5,6},{6,5},{7,4},{8,11},{9,10},{10,... | collective-permute-start | bytes 393224 | tf_op jit(solution)/shard_map/ppermute | solution.py:124
  43.6 7.1 %collective-permute-done.11.refs_8_.refs_6_ = bf16[512,128]{1,0:T(8,128)(2,1)S(1)} collective-permute-done((bf16[512,128]{1,0:T(8,128)(2,1)S(1)}, bf16[512,128]{1,0:T(8,128)(2,1)S(1)}, u32[]{:S(2)}, u32[]{:S(2)}) %collective-permute-start.11) | collective-permute-done | bytes 131104 | tf_op jit(solution)/shard_map/ppermute | solution.py:124
  52.3 3.2 %expand.1 = (bf16[512,768]{1,0:T(8,128)(2,1)S(1)}, bf16[512,768]{1,0:T(8,128)(2,1)S(1)}, f32[128,512]{1,0:T(8,128)S(1)}, f32[128,512]{1,0:T(8,128)S(1)}, bf16[12...) custom-call(s32[3]{0:T(128)S(1)} %pad_add_fusion.refs_0_, ...), custom_call_target="tpu_custom_call" | custom-call | flops 600000000 | bytes 300000 | tf_op jit(solution)/shard_map/expand/pallas_call | solution.py:33
  57.7 2.8 %collective-permute-start.14 = (bf16[128,512]{1,0:T(8,128)(2,1)S(1)}, bf16[128,512]{1,0:T(8,128)(2,1)S(1)}, u32[]{:S(2)}, u32[]{:S(2)}) collective-permute-start(bf16[128,512]{1,0:T(8,128)(2,1)S(1)} %get-tuple-element.121), channel_id=1, source_target_pairs={{0,2},{1,3},{2,0},{3,1},{4,6},{5,7},{6,4},{7,5},{8,10},{9,11},{10,... | collective-permute-start | bytes 393224 | tf_op jit(solution)/shard_map/ppermute | solution.py:158
  60.8 6.4 %collective-permute-done.19.refs_1_ = bf16[128,512]{1,0:T(8,128)(2,1)S(1)} collective-permute-done((bf16[128,512]{1,0:T(8,128)(2,1)S(1)}, bf16[128,512]{1,0:T(8,128)(2,1)S(1)}, u32[]{:S(2)}, u32[]{:S(2)}) %collective-permute-start.19) | collective-permute-done | bytes 131104 | tf_op jit(solution)/shard_map/ppermute | solution.py:159
  67.9 2.4 %collective-permute-start.21 = (bf16[128,512]{1,0:T(8,128)(2,1)S(1)}, bf16[128,512]{1,0:T(8,128)(2,1)S(1)}, u32[]{:S(2)}, u32[]{:S(2)}) collective-permute-start(bf16[128,512]{1,0:T(8,128)(2,1)S(1)} %get-tuple-element.128), channel_id=1, source_target_pairs={{0,1},{1,0},{2,3},{3,2},{4,5},{5,4},{6,7},{7,6},{8,9},{9,8},{10,11... | collective-permute-start | bytes 393224 | tf_op jit(solution)/shard_map/ppermute | solution.py:163
  71.9 8.1 %collective-permute-done.20 = bf16[128,512]{1,0:T(8,128)(2,1)S(1)} collective-permute-done((bf16[128,512]{1,0:T(8,128)(2,1)S(1)}, bf16[128,512]{1,0:T(8,128)(2,1)S(1)}, u32[]{:S(2)}, u32[]{:S(2)}) %collective-permute-start.20) | collective-permute-done | bytes 131104 | tf_op jit(solution)/shard_map/ppermute | solution.py:162
  83.6 2.6 %collective-permute-done.23.refs_15_ = bf16[128,512]{1,0:T(8,128)(2,1)S(1)} collective-permute-done((bf16[128,512]{1,0:T(8,128)(2,1)S(1)}, bf16[128,512]{1,0:T(8,128)(2,1)S(1)}, u32[]{:S(2)}, u32[]{:S(2)}) %collective-permute-start.23) | collective-permute-done | bytes 131104 | tf_op jit(solution)/shard_map/ppermute | solution.py:167
  87.5 3.4 %collective-permute-done.18.refs_12_ = bf16[128,512]{1,0:T(8,128)(2,1)S(1)} collective-permute-done((bf16[128,512]{1,0:T(8,128)(2,1)S(1)}, bf16[128,512]{1,0:T(8,128)(2,1)S(1)}, u32[]{:S(2)}, u32[]{:S(2)}) %collective-permute-start.18) | collective-permute-done | bytes 131104 | tf_op jit(solution)/shard_map/ppermute | solution.py:169
  92.3 4.4 %loss.1 = (bf16[512,1024]{1,0:T(8,128)(2,1)}, bf16[512,1024]{1,0:T(8,128)(2,1)S(1)}, f32[128,1024]{1,0:T(8,128)S(1)}, bf16[512,768]{1,0:T(8,128)(2,1)S(1)}, bf16...) custom-call(s32[3]{0:T(128)S(1)} %pad_add_fusion.refs_0_, ...), custom_call_target="tpu_custom_call" | custom-call | flops 1600000000 | bytes 800000 | tf_op jit(solution)/shard_map/loss/pallas_call | solution.py:33
  100.9 2.4 %collective-permute-start.27 = (bf16[512,128]{1,0:T(8,128)(2,1)S(1)}, bf16[512,128]{1,0:T(8,128)(2,1)S(1)}, u32[]{:S(2)}, u32[]{:S(2)}) collective-permute-start(bf16[512,128]{1,0:T(8,128)(2,1)S(1)} %get-tuple-element.134), channel_id=1, source_target_pairs={{0,3},{1,2},{2,1},{3,0},{4,7},{5,6},{6,5},{7,4},{8,11},{9,10},{10,... | collective-permute-start | bytes 393224 | tf_op jit(solution)/shard_map/ppermute | solution.py:124
  103.3 2.1 %gate_back.1.refs_5_.refs_11_ = f32[512,1024]{1,0:T(8,128)S(1)} custom-call(bf16[512,768]{1,0:T(8,128)(2,1)S(1)} %get-tuple-element.130.refs_0_.refs_2_, bf16[1024,768]{1,0:T(8,128)(2,1)S(1)} %get-tuple-element.108.refs_1_), custom_call_target="tpu_custom_call" | custom-call | flops 200000000 | bytes 100000 | tf_op jit(solution)/shard_map/gate_back/pallas_call | solution.py:33
  113.4 4.0 %taps_back.1.refs_1_ = f32[256,128]{1,0:T(8,128)S(1)} custom-call(s32[3]{0:T(128)S(1)} %pad_add_fusion.refs_0_, s32[1,512]{1,0:T(1,128)S(1)} %copy-done.18, s32[1,512]{1,0:T(1,128)S(1)} %collective-permute-done.6.refs_2_.refs_4_, s32[1,512]{1,0:T(1,128)S(1)} %copy-done.18, s32[1,512]{1,0:T(1,128)S(1)} %collective-permute-done.6.refs_2_.refs_4_, ...), custom_call_target="tpu_custom_call" | custom-call | flops 800000000 | bytes 400000 | tf_op jit(solution)/shard_map/taps_back/pallas_call | solution.py:33
  117.4 4.9 %backward_mix.1 = (bf16[512,128]{1,0:T(8,128)(2,1)S(1)}, f32[1,128]{1,0:T(1,128)S(1)}, f32[128,1024]{1,0:T(8,128)S(1)}, bf16[128,1024]{1,0:T(8,128)(2,1)S(1)}, b...) custom-call(s32[3]{0:T(128)S(1)} %pad_add_fusion.refs_0_, s32[1,512]{1,0:T(1,128)S(1)} %copy-done.18, ...), custom_call_target="tpu_custom_call" | custom-call | flops 1200000000 | bytes 600000 | tf_op jit(solution)/shard_map/backward_mix/pallas_call | solution.py:33
  127.3 2.8 %collective-permute-start.37 = (bf16[128,1024]{1,0:T(8,128)(2,1)S(1)}, bf16[128,1024]{1,0:T(8,128)(2,1)S(1)}, u32[]{:S(2)}, u32[]{:S(2)}) collective-permute-start(bf16[128,1024]{1,0:T(8,128)(2,1)S(1)} %get-tuple-element.150.refs_6_), channel_id=1, source_target_pairs={{0,1},{1,0},{2,3},{3,2},{4,5},{5,4},{6,7},{7,6},{8,9},{9,8},{10,11... | collective-permute-start | bytes 786440 | tf_op jit(solution)/shard_map/ppermute | solution.py:194
  138.8 3.8 %collective-permute-done.34.refs_2_ = bf16[208,896]{1,0:T(8,128)(2,1)S(1)} collective-permute-done((bf16[208,896]{1,0:T(8,128)(2,1)S(1)}, bf16[208,896]{1,0:T(8,128)(2,1)S(1)}, u32[]{:S(2)}, u32[]{:S(2)}) %collective-permute-start.34) | collective-permute-done | bytes 372768 | tf_op jit(solution)/shard_map/ppermute | solution.py:1156
  142.7 7.3 %collective-permute-done.35.refs_3_ = bf16[208,896]{1,0:T(8,128)(2,1)S(1)} collective-permute-done((bf16[208,896]{1,0:T(8,128)(2,1)S(1)}, bf16[208,896]{1,0:T(8,128)(2,1)S(1)}, u32[]{:S(2)}, u32[]{:S(2)}) %collective-permute-start.35) | collective-permute-done | bytes 372768 | tf_op jit(solution)/shard_map/ppermute | solution.py:1156
  155.6 12.4 %modes_back.1.refs_2_ = f32[520,256]{1,0:T(8,128)S(1)} custom-call(s32[3]{0:T(128)S(1)} %pad_add_fusion.refs_0_, f32[560,128]{1,0:T(8,128)S(1)} %get-tuple-element.166.refs_4_.refs_1_.refs_3_, f32[128,512]{1,0:T(8,128)S(1)} %copy-done.10, f32[128,512]{1,0:T(8,128)S(1)} %copy-done.11, f32[128]{0:T(128)S(1)} %copy-done.20, f32[128,512]{1,0:T(8,128)S(1)} %copy-done.12, ...), custom_call_target="tpu_custom_call" | custom-call | flops 800000000 | bytes 400000 | tf_op jit(solution)/shard_map/modes_back/pallas_call | solution.py:33
  175.6 2.1 %collective-permute-done.43.refs_4_ = bf16[144,1024]{1,0:T(8,128)(2,1)S(1)} collective-permute-done((bf16[144,1024]{1,0:T(8,128)(2,1)S(1)}, bf16[144,1024]{1,0:T(8,128)(2,1)S(1)}, u32[]{:S(2)}, u32[]{:S(2)}) %collective-permute-start.43) | collective-permute-done | bytes 294944 | tf_op jit(solution)/shard_map/ppermute | solution.py:187
  (147 shorter events, 71.5 us)
Async XLA Ops:
  12.4 19.4 %collective-permute-start.5 = (bf16[320,768]{1,0:T(8,128)(2,1)S(1)}, bf16[320,768]{1,0:T(8,128)(2,1)S(1)}, u32[]{:S(2)}, u32[]{:S(2)}) collective-permute-start(bf16[320,768]{1,0:T(8,128)(2,1)S(1)} %get-tuple-element.105.refs_1_), channel_id=1, source_target_pairs={{0,24},{8,16},{16,8},{24,0},{1,25},{9,17},{17,9},{25,1},{2,26},{10... | collective-permute-start | bytes 1474568 | tf_op jit(solution)/shard_map/ppermute | solution.py:1236
  13.9 21.3 %collective-permute-start.4 = (bf16[320,768]{1,0:T(8,128)(2,1)S(1)}, bf16[320,768]{1,0:T(8,128)(2,1)S(1)}, u32[]{:S(2)}, u32[]{:S(2)}) collective-permute-start(bf16[320,768]{1,0:T(8,128)(2,1)S(1)} %get-tuple-element.105.refs_1_), channel_id=1, source_target_pairs={{0,16},{8,24},{16,0},{24,8},{1,17},{9,25},{17,1},{25,9},{2,18},{10... | collective-permute-start | bytes 1474568 | tf_op jit(solution)/shard_map/ppermute | solution.py:1236
  14.5 20.7 %collective-permute-start.3 = (bf16[320,768]{1,0:T(8,128)(2,1)S(1)}, bf16[320,768]{1,0:T(8,128)(2,1)S(1)}, u32[]{:S(2)}, u32[]{:S(2)}) collective-permute-start(bf16[320,768]{1,0:T(8,128)(2,1)S(1)} %get-tuple-element.105.refs_1_), channel_id=1, source_target_pairs={{0,8},{8,0},{16,24},{24,16},{1,9},{9,1},{17,25},{25,17},{2,10},{10... | collective-permute-start | bytes 1474568 | tf_op jit(solution)/shard_map/ppermute | solution.py:1236
  16.0 10.6 %collective-permute-start.6 = (s32[1,512]{1,0:T(1,128)S(1)}, s32[1,512]{1,0:T(1,128)S(1)}, u32[]{:S(2)}, u32[]{:S(2)}) collective-permute-start(s32[1,512]{1,0:T(1,128)S(1)} %copy-done.18), channel_id=1, source_target_pairs={{0,4},{4,0},{1,5},{5,1},{2,6},{6,2},{3,7},{7,3},{8,12},{12,8},{9,1... | collective-permute-start | bytes 6152 | tf_op jit(solution)/shard_map/ppermute | solution.py:84
  16.0 11.9 %collective-permute-start.8 = (f32[256,128]{1,0:T(8,128)S(1)}, f32[256,128]{1,0:T(8,128)S(1)}, u32[]{:S(2)}, u32[]{:S(2)}) collective-permute-start(f32[256,128]{1,0:T(8,128)S(1)} %get-tuple-element.104.refs_4_.refs_9_.refs_7_), channel_id=1, source_target_pairs={{0,4},{1,5},{2,6},{3,7},{8,12},{9,13},{10,14},{11,15},{16,20},{17,... | collective-permute-start | bytes 393224 | tf_op jit(solution)/shard_map/ppermute | solution.py:1239
  39.0 11.7 %collective-permute-start.11 = (bf16[512,128]{1,0:T(8,128)(2,1)S(1)}, bf16[512,128]{1,0:T(8,128)(2,1)S(1)}, u32[]{:S(2)}, u32[]{:S(2)}) collective-permute-start(bf16[512,128]{1,0:T(8,128)(2,1)S(1)} %forward_mix.1.refs_3_.refs_6_.refs_4_), channel_id=1, source_target_pairs={{0,2},{1,3},{2,0},{3,1},{4,6},{5,7},{6,4},{7,5},{8,10},{9,11},{10,... | collective-permute-start | bytes 393224 | tf_op jit(solution)/shard_map/ppermute | solution.py:124
  39.0 11.7 %collective-permute-start.10 = (bf16[512,128]{1,0:T(8,128)(2,1)S(1)}, bf16[512,128]{1,0:T(8,128)(2,1)S(1)}, u32[]{:S(2)}, u32[]{:S(2)}) collective-permute-start(bf16[512,128]{1,0:T(8,128)(2,1)S(1)} %forward_mix.1.refs_3_.refs_6_.refs_4_), channel_id=1, source_target_pairs={{0,1},{1,0},{2,3},{3,2},{4,5},{5,4},{6,7},{7,6},{8,9},{9,8},{10,11... | collective-permute-start | bytes 393224 | tf_op jit(solution)/shard_map/ppermute | solution.py:124
  57.7 12.5 %collective-permute-start.14 = (bf16[128,512]{1,0:T(8,128)(2,1)S(1)}, bf16[128,512]{1,0:T(8,128)(2,1)S(1)}, u32[]{:S(2)}, u32[]{:S(2)}) collective-permute-start(bf16[128,512]{1,0:T(8,128)(2,1)S(1)} %get-tuple-element.121), channel_id=1, source_target_pairs={{0,2},{1,3},{2,0},{3,1},{4,6},{5,7},{6,4},{7,5},{8,10},{9,11},{10,... | collective-permute-start | bytes 393224 | tf_op jit(solution)/shard_map/ppermute | solution.py:158
  67.9 12.1 %collective-permute-start.20 = (bf16[128,512]{1,0:T(8,128)(2,1)S(1)}, bf16[128,512]{1,0:T(8,128)(2,1)S(1)}, u32[]{:S(2)}, u32[]{:S(2)}) collective-permute-start(bf16[128,512]{1,0:T(8,128)(2,1)S(1)} %get-tuple-element.127), channel_id=1, source_target_pairs={{0,2},{1,3},{2,0},{3,1},{4,6},{5,7},{6,4},{7,5},{8,10},{9,11},{10,... | collective-permute-start | bytes 393224 | tf_op jit(solution)/shard_map/ppermute | solution.py:162
  67.9 12.1 %collective-permute-start.21 = (bf16[128,512]{1,0:T(8,128)(2,1)S(1)}, bf16[128,512]{1,0:T(8,128)(2,1)S(1)}, u32[]{:S(2)}, u32[]{:S(2)}) collective-permute-start(bf16[128,512]{1,0:T(8,128)(2,1)S(1)} %get-tuple-element.128), channel_id=1, source_target_pairs={{0,1},{1,0},{2,3},{3,2},{4,5},{5,4},{6,7},{7,6},{8,9},{9,8},{10,11... | collective-permute-start | bytes 393224 | tf_op jit(solution)/shard_map/ppermute | solution.py:163
  70.3 12.0 %collective-permute-start.17 = (bf16[128,512]{1,0:T(8,128)(2,1)S(1)}, bf16[128,512]{1,0:T(8,128)(2,1)S(1)}, u32[]{:S(2)}, u32[]{:S(2)}) collective-permute-start(bf16[128,512]{1,0:T(8,128)(2,1)S(1)} %add_convert_fusion.1.refs_9_), channel_id=1, source_target_pairs={{0,2},{1,3},{2,0},{3,1},{4,6},{5,7},{6,4},{7,5},{8,10},{9,11},{10,... | collective-permute-start | bytes 393224 | tf_op jit(solution)/shard_map/ppermute | solution.py:167
  98.9 12.9 %collective-permute-start.26 = (bf16[512,128]{1,0:T(8,128)(2,1)S(1)}, bf16[512,128]{1,0:T(8,128)(2,1)S(1)}, u32[]{:S(2)}, u32[]{:S(2)}) collective-permute-start(bf16[512,128]{1,0:T(8,128)(2,1)S(1)} %get-tuple-element.133), channel_id=1, source_target_pairs={{0,2},{1,3},{2,0},{3,1},{4,6},{5,7},{6,4},{7,5},{8,10},{9,11},{10,... | collective-permute-start | bytes 393224 | tf_op jit(solution)/shard_map/ppermute | solution.py:124
  100.9 11.0 %collective-permute-start.27 = (bf16[512,128]{1,0:T(8,128)(2,1)S(1)}, bf16[512,128]{1,0:T(8,128)(2,1)S(1)}, u32[]{:S(2)}, u32[]{:S(2)}) collective-permute-start(bf16[512,128]{1,0:T(8,128)(2,1)S(1)} %get-tuple-element.134), channel_id=1, source_target_pairs={{0,3},{1,2},{2,1},{3,0},{4,7},{5,6},{6,5},{7,4},{8,11},{9,10},{10,... | collective-permute-start | bytes 393224 | tf_op jit(solution)/shard_map/ppermute | solution.py:124
  106.3 17.2 %collective-permute-start.30 = (bf16[192,768]{1,0:T(8,128)(2,1)S(1)}, bf16[192,768]{1,0:T(8,128)(2,1)S(1)}, u32[]{:S(2)}, u32[]{:S(2)}) collective-permute-start(bf16[192,768]{1,0:T(8,128)(2,1)S(1)} %get-tuple-element.156), channel_id=1, source_target_pairs={{0,8},{8,0},{16,24},{24,16},{1,9},{9,1},{17,25},{25,17},{2,10},{10... | collective-permute-start | bytes 884744 | tf_op jit(solution)/shard_map/ppermute | solution.py:1340
  107.7 15.7 %collective-permute-start.31 = (bf16[192,768]{1,0:T(8,128)(2,1)S(1)}, bf16[192,768]{1,0:T(8,128)(2,1)S(1)}, u32[]{:S(2)}, u32[]{:S(2)}) collective-permute-start(bf16[192,768]{1,0:T(8,128)(2,1)S(1)} %get-tuple-element.157), channel_id=1, source_target_pairs={{0,16},{8,24},{16,0},{24,8},{1,17},{9,25},{17,1},{25,9},{2,18},{10... | collective-permute-start | bytes 884744 | tf_op jit(solution)/shard_map/ppermute | solution.py:1340
  108.6 14.8 %collective-permute-start.32 = (bf16[192,768]{1,0:T(8,128)(2,1)S(1)}, bf16[192,768]{1,0:T(8,128)(2,1)S(1)}, u32[]{:S(2)}, u32[]{:S(2)}) collective-permute-start(bf16[192,768]{1,0:T(8,128)(2,1)S(1)} %get-tuple-element.158), channel_id=1, source_target_pairs={{0,24},{8,16},{16,8},{24,0},{1,25},{9,17},{17,9},{25,1},{2,26},{10... | collective-permute-start | bytes 884744 | tf_op jit(solution)/shard_map/ppermute | solution.py:1340
  131.0 11.6 %collective-permute-start.34 = (bf16[208,896]{1,0:T(8,128)(2,1)S(1)}, bf16[208,896]{1,0:T(8,128)(2,1)S(1)}, u32[]{:S(2)}, u32[]{:S(2)}) collective-permute-start(bf16[208,896]{1,0:T(8,128)(2,1)S(1)} %get-tuple-element.163), channel_id=1, source_target_pairs={{0,8},{8,0},{16,24},{24,16},{1,9},{9,1},{17,25},{25,17},{2,10},{10... | collective-permute-start | bytes 1118216 | tf_op jit(solution)/shard_map/ppermute | solution.py:1156
  131.6 18.3 %collective-permute-start.35 = (bf16[208,896]{1,0:T(8,128)(2,1)S(1)}, bf16[208,896]{1,0:T(8,128)(2,1)S(1)}, u32[]{:S(2)}, u32[]{:S(2)}) collective-permute-start(bf16[208,896]{1,0:T(8,128)(2,1)S(1)} %get-tuple-element.164), channel_id=1, source_target_pairs={{0,16},{8,24},{16,0},{24,8},{1,17},{9,25},{17,1},{25,9},{2,18},{10... | collective-permute-start | bytes 1118216 | tf_op jit(solution)/shard_map/ppermute | solution.py:1156
  133.4 16.5 %collective-permute-start.36 = (bf16[208,896]{1,0:T(8,128)(2,1)S(1)}, bf16[208,896]{1,0:T(8,128)(2,1)S(1)}, u32[]{:S(2)}, u32[]{:S(2)}) collective-permute-start(bf16[208,896]{1,0:T(8,128)(2,1)S(1)} %get-tuple-element.165), channel_id=1, source_target_pairs={{0,24},{8,16},{16,8},{24,0},{1,25},{9,17},{17,9},{25,1},{2,26},{10... | collective-permute-start | bytes 1118216 | tf_op jit(solution)/shard_map/ppermute | solution.py:1156
  136.7 13.5 %collective-permute-start.38 = (bf16[128,1024]{1,0:T(8,128)(2,1)S(1)}, bf16[128,1024]{1,0:T(8,128)(2,1)S(1)}, u32[]{:S(2)}, u32[]{:S(2)}) collective-permute-start(bf16[128,1024]{1,0:T(8,128)(2,1)S(1)} %get-tuple-element.168), channel_id=1, source_target_pairs={{0,1},{1,0},{2,3},{3,2},{4,5},{5,4},{6,7},{7,6},{8,9},{9,8},{10,11... | collective-permute-start | bytes 786440 | tf_op jit(solution)/shard_map/ppermute | solution.py:204
  138.5 13.7 %collective-permute-start.39 = (bf16[128,1024]{1,0:T(8,128)(2,1)S(1)}, bf16[128,1024]{1,0:T(8,128)(2,1)S(1)}, u32[]{:S(2)}, u32[]{:S(2)}) collective-permute-start(bf16[128,1024]{1,0:T(8,128)(2,1)S(1)} %get-tuple-element.169), channel_id=1, source_target_pairs={{0,2},{1,3},{2,0},{3,1},{4,6},{5,7},{6,4},{7,5},{8,10},{9,11},{10,... | collective-permute-start | bytes 786440 | tf_op jit(solution)/shard_map/ppermute | solution.py:205
  142.7 26.7 %collective-permute-start.45 = (f32[192,768]{1,0:T(8,128)S(1)}, f32[192,768]{1,0:T(8,128)S(1)}, u32[]{:S(2)}, u32[]{:S(2)}) collective-permute-start(f32[192,768]{1,0:T(8,128)S(1)} %add_add_fusion.refs_5_.refs_1_), channel_id=1, source_target_pairs={{0,4},{4,0},{1,5},{5,1},{2,6},{6,2},{3,7},{7,3},{8,12},{12,8},{9,1... | collective-permute-start | bytes 1769480 | tf_op jit(solution)/shard_map/ppermute | solution.py:84
  153.5 15.1 %collective-permute-start.42 = (bf16[144,1024]{1,0:T(8,128)(2,1)S(1)}, bf16[144,1024]{1,0:T(8,128)(2,1)S(1)}, u32[]{:S(2)}, u32[]{:S(2)}) collective-permute-start(bf16[144,1024]{1,0:T(8,128)(2,1)S(1)} %rows.1.refs_7_.refs_1_), channel_id=1, source_target_pairs={{0,2},{1,3},{2,0},{3,1},{4,6},{5,7},{6,4},{7,5},{8,10},{9,11},{10,... | collective-permute-start | bytes 884744 | tf_op jit(solution)/shard_map/ppermute | solution.py:177
  154.3 14.3 %collective-permute-start.41 = (bf16[144,1024]{1,0:T(8,128)(2,1)S(1)}, bf16[144,1024]{1,0:T(8,128)(2,1)S(1)}, u32[]{:S(2)}, u32[]{:S(2)}) collective-permute-start(bf16[144,1024]{1,0:T(8,128)(2,1)S(1)} %rows.1.refs_7_.refs_1_), channel_id=1, source_target_pairs={{0,1},{1,0},{2,3},{3,2},{4,5},{5,4},{6,7},{7,6},{8,9},{9,8},{10,11... | collective-permute-start | bytes 884744 | tf_op jit(solution)/shard_map/ppermute | solution.py:176
  (43 other events, 397.8 us)

commit v4 on v3

--- a/solution.py
+++ b/solution.py
@@ -10,7 +10,7 @@
 
 REACH = 256
 EPSILON = 1e-05
-EARLY, PAIR, LATE, TAPS_BACK, MODES_BACK, TAPS = 2, 1, 2, 4, 4, 9
+EARLY, PAIR, LATE, TAPS_BACK, MODES_BACK, TAPS = 2,1,2,4,4,60
 GELU_SCALE = 0.7978845608028654
 F32 = jnp.float32
 BF16 = jnp.bfloat16
@@ -1209,16 +1209,17 @@
         expand_full = lax.all_gather(expand_weight, "shard", axis=0, tiled=True)
         output_full = lax.all_gather(output_weight.T, "shard", axis=0, tiled=True)
 
+    mode_args = (damping, frequency, timestep, mix_real, mix_imaginary)
+    taps_mine = make_taps(place, *mode_args, REACH // 2)
+    taps = (taps_mine, swap_context(taps_mine))
     normed, unit = call(
         norm_kernel,
         "norm",
         [(inputs.shape, BF16)] * 2,
         (inputs, norm_gain, norm_bias),
         scalars=0,
-    )
-    mode_args = (damping, frequency, timestep, mix_real, mix_imaginary)
-    taps_mine = make_taps(place, *mode_args, REACH // 2)
-    taps = (taps_mine, swap_context(taps_mine))
+        ties=(taps_mine,),
+    )
     half_rows = (tokens // 2, channels)
     u_low, u_high, reduce_slope, reduce_full = call(
         partial(reduce_kernel, count=len(reduce_pieces)),
@@ -1231,7 +1232,6 @@
         shape = (gate_weight.shape[0] + some, units)
         mine, rest = call(
             pack_kernel, "pack", [(shape, BF16)] * 2, (place, gate_weight, expand_weight, output_weight),
-            ties=(u_high,),
         )
         nears = [lax.ppermute(mine, "shard", xor_pairs(4, k)) for k in (1, 2, 3)]
     before = [(i, i + 1) for i in range(contexts - 1)]

time: 180 us -> 177 us (0.983)
  waiting for transfers between devices: 58.3 us -> 56.1 us
  transfers between devices with their start and end apart: 46 -> 46, of which waited for: 18 -> 21; matrix products, arithmetic and copies ran while one was open for 1% -> 1% of each run, Pallas kernels for 29% -> 30%
where the time goes in v4:
time: 177 us
  Pallas kernels  65 us (37%)
  waiting for transfers between devices  56.1 us (32%)
  starting transfers between devices  50 us (28%)
  local copies, waits for them, and re-layouts  3 us (2%)
    pallas_call x31, Pallas kernels, call(): pl.pallas_call(kernel, out_shape=[jax.ShapeDtypeStruct(shape, kind) for s...  65 us
    ppermute x3, waiting for transfers between devices, send_late(): lax.ppermute(sends[k - 1], 'shard', xor_pairs(4, k))  11.7 us
    ppermute x6, waiting for transfers between devices, exchange_tensor(): lax.ppermute(x, 'tensor', tensor_pairs(size, k + 1))  9.87 us
    ppermute x6, starting transfers between devices, exchange_tensor(): lax.ppermute(x, 'tensor', tensor_pairs(size, k + 1))  8.9 us
    ppermute x1, waiting for transfers between devices, sum_tensor(): second_far = lax.ppermute(joined, 'tensor', far_pairs)  8.14 us
    ppermute x1, waiting for transfers between devices, sum_tensor(): passed = lax.ppermute(after, 'tensor', near_pairs)  6.4 us
    ppermute x2, waiting for transfers between devices, sum_tensor(): lax.ppermute(away, 'tensor', near_pairs)  4.78 us
    ppermute x3, starting transfers between devices, per_device(): lax.ppermute(reduce_weight, 'shard', xor_pairs(4, k))  4.57 us
  transfers between devices with their start and end apart: 46, of which 21 were waited for; matrix products, arithmetic and copies ran while one was open for 1% of the time, Pallas kernels for 30%

profile of v4, /device:TPU:0, one launch (start us, length us, event | category | flops | bytes accessed | tf_op | source)
XLA Modules:
  0.0 176.9 jit_solution(12456120021611625090)
XLA Ops:
  0.7 3.0 %collective-permute-start.6 = (bf16[256,128]{1,0:T(8,128)(2,1)}, bf16[256,128]{1,0:T(8,128)(2,1)S(1)}, u32[]{:S(2)}, u32[]{:S(2)}) collective-permute-start(bf16[256,128]{1,0:T(8,128)(2,1)} %refs_3_.10), channel_id=1, source_target_pairs={{0,16},{8,24},{16,0},{24,8},{1,17},{9,25},{17,1},{25,9},{2,18},{10... | collective-permute-start | bytes 196616 | tf_op jit(solution)/shard_map/ppermute | solution.py:1204
  9.0 2.9 %collective-permute-start.2 = (bf16[320,768]{1,0:T(8,128)(2,1)S(1)}, bf16[320,768]{1,0:T(8,128)(2,1)S(1)}, u32[]{:S(2)}, u32[]{:S(2)}) collective-permute-start(bf16[320,768]{1,0:T(8,128)(2,1)S(1)} %get-tuple-element.104.refs_1_), channel_id=1, source_target_pairs={{0,24},{8,16},{16,8},{24,0},{1,25},{9,17},{17,9},{25,1},{2,26},{10... | collective-permute-start | bytes 1474568 | tf_op jit(solution)/shard_map/ppermute | solution.py:1236
  12.6 8.1 %taps.1.refs_3_.refs_5_ = f32[128,128]{1,0:T(8,128)S(1)} custom-call(s32[3]{0:T(128)S(1)} %pad_add_fusion.refs_0_, f32[128,512]{1,0:T(8,128)S(1)} %copy-done.8, f32[128,512]{1,0:T(8,128)S(1)} %copy-done.9, f32[128]{0:T(128)S(1)} %copy-done.18, f32[128,512]{1,0:T(8,128)S(1)} %copy-done.10, f32[128,512]{1,0:T(8,128)S(1)} %copy-done.11), custom_call_target="tpu_custom_call" | custom-call | flops 12000000000 | bytes 6000000 | tf_op jit(solution)/shard_map/taps/pallas_call | solution.py:33
  26.8 3.6 %forward_mix.1.refs_3_.refs_6_.refs_4_ = bf16[512,128]{1,0:T(8,128)(2,1)S(1)} custom-call(s32[3]{0:T(128)S(1)} %pad_add_fusion.refs_0_, s32[1,512]{1,0:T(1,128)S(1)} %copy-done.16, s32[1,512]{1,0:T(1,128)S(1)} %collective-permute-done.3.refs_2_.refs_4_, s32[1,512]{1,0:T(1,128)S(1)} %copy-done.16, s32[1,512]{1,0:T(1,128)S(1)} %collective-permute-done.3.refs_2_.refs_4_, ...), custom_call_target="tpu_custom_call" | custom-call | flops 1000000000 | bytes 500000 | tf_op jit(solution)/shard_map/forward_mix/pallas_call | solution.py:33
  30.4 2.5 %collective-permute-done.1.refs_1_ = bf16[320,768]{1,0:T(8,128)(2,1)S(1)} collective-permute-done((bf16[320,768]{1,0:T(8,128)(2,1)S(1)}, bf16[320,768]{1,0:T(8,128)(2,1)S(1)}, u32[]{:S(2)}, u32[]{:S(2)}) %collective-permute-start.1) | collective-permute-done | bytes 491552 | tf_op jit(solution)/shard_map/ppermute | solution.py:1236
  33.3 3.7 %collective-permute-start.12 = (bf16[512,128]{1,0:T(8,128)(2,1)S(1)}, bf16[512,128]{1,0:T(8,128)(2,1)S(1)}, u32[]{:S(2)}, u32[]{:S(2)}) collective-permute-start(bf16[512,128]{1,0:T(8,128)(2,1)S(1)} %forward_mix.1.refs_3_.refs_6_.refs_4_), channel_id=1, source_target_pairs={{0,3},{1,2},{2,1},{3,0},{4,7},{5,6},{6,5},{7,4},{8,11},{9,10},{10,... | collective-permute-start | bytes 393224 | tf_op jit(solution)/shard_map/ppermute | solution.py:124
  41.6 7.1 %collective-permute-done.11.refs_8_.refs_6_ = bf16[512,128]{1,0:T(8,128)(2,1)S(1)} collective-permute-done((bf16[512,128]{1,0:T(8,128)(2,1)S(1)}, bf16[512,128]{1,0:T(8,128)(2,1)S(1)}, u32[]{:S(2)}, u32[]{:S(2)}) %collective-permute-start.11) | collective-permute-done | bytes 131104 | tf_op jit(solution)/shard_map/ppermute | solution.py:124
  50.3 3.2 %expand.1 = (bf16[512,768]{1,0:T(8,128)(2,1)S(1)}, bf16[512,768]{1,0:T(8,128)(2,1)S(1)}, f32[128,512]{1,0:T(8,128)S(1)}, f32[128,512]{1,0:T(8,128)S(1)}, bf16[12...) custom-call(s32[3]{0:T(128)S(1)} %pad_add_fusion.refs_0_, ...), custom_call_target="tpu_custom_call" | custom-call | flops 600000000 | bytes 300000 | tf_op jit(solution)/shard_map/expand/pallas_call | solution.py:33
  55.7 2.8 %collective-permute-start.14 = (bf16[128,512]{1,0:T(8,128)(2,1)S(1)}, bf16[128,512]{1,0:T(8,128)(2,1)S(1)}, u32[]{:S(2)}, u32[]{:S(2)}) collective-permute-start(bf16[128,512]{1,0:T(8,128)(2,1)S(1)} %get-tuple-element.121), channel_id=1, source_target_pairs={{0,2},{1,3},{2,0},{3,1},{4,6},{5,7},{6,4},{7,5},{8,10},{9,11},{10,... | collective-permute-start | bytes 393224 | tf_op jit(solution)/shard_map/ppermute | solution.py:158
  58.8 6.4 %collective-permute-done.19.refs_1_ = bf16[128,512]{1,0:T(8,128)(2,1)S(1)} collective-permute-done((bf16[128,512]{1,0:T(8,128)(2,1)S(1)}, bf16[128,512]{1,0:T(8,128)(2,1)S(1)}, u32[]{:S(2)}, u32[]{:S(2)}) %collective-permute-start.19) | collective-permute-done | bytes 131104 | tf_op jit(solution)/shard_map/ppermute | solution.py:159
  65.9 2.4 %collective-permute-start.21 = (bf16[128,512]{1,0:T(8,128)(2,1)S(1)}, bf16[128,512]{1,0:T(8,128)(2,1)S(1)}, u32[]{:S(2)}, u32[]{:S(2)}) collective-permute-start(bf16[128,512]{1,0:T(8,128)(2,1)S(1)} %get-tuple-element.128), channel_id=1, source_target_pairs={{0,1},{1,0},{2,3},{3,2},{4,5},{5,4},{6,7},{7,6},{8,9},{9,8},{10,11... | collective-permute-start | bytes 393224 | tf_op jit(solution)/shard_map/ppermute | solution.py:163
  69.9 8.1 %collective-permute-done.20 = bf16[128,512]{1,0:T(8,128)(2,1)S(1)} collective-permute-done((bf16[128,512]{1,0:T(8,128)(2,1)S(1)}, bf16[128,512]{1,0:T(8,128)(2,1)S(1)}, u32[]{:S(2)}, u32[]{:S(2)}) %collective-permute-start.20) | collective-permute-done | bytes 131104 | tf_op jit(solution)/shard_map/ppermute | solution.py:162
  81.8 2.5 %collective-permute-done.23.refs_15_ = bf16[128,512]{1,0:T(8,128)(2,1)S(1)} collective-permute-done((bf16[128,512]{1,0:T(8,128)(2,1)S(1)}, bf16[128,512]{1,0:T(8,128)(2,1)S(1)}, u32[]{:S(2)}, u32[]{:S(2)}) %collective-permute-start.23) | collective-permute-done | bytes 131104 | tf_op jit(solution)/shard_map/ppermute | solution.py:167
  85.4 3.4 %collective-permute-done.18.refs_12_ = bf16[128,512]{1,0:T(8,128)(2,1)S(1)} collective-permute-done((bf16[128,512]{1,0:T(8,128)(2,1)S(1)}, bf16[128,512]{1,0:T(8,128)(2,1)S(1)}, u32[]{:S(2)}, u32[]{:S(2)}) %collective-permute-start.18) | collective-permute-done | bytes 131104 | tf_op jit(solution)/shard_map/ppermute | solution.py:169
  90.2 4.4 %loss.1 = (bf16[512,1024]{1,0:T(8,128)(2,1)}, bf16[512,1024]{1,0:T(8,128)(2,1)S(1)}, f32[128,1024]{1,0:T(8,128)S(1)}, bf16[512,768]{1,0:T(8,128)(2,1)S(1)}, bf16...) custom-call(s32[3]{0:T(128)S(1)} %pad_add_fusion.refs_0_, ...), custom_call_target="tpu_custom_call" | custom-call | flops 1600000000 | bytes 800000 | tf_op jit(solution)/shard_map/loss/pallas_call | solution.py:33
  98.8 2.4 %collective-permute-start.27 = (bf16[512,128]{1,0:T(8,128)(2,1)S(1)}, bf16[512,128]{1,0:T(8,128)(2,1)S(1)}, u32[]{:S(2)}, u32[]{:S(2)}) collective-permute-start(bf16[512,128]{1,0:T(8,128)(2,1)S(1)} %get-tuple-element.134), channel_id=1, source_target_pairs={{0,3},{1,2},{2,1},{3,0},{4,7},{5,6},{6,5},{7,4},{8,11},{9,10},{10,... | collective-permute-start | bytes 393224 | tf_op jit(solution)/shard_map/ppermute | solution.py:124
  101.2 2.1 %gate_back.1.refs_5_.refs_11_ = f32[512,1024]{1,0:T(8,128)S(1)} custom-call(bf16[512,768]{1,0:T(8,128)(2,1)S(1)} %get-tuple-element.130.refs_0_.refs_2_, bf16[1024,768]{1,0:T(8,128)(2,1)S(1)} %get-tuple-element.108.refs_1_), custom_call_target="tpu_custom_call" | custom-call | flops 200000000 | bytes 100000 | tf_op jit(solution)/shard_map/gate_back/pallas_call | solution.py:33
  111.4 3.6 %taps_back.1.refs_1_ = f32[256,128]{1,0:T(8,128)S(1)} custom-call(s32[3]{0:T(128)S(1)} %pad_add_fusion.refs_0_, s32[1,512]{1,0:T(1,128)S(1)} %copy-done.16, s32[1,512]{1,0:T(1,128)S(1)} %collective-permute-done.3.refs_2_.refs_4_, s32[1,512]{1,0:T(1,128)S(1)} %copy-done.16, s32[1,512]{1,0:T(1,128)S(1)} %collective-permute-done.3.refs_2_.refs_4_, ...), custom_call_target="tpu_custom_call" | custom-call | flops 800000000 | bytes 400000 | tf_op jit(solution)/shard_map/taps_back/pallas_call | solution.py:33
  115.0 4.3 %backward_mix.1 = (bf16[512,128]{1,0:T(8,128)(2,1)S(1)}, f32[1,128]{1,0:T(1,128)S(1)}, f32[128,1024]{1,0:T(8,128)S(1)}, bf16[128,1024]{1,0:T(8,128)(2,1)S(1)}, b...) custom-call(s32[3]{0:T(128)S(1)} %pad_add_fusion.refs_0_, s32[1,512]{1,0:T(1,128)S(1)} %copy-done.16, ...), custom_call_target="tpu_custom_call" | custom-call | flops 1200000000 | bytes 600000 | tf_op jit(solution)/shard_map/backward_mix/pallas_call | solution.py:33
  122.5 2.4 %collective-permute-start.33 = (bf16[592,896]{1,0:T(8,128)(2,1)S(1)}, bf16[592,896]{1,0:T(8,128)(2,1)S(1)}, u32[]{:S(2)}, u32[]{:S(2)}) collective-permute-start(bf16[592,896]{1,0:T(8,128)(2,1)S(1)} %get-tuple-element.160), channel_id=1, source_target_pairs={{0,4},{4,0},{1,5},{5,1},{2,6},{6,2},{3,7},{7,3},{8,12},{12,8},{9,1... | collective-permute-start | bytes 3182600 | tf_op jit(solution)/shard_map/ppermute | solution.py:84
  124.9 2.8 %collective-permute-start.37 = (bf16[128,1024]{1,0:T(8,128)(2,1)S(1)}, bf16[128,1024]{1,0:T(8,128)(2,1)S(1)}, u32[]{:S(2)}, u32[]{:S(2)}) collective-permute-start(bf16[128,1024]{1,0:T(8,128)(2,1)S(1)} %get-tuple-element.150.refs_6_), channel_id=1, source_target_pairs={{0,1},{1,0},{2,3},{3,2},{4,5},{5,4},{6,7},{7,6},{8,9},{9,8},{10,11... | collective-permute-start | bytes 786440 | tf_op jit(solution)/shard_map/ppermute | solution.py:194
  136.5 3.8 %collective-permute-done.34.refs_2_ = bf16[208,896]{1,0:T(8,128)(2,1)S(1)} collective-permute-done((bf16[208,896]{1,0:T(8,128)(2,1)S(1)}, bf16[208,896]{1,0:T(8,128)(2,1)S(1)}, u32[]{:S(2)}, u32[]{:S(2)}) %collective-permute-start.34) | collective-permute-done | bytes 372768 | tf_op jit(solution)/shard_map/ppermute | solution.py:1156
  141.2 7.0 %collective-permute-done.36.refs_4_ = bf16[208,896]{1,0:T(8,128)(2,1)S(1)} collective-permute-done((bf16[208,896]{1,0:T(8,128)(2,1)S(1)}, bf16[208,896]{1,0:T(8,128)(2,1)S(1)}, u32[]{:S(2)}, u32[]{:S(2)}) %collective-permute-start.36) | collective-permute-done | bytes 372768 | tf_op jit(solution)/shard_map/ppermute | solution.py:1156
  153.2 12.4 %modes_back.1.refs_2_ = f32[520,256]{1,0:T(8,128)S(1)} custom-call(s32[3]{0:T(128)S(1)} %pad_add_fusion.refs_0_, f32[560,128]{1,0:T(8,128)S(1)} %get-tuple-element.166.refs_4_.refs_1_.refs_3_, f32[128,512]{1,0:T(8,128)S(1)} %copy-done.8, f32[128,512]{1,0:T(8,128)S(1)} %copy-done.9, f32[128]{0:T(128)S(1)} %copy-done.18, f32[128,512]{1,0:T(8,128)S(1)} %copy-done.10, ...), custom_call_target="tpu_custom_call" | custom-call | flops 800000000 | bytes 400000 | tf_op jit(solution)/shard_map/modes_back/pallas_call | solution.py:33
  (143 shorter events, 70.7 us)
Async XLA Ops:
  0.7 11.8 %collective-permute-start.6 = (bf16[256,128]{1,0:T(8,128)(2,1)}, bf16[256,128]{1,0:T(8,128)(2,1)S(1)}, u32[]{:S(2)}, u32[]{:S(2)}) collective-permute-start(bf16[256,128]{1,0:T(8,128)(2,1)} %refs_3_.10), channel_id=1, source_target_pairs={{0,16},{8,24},{16,0},{24,8},{1,17},{9,25},{17,1},{25,9},{2,18},{10... | collective-permute-start | bytes 196616 | tf_op jit(solution)/shard_map/ppermute | solution.py:1204
  3.7 18.2 %collective-permute-start.5 = (bf16[256,128]{1,0:T(8,128)(2,1)}, bf16[256,128]{1,0:T(8,128)(2,1)S(1)}, u32[]{:S(2)}, u32[]{:S(2)}) collective-permute-start(bf16[256,128]{1,0:T(8,128)(2,1)} %refs_3_.10), channel_id=1, source_target_pairs={{0,8},{8,0},{16,24},{24,16},{1,9},{9,1},{17,25},{25,17},{2,10},{10... | collective-permute-start | bytes 196616 | tf_op jit(solution)/shard_map/ppermute | solution.py:1204
  5.2 16.7 %collective-permute-start.7 = (bf16[256,128]{1,0:T(8,128)(2,1)}, bf16[256,128]{1,0:T(8,128)(2,1)S(1)}, u32[]{:S(2)}, u32[]{:S(2)}) collective-permute-start(bf16[256,128]{1,0:T(8,128)(2,1)} %refs_3_.10), channel_id=1, source_target_pairs={{0,24},{8,16},{16,8},{24,0},{1,25},{9,17},{17,9},{25,1},{2,26},{10... | collective-permute-start | bytes 196616 | tf_op jit(solution)/shard_map/ppermute | solution.py:1204
  9.0 21.4 %collective-permute-start.2 = (bf16[320,768]{1,0:T(8,128)(2,1)S(1)}, bf16[320,768]{1,0:T(8,128)(2,1)S(1)}, u32[]{:S(2)}, u32[]{:S(2)}) collective-permute-start(bf16[320,768]{1,0:T(8,128)(2,1)S(1)} %get-tuple-element.104.refs_1_), channel_id=1, source_target_pairs={{0,24},{8,16},{16,8},{24,0},{1,25},{9,17},{17,9},{25,1},{2,26},{10... | collective-permute-start | bytes 1474568 | tf_op jit(solution)/shard_map/ppermute | solution.py:1236
  11.9 21.0 %collective-permute-start.1 = (bf16[320,768]{1,0:T(8,128)(2,1)S(1)}, bf16[320,768]{1,0:T(8,128)(2,1)S(1)}, u32[]{:S(2)}, u32[]{:S(2)}) collective-permute-start(bf16[320,768]{1,0:T(8,128)(2,1)S(1)} %get-tuple-element.104.refs_1_), channel_id=1, source_target_pairs={{0,16},{8,24},{16,0},{24,8},{1,17},{9,25},{17,1},{25,9},{2,18},{10... | collective-permute-start | bytes 1474568 | tf_op jit(solution)/shard_map/ppermute | solution.py:1236
  12.4 20.7 %collective-permute-start = (bf16[320,768]{1,0:T(8,128)(2,1)S(1)}, bf16[320,768]{1,0:T(8,128)(2,1)S(1)}, u32[]{:S(2)}, u32[]{:S(2)}) collective-permute-start(bf16[320,768]{1,0:T(8,128)(2,1)S(1)} %get-tuple-element.104.refs_1_), channel_id=1, source_target_pairs={{0,8},{8,0},{16,24},{24,16},{1,9},{9,1},{17,25},{25,17},{2,10},{10... | collective-permute-start | bytes 1474568 | tf_op jit(solution)/shard_map/ppermute | solution.py:1236
  37.0 11.7 %collective-permute-start.11 = (bf16[512,128]{1,0:T(8,128)(2,1)S(1)}, bf16[512,128]{1,0:T(8,128)(2,1)S(1)}, u32[]{:S(2)}, u32[]{:S(2)}) collective-permute-start(bf16[512,128]{1,0:T(8,128)(2,1)S(1)} %forward_mix.1.refs_3_.refs_6_.refs_4_), channel_id=1, source_target_pairs={{0,2},{1,3},{2,0},{3,1},{4,6},{5,7},{6,4},{7,5},{8,10},{9,11},{10,... | collective-permute-start | bytes 393224 | tf_op jit(solution)/shard_map/ppermute | solution.py:124
  37.0 11.7 %collective-permute-start.10 = (bf16[512,128]{1,0:T(8,128)(2,1)S(1)}, bf16[512,128]{1,0:T(8,128)(2,1)S(1)}, u32[]{:S(2)}, u32[]{:S(2)}) collective-permute-start(bf16[512,128]{1,0:T(8,128)(2,1)S(1)} %forward_mix.1.refs_3_.refs_6_.refs_4_), channel_id=1, source_target_pairs={{0,1},{1,0},{2,3},{3,2},{4,5},{5,4},{6,7},{7,6},{8,9},{9,8},{10,11... | collective-permute-start | bytes 393224 | tf_op jit(solution)/shard_map/ppermute | solution.py:124
  55.7 12.5 %collective-permute-start.14 = (bf16[128,512]{1,0:T(8,128)(2,1)S(1)}, bf16[128,512]{1,0:T(8,128)(2,1)S(1)}, u32[]{:S(2)}, u32[]{:S(2)}) collective-permute-start(bf16[128,512]{1,0:T(8,128)(2,1)S(1)} %get-tuple-element.121), channel_id=1, source_target_pairs={{0,2},{1,3},{2,0},{3,1},{4,6},{5,7},{6,4},{7,5},{8,10},{9,11},{10,... | collective-permute-start | bytes 393224 | tf_op jit(solution)/shard_map/ppermute | solution.py:158
  65.8 12.2 %collective-permute-start.20 = (bf16[128,512]{1,0:T(8,128)(2,1)S(1)}, bf16[128,512]{1,0:T(8,128)(2,1)S(1)}, u32[]{:S(2)}, u32[]{:S(2)}) collective-permute-start(bf16[128,512]{1,0:T(8,128)(2,1)S(1)} %get-tuple-element.127), channel_id=1, source_target_pairs={{0,2},{1,3},{2,0},{3,1},{4,6},{5,7},{6,4},{7,5},{8,10},{9,11},{10,... | collective-permute-start | bytes 393224 | tf_op jit(solution)/shard_map/ppermute | solution.py:162
  65.9 12.2 %collective-permute-start.21 = (bf16[128,512]{1,0:T(8,128)(2,1)S(1)}, bf16[128,512]{1,0:T(8,128)(2,1)S(1)}, u32[]{:S(2)}, u32[]{:S(2)}) collective-permute-start(bf16[128,512]{1,0:T(8,128)(2,1)S(1)} %get-tuple-element.128), channel_id=1, source_target_pairs={{0,1},{1,0},{2,3},{3,2},{4,5},{5,4},{6,7},{7,6},{8,9},{9,8},{10,11... | collective-permute-start | bytes 393224 | tf_op jit(solution)/shard_map/ppermute | solution.py:163
  68.3 12.0 %collective-permute-start.17 = (bf16[128,512]{1,0:T(8,128)(2,1)S(1)}, bf16[128,512]{1,0:T(8,128)(2,1)S(1)}, u32[]{:S(2)}, u32[]{:S(2)}) collective-permute-start(bf16[128,512]{1,0:T(8,128)(2,1)S(1)} %add_convert_fusion.1.refs_9_), channel_id=1, source_target_pairs={{0,2},{1,3},{2,0},{3,1},{4,6},{5,7},{6,4},{7,5},{8,10},{9,11},{10,... | collective-permute-start | bytes 393224 | tf_op jit(solution)/shard_map/ppermute | solution.py:167
  96.9 12.9 %collective-permute-start.26 = (bf16[512,128]{1,0:T(8,128)(2,1)S(1)}, bf16[512,128]{1,0:T(8,128)(2,1)S(1)}, u32[]{:S(2)}, u32[]{:S(2)}) collective-permute-start(bf16[512,128]{1,0:T(8,128)(2,1)S(1)} %get-tuple-element.133), channel_id=1, source_target_pairs={{0,2},{1,3},{2,0},{3,1},{4,6},{5,7},{6,4},{7,5},{8,10},{9,11},{10,... | collective-permute-start | bytes 393224 | tf_op jit(solution)/shard_map/ppermute | solution.py:124
  104.2 16.2 %collective-permute-start.30 = (bf16[192,768]{1,0:T(8,128)(2,1)S(1)}, bf16[192,768]{1,0:T(8,128)(2,1)S(1)}, u32[]{:S(2)}, u32[]{:S(2)}) collective-permute-start(bf16[192,768]{1,0:T(8,128)(2,1)S(1)} %get-tuple-element.156), channel_id=1, source_target_pairs={{0,8},{8,0},{16,24},{24,16},{1,9},{9,1},{17,25},{25,17},{2,10},{10... | collective-permute-start | bytes 884744 | tf_op jit(solution)/shard_map/ppermute | solution.py:1340
  105.8 14.7 %collective-permute-start.31 = (bf16[192,768]{1,0:T(8,128)(2,1)S(1)}, bf16[192,768]{1,0:T(8,128)(2,1)S(1)}, u32[]{:S(2)}, u32[]{:S(2)}) collective-permute-start(bf16[192,768]{1,0:T(8,128)(2,1)S(1)} %get-tuple-element.157), channel_id=1, source_target_pairs={{0,16},{8,24},{16,0},{24,8},{1,17},{9,25},{17,1},{25,9},{2,18},{10... | collective-permute-start | bytes 884744 | tf_op jit(solution)/shard_map/ppermute | solution.py:1340
  106.5 14.0 %collective-permute-start.32 = (bf16[192,768]{1,0:T(8,128)(2,1)S(1)}, bf16[192,768]{1,0:T(8,128)(2,1)S(1)}, u32[]{:S(2)}, u32[]{:S(2)}) collective-permute-start(bf16[192,768]{1,0:T(8,128)(2,1)S(1)} %get-tuple-element.158), channel_id=1, source_target_pairs={{0,24},{8,16},{16,8},{24,0},{1,25},{9,17},{17,9},{25,1},{2,26},{10... | collective-permute-start | bytes 884744 | tf_op jit(solution)/shard_map/ppermute | solution.py:1340
  128.7 11.6 %collective-permute-start.34 = (bf16[208,896]{1,0:T(8,128)(2,1)S(1)}, bf16[208,896]{1,0:T(8,128)(2,1)S(1)}, u32[]{:S(2)}, u32[]{:S(2)}) collective-permute-start(bf16[208,896]{1,0:T(8,128)(2,1)S(1)} %get-tuple-element.163), channel_id=1, source_target_pairs={{0,8},{8,0},{16,24},{24,16},{1,9},{9,1},{17,25},{25,17},{2,10},{10... | collective-permute-start | bytes 1118216 | tf_op jit(solution)/shard_map/ppermute | solution.py:1156
  129.7 11.5 %collective-permute-start.35 = (bf16[208,896]{1,0:T(8,128)(2,1)S(1)}, bf16[208,896]{1,0:T(8,128)(2,1)S(1)}, u32[]{:S(2)}, u32[]{:S(2)}) collective-permute-start(bf16[208,896]{1,0:T(8,128)(2,1)S(1)} %get-tuple-element.164), channel_id=1, source_target_pairs={{0,16},{8,24},{16,0},{24,8},{1,17},{9,25},{17,1},{25,9},{2,18},{10... | collective-permute-start | bytes 1118216 | tf_op jit(solution)/shard_map/ppermute | solution.py:1156
  130.4 17.8 %collective-permute-start.36 = (bf16[208,896]{1,0:T(8,128)(2,1)S(1)}, bf16[208,896]{1,0:T(8,128)(2,1)S(1)}, u32[]{:S(2)}, u32[]{:S(2)}) collective-permute-start(bf16[208,896]{1,0:T(8,128)(2,1)S(1)} %get-tuple-element.165), channel_id=1, source_target_pairs={{0,24},{8,16},{16,8},{24,0},{1,25},{9,17},{17,9},{25,1},{2,26},{10... | collective-permute-start | bytes 1118216 | tf_op jit(solution)/shard_map/ppermute | solution.py:1156
  134.4 14.1 %collective-permute-start.38 = (bf16[128,1024]{1,0:T(8,128)(2,1)S(1)}, bf16[128,1024]{1,0:T(8,128)(2,1)S(1)}, u32[]{:S(2)}, u32[]{:S(2)}) collective-permute-start(bf16[128,1024]{1,0:T(8,128)(2,1)S(1)} %get-tuple-element.168), channel_id=1, source_target_pairs={{0,1},{1,0},{2,3},{3,2},{4,5},{5,4},{6,7},{7,6},{8,9},{9,8},{10,11... | collective-permute-start | bytes 786440 | tf_op jit(solution)/shard_map/ppermute | solution.py:204
  136.2 13.7 %collective-permute-start.39 = (bf16[128,1024]{1,0:T(8,128)(2,1)S(1)}, bf16[128,1024]{1,0:T(8,128)(2,1)S(1)}, u32[]{:S(2)}, u32[]{:S(2)}) collective-permute-start(bf16[128,1024]{1,0:T(8,128)(2,1)S(1)} %get-tuple-element.169), channel_id=1, source_target_pairs={{0,2},{1,3},{2,0},{3,1},{4,6},{5,7},{6,4},{7,5},{8,10},{9,11},{10,... | collective-permute-start | bytes 786440 | tf_op jit(solution)/shard_map/ppermute | solution.py:205
  140.3 27.4 %collective-permute-start.45 = (f32[192,768]{1,0:T(8,128)S(1)}, f32[192,768]{1,0:T(8,128)S(1)}, u32[]{:S(2)}, u32[]{:S(2)}) collective-permute-start(f32[192,768]{1,0:T(8,128)S(1)} %add_add_fusion.refs_5_.refs_1_), channel_id=1, source_target_pairs={{0,4},{4,0},{1,5},{5,1},{2,6},{6,2},{3,7},{7,3},{8,12},{12,8},{9,1... | collective-permute-start | bytes 1769480 | tf_op jit(solution)/shard_map/ppermute | solution.py:84
  151.1 15.1 %collective-permute-start.42 = (bf16[144,1024]{1,0:T(8,128)(2,1)S(1)}, bf16[144,1024]{1,0:T(8,128)(2,1)S(1)}, u32[]{:S(2)}, u32[]{:S(2)}) collective-permute-start(bf16[144,1024]{1,0:T(8,128)(2,1)S(1)} %rows.1.refs_7_.refs_1_), channel_id=1, source_target_pairs={{0,2},{1,3},{2,0},{3,1},{4,6},{5,7},{6,4},{7,5},{8,10},{9,11},{10,... | collective-permute-start | bytes 884744 | tf_op jit(solution)/shard_map/ppermute | solution.py:177
  152.6 13.6 %collective-permute-start.41 = (bf16[144,1024]{1,0:T(8,128)(2,1)S(1)}, bf16[144,1024]{1,0:T(8,128)(2,1)S(1)}, u32[]{:S(2)}, u32[]{:S(2)}) collective-permute-start(bf16[144,1024]{1,0:T(8,128)(2,1)S(1)} %rows.1.refs_7_.refs_1_), channel_id=1, source_target_pairs={{0,1},{1,0},{2,3},{3,2},{4,5},{5,4},{6,7},{7,6},{8,9},{9,8},{10,11... | collective-permute-start | bytes 884744 | tf_op jit(solution)/shard_map/ppermute | solution.py:176
  (41 other events, 340.4 us)

commit v5 on v4

--- a/solution.py
+++ b/solution.py
@@ -812,8 +812,9 @@
             s = place[0] ^ k
             gate_ref[at(rows * s, rows), :] = firsts[k][0:rows, :]
             output_ref[at(rows * s, rows), :] = seconds[k][0:rows, :]
-            expand_ref[at(2 * some * s, some), :] = firsts[k][rows:, :]
-            expand_ref[at(2 * some * s + some, some), :] = seconds[k][rows:, :]
+            start = 2 * some * (s ^ place[2])
+            expand_ref[at(start, some), :] = firsts[k][rows:, :]
+            expand_ref[at(start + some, some), :] = seconds[k][rows:, :]
 
     @pl.when(place[1] == 0)
     def _():
@@ -824,34 +825,40 @@
         store(rests, mines)
 
 
-def expand_rows(place, k, refs, pieces, size):
+def expand_rows(place, k, refs, pieces, size, ordered):
     act_ref, slope_ref, we_ref, b_ref, wo_ref = refs
     height = pieces[0].shape[0] // size
     channels = pieces[0].shape[1]
     rows = at(height * toward(place, k, size), height)
     expanded = b_ref[...][None, :]
-    for j in range(size):
-        source = origin(place, j, size)
-        expanded = expanded + dot(pieces[j][rows, :], we_ref[at(channels * source, channels), :])
+    if ordered:
+        mixed = jnp.concatenate([piece[rows, :] for piece in pieces], 1)
+        expanded = expanded + dot(mixed, we_ref[...])
+    else:
+        for j in range(size):
+            source = origin(place, j, size)
+            expanded = expanded + dot(pieces[j][rows, :], we_ref[at(channels * source, channels), :])
     coef = (slope_ref[rows, :].astype(F32) * expanded).astype(BF16)
     gated = (expanded * act_ref[rows, :].astype(F32)).astype(BF16)
     half = wo_ref.shape[0] // 2
     return rows, gated, coef, [dot_t(gated, wo_ref[half * h : half * (h + 1), :]) for h in range(2)]
 
 
-def expand_first_kernel(place, *rest, size):
+def expand_first_kernel(place, *rest, size, ordered):
     refs, pieces, (gated_ref, coef_ref, *sends) = rest[:5], rest[5 : 5 + size], rest[5 + size :]
-    _, gated_ref[...], coef_ref[...], parts = expand_rows(place, size - 1, refs, pieces, size)
+    _, gated_ref[...], coef_ref[...], parts = expand_rows(
+        place, size - 1, refs, pieces, size, ordered
+    )
     for send, part in zip(sends, parts):
         send[...] = part.astype(BF16)
 
 
-def expand_kernel(place, *rest, size):
+def expand_kernel(place, *rest, size, ordered):
     refs, pieces, rest = rest[:5], rest[5 : 5 + size], rest[5 + size :]
     last_gated_ref, last_coef_ref, gated_ref, coef_ref, *rest = rest
     owns, sends = rest[:2], rest[2:]
     for k in range(size - 1):
-        rows, gated, coef, parts = expand_rows(place, k, refs, pieces, size)
+        rows, gated, coef, parts = expand_rows(place, k, refs, pieces, size, ordered)
         gated_ref[rows, :] = gated
         coef_ref[rows, :] = coef
         for h, part in enumerate(parts):
@@ -871,7 +878,7 @@
 
 
 def loss_kernel(
-    place, x_ref, t_ref, mask_ref, b_ref, act_ref, coef_ref, wo_ref, we_ref, *rest, size
+    place, x_ref, t_ref, mask_ref, b_ref, act_ref, coef_ref, wo_ref, we_ref, *rest, size, ordered
 ):
     pieces, others, rest = rest[:size], rest[size : 2 * size], rest[2 * size :]
     out_ref, back_ref, keep_ref, low_ref, gate_ref, ob_ref, eb_ref, gb_ref, err_ref, own_ref, *rest = rest
@@ -903,9 +910,14 @@
         gate_back = gated_back * coef_ref[rows, :].astype(F32)
         gatb = gatb + jnp.sum(gate_back, axis=0, keepdims=True)
         gate_ref[rows, :] = gate_back.astype(BF16)
+        if ordered:
+            whole = dot_t(expand_low, we_ref[...])
         for k in range(size):
-            target = toward(place, k, size)
-            part = dot_t(expand_low, we_ref[at(channels * target, channels), :])
+            if ordered:
+                part = whole[:, channels * k : channels * (k + 1)]
+            else:
+                target = toward(place, k, size)
+                part = dot_t(expand_low, we_ref[at(channels * target, channels), :])
             if k == 0:
                 own_ref[rows, :] = part
             else:
@@ -1030,10 +1042,9 @@
     some = mixed_s.shape[1] // 8
     for s in range(4):
         k = s
-        keep_ref[k, 0:half, :] = t_dot(back_ref[:, at((2 * s + core) * half, half)], gated_ref[...])
-        give_ref[k, 0:half, :] = t_dot(
-            back_ref[:, at((2 * s + 1 - core) * half, half)], gated_ref[...]
-        ).astype(BF16)
+        both = t_dot(back_ref[:, 2 * half * s : 2 * half * (s + 1)], gated_ref[...])
+        keep_ref[k, 0:half, :] = jnp.where(core == 0, both[:half], both[half:])
+        give_ref[k, 0:half, :] = jnp.where(core == 0, both[half:], both[:half]).astype(BF16)
         both = t_dot(mixed_s[:, at(2 * some * s, 2 * some)], low_ref[...])
         keep_ref[k, half:, :] = jnp.where(core == 0, both[:some], both[some:])
         give_ref[k, half:, :] = jnp.where(core == 0, both[some:], both[:some]).astype(BF16)
@@ -1048,12 +1059,11 @@
     units = gate_ref.shape[1]
     for s in range(4):
         lines = slice(half * s, half * (s + 1))
-        mine = x_ref[:, at((2 * s + core) * half, half)]
-        keep_ref[lines, 0:units] = t_dot(mine, gate_ref[...])
-        keep_ref[lines, units:] = t_dot(mine, reduce_ref[...])
-        other = x_ref[:, at((2 * s + 1 - core) * half, half)]
-        give_ref[lines, 0:units] = t_dot(other, gate_ref[...]).astype(BF16)
-        give_ref[lines, units:] = t_dot(other, reduce_ref[...]).astype(BF16)
+        rows = x_ref[:, 2 * half * s : 2 * half * (s + 1)]
+        for right, lanes in ((gate_ref, slice(0, units)), (reduce_ref, slice(units, None))):
+            both = t_dot(rows, right[...])
+            keep_ref[lines, lanes] = jnp.where(core == 0, both[:half], both[half:])
+            give_ref[lines, lanes] = jnp.where(core == 0, both[half:], both[:half]).astype(BF16)
     pack_s[...] = jnp.zeros_like(pack_s)
     sums = pack_ref.shape[0]
     high, low = halves(pack_ref[0:REACH, :])
@@ -1265,14 +1275,14 @@
     half_piece = (height, width // 2)
     expand_args = (gate_act, gate_slope, expand_full, expand_bias, output_full, *mixed)
     last_gated, last_coef, *last_sends = call(
-        partial(expand_first_kernel, size=size),
+        partial(expand_first_kernel, size=size, ordered=fast),
         "expand_first",
         [((height, units), BF16)] * 2 + [(half_piece, BF16)] * 2,
         (place, *expand_args),
         micros=1,
     )
     gated, coef, first_part, second_part, *branch_sends = call(
-        partial(expand_kernel, size=size),
+        partial(expand_kernel, size=size, ordered=fast),
         "expand",
         [((tokens, units), BF16)] * 2 + [(half_piece, F32)] * 2 + [(half_piece, BF16)] * (2 * size - 4),
         (place, *expand_args, last_gated, last_coef),
@@ -1285,7 +1295,7 @@
     )
 
     output, branch_back, keep_back, expand_low, gate_low, *rest = call(
-        partial(loss_kernel, size=size),
+        partial(loss_kernel, size=size, ordered=fast),
         "loss",
         [
             (inputs.shape, BF16),

time: 177 us -> 177 us (level)
  starting transfers between devices: 50 us -> 57.1 us
  waiting for transfers between devices: 56.1 us -> 49.9 us
    ppermute x1, waiting for transfers between devices: 8.14 us -> 3.65 us  [sum_tensor(): second_far = lax.ppermute(joined, 'tensor', far_pairs)]
    ppermute x2, starting transfers between devices: 2.09 us -> 5.77 us  [sum_tensor(): beside = lax.ppermute(total, 'tensor', near_pairs)]
    ppermute x2, waiting for transfers between devices: 2.53 us -> 0.01 us  [sum_tensor(): away = lax.ppermute(total, 'tensor', far_pairs)]
    ppermute x1, waiting for transfers between devices: 0.01 us -> 1.87 us  [sum_tensor(): first_near = lax.ppermute(near, 'tensor', near_pairs)]
  transfers between devices with their start and end apart: 46 -> 46, of which waited for: 21 -> 20; matrix products, arithmetic and copies ran while one was open for 1% -> 1% of each run, Pallas kernels for 30% -> 30%
where the time goes in v5:
time: 177 us
  Pallas kernels  64.4 us (36%)
  starting transfers between devices  57.1 us (32%)
  waiting for transfers between devices  49.9 us (28%)
  local copies, waits for them, and re-layouts  3 us (2%)
    pallas_call x31, Pallas kernels, call(): pl.pallas_call(kernel, out_shape=[jax.ShapeDtypeStruct(shape, kind) for s...  64.4 us
    ppermute x3, waiting for transfers between devices, send_late(): lax.ppermute(sends[k - 1], 'shard', xor_pairs(4, k))  10.6 us
    ppermute x6, waiting for transfers between devices, exchange_tensor(): lax.ppermute(x, 'tensor', tensor_pairs(size, k + 1))  10.6 us
    ppermute x6, starting transfers between devices, exchange_tensor(): lax.ppermute(x, 'tensor', tensor_pairs(size, k + 1))  8.9 us
    ppermute x2, starting transfers between devices, sum_tensor(): beside = lax.ppermute(total, 'tensor', near_pairs)  5.77 us
    ppermute x1, waiting for transfers between devices, sum_tensor(): passed = lax.ppermute(after, 'tensor', near_pairs)  5.05 us
    ppermute x3, starting transfers between devices, per_device(): lax.ppermute(reduce_weight, 'shard', xor_pairs(4, k))  4.57 us
    ppermute x2, waiting for transfers between devices, sum_tensor(): lax.ppermute(away, 'tensor', near_pairs)  4.21 us
  transfers between devices with their start and end apart: 46, of which 20 were waited for; matrix products, arithmetic and copies ran while one was open for 1% of the time, Pallas kernels for 30%

profile of v5, /device:TPU:0, one launch (start us, length us, event | category | flops | bytes accessed | tf_op | source)
XLA Modules:
  0.0 177.1 jit_solution(12370555441138815495)
XLA Ops:
  0.7 3.0 %collective-permute-start.6 = (bf16[256,128]{1,0:T(8,128)(2,1)}, bf16[256,128]{1,0:T(8,128)(2,1)S(1)}, u32[]{:S(2)}, u32[]{:S(2)}) collective-permute-start(bf16[256,128]{1,0:T(8,128)(2,1)} %refs_3_.10), channel_id=1, source_target_pairs={{0,16},{8,24},{16,0},{24,8},{1,17},{9,25},{17,1},{25,9},{2,18},{10... | collective-permute-start | bytes 196616 | tf_op jit(solution)/shard_map/ppermute | solution.py:1214
  9.0 2.9 %collective-permute-start.2 = (bf16[320,768]{1,0:T(8,128)(2,1)S(1)}, bf16[320,768]{1,0:T(8,128)(2,1)S(1)}, u32[]{:S(2)}, u32[]{:S(2)}) collective-permute-start(bf16[320,768]{1,0:T(8,128)(2,1)S(1)} %get-tuple-element.104.refs_1_), channel_id=1, source_target_pairs={{0,24},{8,16},{16,8},{24,0},{1,25},{9,17},{17,9},{25,1},{2,26},{10... | collective-permute-start | bytes 1474568 | tf_op jit(solution)/shard_map/ppermute | solution.py:1246
  12.6 8.1 %taps.1.refs_3_.refs_5_ = f32[128,128]{1,0:T(8,128)S(1)} custom-call(s32[3]{0:T(128)S(1)} %pad_add_fusion.refs_0_, f32[128,512]{1,0:T(8,128)S(1)} %copy-done.8, f32[128,512]{1,0:T(8,128)S(1)} %copy-done.9, f32[128]{0:T(128)S(1)} %copy-done.18, f32[128,512]{1,0:T(8,128)S(1)} %copy-done.10, f32[128,512]{1,0:T(8,128)S(1)} %copy-done.11), custom_call_target="tpu_custom_call" | custom-call | flops 12000000000 | bytes 6000000 | tf_op jit(solution)/shard_map/taps/pallas_call | solution.py:33
  26.8 3.6 %forward_mix.1.refs_3_.refs_6_.refs_4_ = bf16[512,128]{1,0:T(8,128)(2,1)S(1)} custom-call(s32[3]{0:T(128)S(1)} %pad_add_fusion.refs_0_, s32[1,512]{1,0:T(1,128)S(1)} %copy-done.16, s32[1,512]{1,0:T(1,128)S(1)} %collective-permute-done.3.refs_2_.refs_4_, s32[1,512]{1,0:T(1,128)S(1)} %copy-done.16, s32[1,512]{1,0:T(1,128)S(1)} %collective-permute-done.3.refs_2_.refs_4_, ...), custom_call_target="tpu_custom_call" | custom-call | flops 1000000000 | bytes 500000 | tf_op jit(solution)/shard_map/forward_mix/pallas_call | solution.py:33
  30.4 2.5 %collective-permute-done.1.refs_1_ = bf16[320,768]{1,0:T(8,128)(2,1)S(1)} collective-permute-done((bf16[320,768]{1,0:T(8,128)(2,1)S(1)}, bf16[320,768]{1,0:T(8,128)(2,1)S(1)}, u32[]{:S(2)}, u32[]{:S(2)}) %collective-permute-start.1) | collective-permute-done | bytes 491552 | tf_op jit(solution)/shard_map/ppermute | solution.py:1246
  33.3 3.7 %collective-permute-start.12 = (bf16[512,128]{1,0:T(8,128)(2,1)S(1)}, bf16[512,128]{1,0:T(8,128)(2,1)S(1)}, u32[]{:S(2)}, u32[]{:S(2)}) collective-permute-start(bf16[512,128]{1,0:T(8,128)(2,1)S(1)} %forward_mix.1.refs_3_.refs_6_.refs_4_), channel_id=1, source_target_pairs={{0,3},{1,2},{2,1},{3,0},{4,7},{5,6},{6,5},{7,4},{8,11},{9,10},{10,... | collective-permute-start | bytes 393224 | tf_op jit(solution)/shard_map/ppermute | solution.py:124
  41.6 7.1 %collective-permute-done.11.refs_8_.refs_6_ = bf16[512,128]{1,0:T(8,128)(2,1)S(1)} collective-permute-done((bf16[512,128]{1,0:T(8,128)(2,1)S(1)}, bf16[512,128]{1,0:T(8,128)(2,1)S(1)}, u32[]{:S(2)}, u32[]{:S(2)}) %collective-permute-start.11) | collective-permute-done | bytes 131104 | tf_op jit(solution)/shard_map/ppermute | solution.py:124
  50.1 2.5 %expand.1 = (bf16[512,768]{1,0:T(8,128)(2,1)S(1)}, bf16[512,768]{1,0:T(8,128)(2,1)S(1)}, f32[128,512]{1,0:T(8,128)S(1)}, f32[128,512]{1,0:T(8,128)S(1)}, bf16[12...) custom-call(s32[3]{0:T(128)S(1)} %pad_add_fusion.refs_0_, ...), custom_call_target="tpu_custom_call" | custom-call | flops 600000000 | bytes 300000 | tf_op jit(solution)/shard_map/expand/pallas_call | solution.py:33
  52.7 2.5 %collective-permute-done.13.refs_1_ = bf16[128,512]{1,0:T(8,128)(2,1)S(1)} collective-permute-done((bf16[128,512]{1,0:T(8,128)(2,1)S(1)}, bf16[128,512]{1,0:T(8,128)(2,1)S(1)}, u32[]{:S(2)}, u32[]{:S(2)}) %collective-permute-start.13) | collective-permute-done | bytes 131104 | tf_op jit(solution)/shard_map/ppermute | solution.py:156
  55.6 2.8 %collective-permute-start.14 = (bf16[128,512]{1,0:T(8,128)(2,1)S(1)}, bf16[128,512]{1,0:T(8,128)(2,1)S(1)}, u32[]{:S(2)}, u32[]{:S(2)}) collective-permute-start(bf16[128,512]{1,0:T(8,128)(2,1)S(1)} %get-tuple-element.121), channel_id=1, source_target_pairs={{0,2},{1,3},{2,0},{3,1},{4,6},{5,7},{6,4},{7,5},{8,10},{9,11},{10,... | collective-permute-start | bytes 393224 | tf_op jit(solution)/shard_map/ppermute | solution.py:158
  58.6 5.1 %collective-permute-done.19.refs_1_ = bf16[128,512]{1,0:T(8,128)(2,1)S(1)} collective-permute-done((bf16[128,512]{1,0:T(8,128)(2,1)S(1)}, bf16[128,512]{1,0:T(8,128)(2,1)S(1)}, u32[]{:S(2)}, u32[]{:S(2)}) %collective-permute-start.19) | collective-permute-done | bytes 131104 | tf_op jit(solution)/shard_map/ppermute | solution.py:159
  64.7 2.9 %collective-permute-start.21 = (bf16[128,512]{1,0:T(8,128)(2,1)S(1)}, bf16[128,512]{1,0:T(8,128)(2,1)S(1)}, u32[]{:S(2)}, u32[]{:S(2)}) collective-permute-start(bf16[128,512]{1,0:T(8,128)(2,1)S(1)} %get-tuple-element.128), channel_id=1, source_target_pairs={{0,1},{1,0},{2,3},{3,2},{4,5},{5,4},{6,7},{7,6},{8,9},{9,8},{10,11... | collective-permute-start | bytes 393224 | tf_op jit(solution)/shard_map/ppermute | solution.py:163
  69.6 3.6 %collective-permute-done.20 = bf16[128,512]{1,0:T(8,128)(2,1)S(1)} collective-permute-done((bf16[128,512]{1,0:T(8,128)(2,1)S(1)}, bf16[128,512]{1,0:T(8,128)(2,1)S(1)}, u32[]{:S(2)}, u32[]{:S(2)}) %collective-permute-start.20) | collective-permute-done | bytes 131104 | tf_op jit(solution)/shard_map/ppermute | solution.py:162
  74.4 5.7 %collective-permute-start.16 = (bf16[128,512]{1,0:T(8,128)(2,1)S(1)}, bf16[128,512]{1,0:T(8,128)(2,1)S(1)}, u32[]{:S(2)}, u32[]{:S(2)}) collective-permute-start(bf16[128,512]{1,0:T(8,128)(2,1)S(1)} %add_convert_fusion.1.refs_9_), channel_id=1, source_target_pairs={{0,1},{1,0},{2,3},{3,2},{4,5},{5,4},{6,7},{7,6},{8,9},{9,8},{10,11... | collective-permute-start | bytes 393224 | tf_op jit(solution)/shard_map/ppermute | solution.py:168
  84.3 2.8 %collective-permute-done.18.refs_12_ = bf16[128,512]{1,0:T(8,128)(2,1)S(1)} collective-permute-done((bf16[128,512]{1,0:T(8,128)(2,1)S(1)}, bf16[128,512]{1,0:T(8,128)(2,1)S(1)}, u32[]{:S(2)}, u32[]{:S(2)}) %collective-permute-start.18) | collective-permute-done | bytes 131104 | tf_op jit(solution)/shard_map/ppermute | solution.py:169
  88.5 4.3 %loss.1 = (bf16[512,1024]{1,0:T(8,128)(2,1)}, bf16[512,1024]{1,0:T(8,128)(2,1)S(1)}, f32[128,1024]{1,0:T(8,128)S(1)}, bf16[512,768]{1,0:T(8,128)(2,1)S(1)}, bf16...) custom-call(s32[3]{0:T(128)S(1)} %pad_add_fusion.refs_0_, ...), custom_call_target="tpu_custom_call" | custom-call | flops 1600000000 | bytes 800000 | tf_op jit(solution)/shard_map/loss/pallas_call | solution.py:33
  95.8 2.9 %collective-permute-start.26 = (bf16[512,128]{1,0:T(8,128)(2,1)S(1)}, bf16[512,128]{1,0:T(8,128)(2,1)S(1)}, u32[]{:S(2)}, u32[]{:S(2)}) collective-permute-start(bf16[512,128]{1,0:T(8,128)(2,1)S(1)} %get-tuple-element.133), channel_id=1, source_target_pairs={{0,2},{1,3},{2,0},{3,1},{4,6},{5,7},{6,4},{7,5},{8,10},{9,11},{10,... | collective-permute-start | bytes 393224 | tf_op jit(solution)/shard_map/ppermute | solution.py:124
  105.9 2.8 %collective-permute-done.26.refs_2_ = bf16[512,128]{1,0:T(8,128)(2,1)S(1)} collective-permute-done((bf16[512,128]{1,0:T(8,128)(2,1)S(1)}, bf16[512,128]{1,0:T(8,128)(2,1)S(1)}, u32[]{:S(2)}, u32[]{:S(2)}) %collective-permute-start.26) | collective-permute-done | bytes 131104 | tf_op jit(solution)/shard_map/ppermute | solution.py:124
  110.2 3.6 %taps_back.1.refs_1_ = f32[256,128]{1,0:T(8,128)S(1)} custom-call(s32[3]{0:T(128)S(1)} %pad_add_fusion.refs_0_, s32[1,512]{1,0:T(1,128)S(1)} %copy-done.16, s32[1,512]{1,0:T(1,128)S(1)} %collective-permute-done.3.refs_2_.refs_4_, s32[1,512]{1,0:T(1,128)S(1)} %copy-done.16, s32[1,512]{1,0:T(1,128)S(1)} %collective-permute-done.3.refs_2_.refs_4_, ...), custom_call_target="tpu_custom_call" | custom-call | flops 800000000 | bytes 400000 | tf_op jit(solution)/shard_map/taps_back/pallas_call | solution.py:33
  113.9 4.7 %backward_mix.1 = (bf16[512,128]{1,0:T(8,128)(2,1)S(1)}, f32[1,128]{1,0:T(1,128)S(1)}, f32[128,1024]{1,0:T(8,128)S(1)}, bf16[128,1024]{1,0:T(8,128)(2,1)S(1)}, b...) custom-call(s32[3]{0:T(128)S(1)} %pad_add_fusion.refs_0_, s32[1,512]{1,0:T(1,128)S(1)} %copy-done.16, ...), custom_call_target="tpu_custom_call" | custom-call | flops 1200000000 | bytes 600000 | tf_op jit(solution)/shard_map/backward_mix/pallas_call | solution.py:33
  124.2 2.9 %collective-permute-start.37 = (bf16[128,1024]{1,0:T(8,128)(2,1)S(1)}, bf16[128,1024]{1,0:T(8,128)(2,1)S(1)}, u32[]{:S(2)}, u32[]{:S(2)}) collective-permute-start(bf16[128,1024]{1,0:T(8,128)(2,1)S(1)} %get-tuple-element.150.refs_6_), channel_id=1, source_target_pairs={{0,1},{1,0},{2,3},{3,2},{4,5},{5,4},{6,7},{7,6},{8,9},{9,8},{10,11... | collective-permute-start | bytes 786440 | tf_op jit(solution)/shard_map/ppermute | solution.py:194
  136.7 3.0 %collective-permute-done.34.refs_2_ = bf16[208,896]{1,0:T(8,128)(2,1)S(1)} collective-permute-done((bf16[208,896]{1,0:T(8,128)(2,1)S(1)}, bf16[208,896]{1,0:T(8,128)(2,1)S(1)}, u32[]{:S(2)}, u32[]{:S(2)}) %collective-permute-start.34) | collective-permute-done | bytes 372768 | tf_op jit(solution)/shard_map/ppermute | solution.py:1166
  139.7 6.7 %collective-permute-done.35.refs_3_ = bf16[208,896]{1,0:T(8,128)(2,1)S(1)} collective-permute-done((bf16[208,896]{1,0:T(8,128)(2,1)S(1)}, bf16[208,896]{1,0:T(8,128)(2,1)S(1)}, u32[]{:S(2)}, u32[]{:S(2)}) %collective-permute-start.35) | collective-permute-done | bytes 372768 | tf_op jit(solution)/shard_map/ppermute | solution.py:1166
  153.5 12.4 %modes_back.1.refs_2_ = f32[520,256]{1,0:T(8,128)S(1)} custom-call(s32[3]{0:T(128)S(1)} %pad_add_fusion.refs_0_, f32[560,128]{1,0:T(8,128)S(1)} %get-tuple-element.166.refs_4_.refs_1_.refs_3_, f32[128,512]{1,0:T(8,128)S(1)} %copy-done.8, f32[128,512]{1,0:T(8,128)S(1)} %copy-done.9, f32[128]{0:T(128)S(1)} %copy-done.18, f32[128,512]{1,0:T(8,128)S(1)} %copy-done.10, ...), custom_call_target="tpu_custom_call" | custom-call | flops 800000000 | bytes 400000 | tf_op jit(solution)/shard_map/modes_back/pallas_call | solution.py:33
  (143 shorter events, 73.8 us)
Async XLA Ops:
  0.7 11.8 %collective-permute-start.6 = (bf16[256,128]{1,0:T(8,128)(2,1)}, bf16[256,128]{1,0:T(8,128)(2,1)S(1)}, u32[]{:S(2)}, u32[]{:S(2)}) collective-permute-start(bf16[256,128]{1,0:T(8,128)(2,1)} %refs_3_.10), channel_id=1, source_target_pairs={{0,16},{8,24},{16,0},{24,8},{1,17},{9,25},{17,1},{25,9},{2,18},{10... | collective-permute-start | bytes 196616 | tf_op jit(solution)/shard_map/ppermute | solution.py:1214
  3.7 18.2 %collective-permute-start.5 = (bf16[256,128]{1,0:T(8,128)(2,1)}, bf16[256,128]{1,0:T(8,128)(2,1)S(1)}, u32[]{:S(2)}, u32[]{:S(2)}) collective-permute-start(bf16[256,128]{1,0:T(8,128)(2,1)} %refs_3_.10), channel_id=1, source_target_pairs={{0,8},{8,0},{16,24},{24,16},{1,9},{9,1},{17,25},{25,17},{2,10},{10... | collective-permute-start | bytes 196616 | tf_op jit(solution)/shard_map/ppermute | solution.py:1214
  5.2 16.7 %collective-permute-start.7 = (bf16[256,128]{1,0:T(8,128)(2,1)}, bf16[256,128]{1,0:T(8,128)(2,1)S(1)}, u32[]{:S(2)}, u32[]{:S(2)}) collective-permute-start(bf16[256,128]{1,0:T(8,128)(2,1)} %refs_3_.10), channel_id=1, source_target_pairs={{0,24},{8,16},{16,8},{24,0},{1,25},{9,17},{17,9},{25,1},{2,26},{10... | collective-permute-start | bytes 196616 | tf_op jit(solution)/shard_map/ppermute | solution.py:1214
  9.0 21.4 %collective-permute-start.2 = (bf16[320,768]{1,0:T(8,128)(2,1)S(1)}, bf16[320,768]{1,0:T(8,128)(2,1)S(1)}, u32[]{:S(2)}, u32[]{:S(2)}) collective-permute-start(bf16[320,768]{1,0:T(8,128)(2,1)S(1)} %get-tuple-element.104.refs_1_), channel_id=1, source_target_pairs={{0,24},{8,16},{16,8},{24,0},{1,25},{9,17},{17,9},{25,1},{2,26},{10... | collective-permute-start | bytes 1474568 | tf_op jit(solution)/shard_map/ppermute | solution.py:1246
  11.9 21.0 %collective-permute-start.1 = (bf16[320,768]{1,0:T(8,128)(2,1)S(1)}, bf16[320,768]{1,0:T(8,128)(2,1)S(1)}, u32[]{:S(2)}, u32[]{:S(2)}) collective-permute-start(bf16[320,768]{1,0:T(8,128)(2,1)S(1)} %get-tuple-element.104.refs_1_), channel_id=1, source_target_pairs={{0,16},{8,24},{16,0},{24,8},{1,17},{9,25},{17,1},{25,9},{2,18},{10... | collective-permute-start | bytes 1474568 | tf_op jit(solution)/shard_map/ppermute | solution.py:1246
  12.4 20.7 %collective-permute-start = (bf16[320,768]{1,0:T(8,128)(2,1)S(1)}, bf16[320,768]{1,0:T(8,128)(2,1)S(1)}, u32[]{:S(2)}, u32[]{:S(2)}) collective-permute-start(bf16[320,768]{1,0:T(8,128)(2,1)S(1)} %get-tuple-element.104.refs_1_), channel_id=1, source_target_pairs={{0,8},{8,0},{16,24},{24,16},{1,9},{9,1},{17,25},{25,17},{2,10},{10... | collective-permute-start | bytes 1474568 | tf_op jit(solution)/shard_map/ppermute | solution.py:1246
  37.0 11.7 %collective-permute-start.11 = (bf16[512,128]{1,0:T(8,128)(2,1)S(1)}, bf16[512,128]{1,0:T(8,128)(2,1)S(1)}, u32[]{:S(2)}, u32[]{:S(2)}) collective-permute-start(bf16[512,128]{1,0:T(8,128)(2,1)S(1)} %forward_mix.1.refs_3_.refs_6_.refs_4_), channel_id=1, source_target_pairs={{0,2},{1,3},{2,0},{3,1},{4,6},{5,7},{6,4},{7,5},{8,10},{9,11},{10,... | collective-permute-start | bytes 393224 | tf_op jit(solution)/shard_map/ppermute | solution.py:124
  37.0 11.7 %collective-permute-start.10 = (bf16[512,128]{1,0:T(8,128)(2,1)S(1)}, bf16[512,128]{1,0:T(8,128)(2,1)S(1)}, u32[]{:S(2)}, u32[]{:S(2)}) collective-permute-start(bf16[512,128]{1,0:T(8,128)(2,1)S(1)} %forward_mix.1.refs_3_.refs_6_.refs_4_), channel_id=1, source_target_pairs={{0,1},{1,0},{2,3},{3,2},{4,5},{5,4},{6,7},{7,6},{8,9},{9,8},{10,11... | collective-permute-start | bytes 393224 | tf_op jit(solution)/shard_map/ppermute | solution.py:124
  55.6 12.1 %collective-permute-start.14 = (bf16[128,512]{1,0:T(8,128)(2,1)S(1)}, bf16[128,512]{1,0:T(8,128)(2,1)S(1)}, u32[]{:S(2)}, u32[]{:S(2)}) collective-permute-start(bf16[128,512]{1,0:T(8,128)(2,1)S(1)} %get-tuple-element.121), channel_id=1, source_target_pairs={{0,2},{1,3},{2,0},{3,1},{4,6},{5,7},{6,4},{7,5},{8,10},{9,11},{10,... | collective-permute-start | bytes 393224 | tf_op jit(solution)/shard_map/ppermute | solution.py:158
  58.3 11.2 %collective-permute-start.15 = (bf16[128,512]{1,0:T(8,128)(2,1)S(1)}, bf16[128,512]{1,0:T(8,128)(2,1)S(1)}, u32[]{:S(2)}, u32[]{:S(2)}) collective-permute-start(bf16[128,512]{1,0:T(8,128)(2,1)S(1)} %get-tuple-element.122), channel_id=1, source_target_pairs={{0,1},{1,0},{2,3},{3,2},{4,5},{5,4},{6,7},{7,6},{8,9},{9,8},{10,11... | collective-permute-start | bytes 393224 | tf_op jit(solution)/shard_map/ppermute | solution.py:160
  69.6 10.6 %collective-permute-start.17 = (bf16[128,512]{1,0:T(8,128)(2,1)S(1)}, bf16[128,512]{1,0:T(8,128)(2,1)S(1)}, u32[]{:S(2)}, u32[]{:S(2)}) collective-permute-start(bf16[128,512]{1,0:T(8,128)(2,1)S(1)} %add_convert_fusion.1.refs_9_), channel_id=1, source_target_pairs={{0,2},{1,3},{2,0},{3,1},{4,6},{5,7},{6,4},{7,5},{8,10},{9,11},{10,... | collective-permute-start | bytes 393224 | tf_op jit(solution)/shard_map/ppermute | solution.py:167
  95.8 12.9 %collective-permute-start.26 = (bf16[512,128]{1,0:T(8,128)(2,1)S(1)}, bf16[512,128]{1,0:T(8,128)(2,1)S(1)}, u32[]{:S(2)}, u32[]{:S(2)}) collective-permute-start(bf16[512,128]{1,0:T(8,128)(2,1)S(1)} %get-tuple-element.133), channel_id=1, source_target_pairs={{0,2},{1,3},{2,0},{3,1},{4,6},{5,7},{6,4},{7,5},{8,10},{9,11},{10,... | collective-permute-start | bytes 393224 | tf_op jit(solution)/shard_map/ppermute | solution.py:124
  98.7 10.0 %collective-permute-start.27 = (bf16[512,128]{1,0:T(8,128)(2,1)S(1)}, bf16[512,128]{1,0:T(8,128)(2,1)S(1)}, u32[]{:S(2)}, u32[]{:S(2)}) collective-permute-start(bf16[512,128]{1,0:T(8,128)(2,1)S(1)} %get-tuple-element.134), channel_id=1, source_target_pairs={{0,3},{1,2},{2,1},{3,0},{4,7},{5,6},{6,5},{7,4},{8,11},{9,10},{10,... | collective-permute-start | bytes 393224 | tf_op jit(solution)/shard_map/ppermute | solution.py:124
  102.3 17.4 %collective-permute-start.30 = (bf16[192,768]{1,0:T(8,128)(2,1)S(1)}, bf16[192,768]{1,0:T(8,128)(2,1)S(1)}, u32[]{:S(2)}, u32[]{:S(2)}) collective-permute-start(bf16[192,768]{1,0:T(8,128)(2,1)S(1)} %get-tuple-element.156), channel_id=1, source_target_pairs={{0,8},{8,0},{16,24},{24,16},{1,9},{9,1},{17,25},{25,17},{2,10},{10... | collective-permute-start | bytes 884744 | tf_op jit(solution)/shard_map/ppermute | solution.py:1350
  103.9 15.8 %collective-permute-start.31 = (bf16[192,768]{1,0:T(8,128)(2,1)S(1)}, bf16[192,768]{1,0:T(8,128)(2,1)S(1)}, u32[]{:S(2)}, u32[]{:S(2)}) collective-permute-start(bf16[192,768]{1,0:T(8,128)(2,1)S(1)} %get-tuple-element.157), channel_id=1, source_target_pairs={{0,16},{8,24},{16,0},{24,8},{1,17},{9,25},{17,1},{25,9},{2,18},{10... | collective-permute-start | bytes 884744 | tf_op jit(solution)/shard_map/ppermute | solution.py:1350
  104.6 15.1 %collective-permute-start.32 = (bf16[192,768]{1,0:T(8,128)(2,1)S(1)}, bf16[192,768]{1,0:T(8,128)(2,1)S(1)}, u32[]{:S(2)}, u32[]{:S(2)}) collective-permute-start(bf16[192,768]{1,0:T(8,128)(2,1)S(1)} %get-tuple-element.158), channel_id=1, source_target_pairs={{0,24},{8,16},{16,8},{24,0},{1,25},{9,17},{17,9},{25,1},{2,26},{10... | collective-permute-start | bytes 884744 | tf_op jit(solution)/shard_map/ppermute | solution.py:1350
  128.0 11.6 %collective-permute-start.34 = (bf16[208,896]{1,0:T(8,128)(2,1)S(1)}, bf16[208,896]{1,0:T(8,128)(2,1)S(1)}, u32[]{:S(2)}, u32[]{:S(2)}) collective-permute-start(bf16[208,896]{1,0:T(8,128)(2,1)S(1)} %get-tuple-element.163), channel_id=1, source_target_pairs={{0,8},{8,0},{16,24},{24,16},{1,9},{9,1},{17,25},{25,17},{2,10},{10... | collective-permute-start | bytes 1118216 | tf_op jit(solution)/shard_map/ppermute | solution.py:1166
  128.5 17.9 %collective-permute-start.35 = (bf16[208,896]{1,0:T(8,128)(2,1)S(1)}, bf16[208,896]{1,0:T(8,128)(2,1)S(1)}, u32[]{:S(2)}, u32[]{:S(2)}) collective-permute-start(bf16[208,896]{1,0:T(8,128)(2,1)S(1)} %get-tuple-element.164), channel_id=1, source_target_pairs={{0,16},{8,24},{16,0},{24,8},{1,17},{9,25},{17,1},{25,9},{2,18},{10... | collective-permute-start | bytes 1118216 | tf_op jit(solution)/shard_map/ppermute | solution.py:1166
  130.8 16.5 %collective-permute-start.36 = (bf16[208,896]{1,0:T(8,128)(2,1)S(1)}, bf16[208,896]{1,0:T(8,128)(2,1)S(1)}, u32[]{:S(2)}, u32[]{:S(2)}) collective-permute-start(bf16[208,896]{1,0:T(8,128)(2,1)S(1)} %get-tuple-element.165), channel_id=1, source_target_pairs={{0,24},{8,16},{16,8},{24,0},{1,25},{9,17},{17,9},{25,1},{2,26},{10... | collective-permute-start | bytes 1118216 | tf_op jit(solution)/shard_map/ppermute | solution.py:1166
  133.7 13.9 %collective-permute-start.38 = (bf16[128,1024]{1,0:T(8,128)(2,1)S(1)}, bf16[128,1024]{1,0:T(8,128)(2,1)S(1)}, u32[]{:S(2)}, u32[]{:S(2)}) collective-permute-start(bf16[128,1024]{1,0:T(8,128)(2,1)S(1)} %get-tuple-element.168), channel_id=1, source_target_pairs={{0,1},{1,0},{2,3},{3,2},{4,5},{5,4},{6,7},{7,6},{8,9},{9,8},{10,11... | collective-permute-start | bytes 786440 | tf_op jit(solution)/shard_map/ppermute | solution.py:204
  135.5 13.7 %collective-permute-start.39 = (bf16[128,1024]{1,0:T(8,128)(2,1)S(1)}, bf16[128,1024]{1,0:T(8,128)(2,1)S(1)}, u32[]{:S(2)}, u32[]{:S(2)}) collective-permute-start(bf16[128,1024]{1,0:T(8,128)(2,1)S(1)} %get-tuple-element.169), channel_id=1, source_target_pairs={{0,2},{1,3},{2,0},{3,1},{4,6},{5,7},{6,4},{7,5},{8,10},{9,11},{10,... | collective-permute-start | bytes 786440 | tf_op jit(solution)/shard_map/ppermute | solution.py:205
  139.7 28.1 %collective-permute-start.45 = (f32[192,768]{1,0:T(8,128)S(1)}, f32[192,768]{1,0:T(8,128)S(1)}, u32[]{:S(2)}, u32[]{:S(2)}) collective-permute-start(f32[192,768]{1,0:T(8,128)S(1)} %add_add_fusion.refs_5_.refs_1_), channel_id=1, source_target_pairs={{0,4},{4,0},{1,5},{5,1},{2,6},{6,2},{3,7},{7,3},{8,12},{12,8},{9,1... | collective-permute-start | bytes 1769480 | tf_op jit(solution)/shard_map/ppermute | solution.py:84
  150.5 15.9 %collective-permute-start.42 = (bf16[144,1024]{1,0:T(8,128)(2,1)S(1)}, bf16[144,1024]{1,0:T(8,128)(2,1)S(1)}, u32[]{:S(2)}, u32[]{:S(2)}) collective-permute-start(bf16[144,1024]{1,0:T(8,128)(2,1)S(1)} %rows.1.refs_7_.refs_1_), channel_id=1, source_target_pairs={{0,2},{1,3},{2,0},{3,1},{4,6},{5,7},{6,4},{7,5},{8,10},{9,11},{10,... | collective-permute-start | bytes 884744 | tf_op jit(solution)/shard_map/ppermute | solution.py:177
  152.7 13.7 %collective-permute-start.41 = (bf16[144,1024]{1,0:T(8,128)(2,1)S(1)}, bf16[144,1024]{1,0:T(8,128)(2,1)S(1)}, u32[]{:S(2)}, u32[]{:S(2)}) collective-permute-start(bf16[144,1024]{1,0:T(8,128)(2,1)S(1)} %rows.1.refs_7_.refs_1_), channel_id=1, source_target_pairs={{0,1},{1,0},{2,3},{3,2},{4,5},{5,4},{6,7},{7,6},{8,9},{9,8},{10,11... | collective-permute-start | bytes 884744 | tf_op jit(solution)/shard_map/ppermute | solution.py:176
  (41 other events, 335.2 us)
